TPU v7x, 32 devices: a whole 2x2x4 slice. The times are simulated.
32 devices in a mesh: blk: 4 (over z), expert: 8 (over y, x, core).
Axes of the slice: x: 2, y: 2, z: 4, core: 2. Of those that a mesh axis runs over, the one named last changes fastest.
Arguments:
- tokens: bfloat16 [16, 2048, 768], P('expert', 'blk'), may hold values from -6 to 6
- doc_ids: int32 [16, 2048], P('expert'), may hold values from 0 to 28, as said below
- routes: int32 [4, 16, 512, 1], P('blk', 'expert'), may hold values from 0 to 7; in each aligned block of 1024 rows (0 to 1023, 1024 to 2047, ..., all dimensions but the last counted through in order) at most 256 rows name the same one
- ln1_gain: float32 [768], replicated, may hold values from 0.5 to 1.5
- ln1_bias: float32 [768], replicated, may hold values from -1 to 1
- qkv_weight: bfloat16 [768, 2304], P('expert'), may hold values from -0.21875 to 0.21875
- qv_bias: float32 [2, 768], replicated, may hold values from -1 to 1
- out_weight: bfloat16 [768, 768], P('expert'), may hold values from -1.5 to 1.5
- out_bias: float32 [768], replicated, may hold values from -1 to 1
- ln2_gain: float32 [768], replicated, may hold values from 0.5 to 1.5
- ln2_bias: float32 [768], replicated, may hold values from -1 to 1
- centroids: bfloat16 [8, 768], replicated, may hold values from -0.15625 to 0.15625
- up_weight: bfloat16 [8, 768, 3072], P('expert'), may hold values from -0.21875 to 0.21875
- up_bias: float32 [8, 3072], P('expert'), may hold values from -0.6 to 0.6
- down_weight: bfloat16 [8, 3072, 768], P('expert'), may hold values from -0.21875 to 0.21875
- down_bias: float32 [8, 768], P('expert'), may hold values from -0.6 to 0.6
- cotangent: bfloat16 [16, 2048, 768], P('expert', 'blk'), may hold values from -6 to 6
Outputs:
- layer_out: float32 [16, 2048, 768], P('expert', 'blk')
- token_grad: float32 [16, 2048, 768], P('expert', 'blk')
- ln1_gain_grad: float32 [768], P('expert')
- ln1_bias_grad: float32 [768], P('expert')
- qkv_grad: float32 [768, 2304], P('expert')
- qv_bias_grad: float32 [2, 768], P(None, 'expert')
- out_weight_grad: float32 [768, 768], P('expert')
- out_bias_grad: float32 [768], P('expert')
- ln2_gain_grad: float32 [768], P('expert')
- ln2_bias_grad: float32 [768], P('expert')
- centroid_grad: float32 [8, 768], P(None, 'expert')
- up_grad: float32 [8, 768, 3072], P('expert', 'blk')
- up_bias_grad: float32 [8, 3072], P('expert', 'blk')
- down_grad: float32 [8, 3072, 768], P('expert', 'blk')
- down_bias_grad: float32 [8, 768], P('expert', 'blk')
Inputs may be any that keep to these rules, and one draw needn't show every extreme that they name: `doc_ids`: within a row the numbers start at 0, never fall and rise by at most one from a position to the next; equal numbers mark one document. In each group of 2 rows (rows g * 2 up to g * 2 + 1), half of the rows hold one document of 2048 tokens, and each other row holds documents of 64 to 256 tokens, one of exactly 256; the last document of a row may be cut shorter by the row's end. In every draw some row reaches the largest number. `routes`: among the tokens of one device (aligned blocks of 1024 consecutive entries in the array's order) at most 256 name one expert; in every draw some device names some expert exactly 256 times.
All inputs are finite; a program needn't handle non-finite values.
Results may differ from a plain program's by a relative error of at most 0.018.
Values may be sent and summed in bfloat16 or wider, within the bound.
A program may use at most 320 MiB of HBM per device.

v0:
```python
import jax
import jax.numpy as jnp
from jax import lax
from jax.sharding import PartitionSpec as P

HEADS = 12


NEGATIVE = -1e30
EPSILON = 1e-05


def layer_norm(values, scales, shifts):
    average = jnp.mean(values, axis=-1, keepdims=True)
    centred = values - average
    variance = jnp.mean(centred * centred, axis=-1, keepdims=True)
    return centred * lax.rsqrt(variance + EPSILON) * scales + shifts


def gelu_exact(values):
    return jax.nn.gelu(values, approximate=False)


def unchanged(running):
    return running


def masked_scores(query_part, key_part, visible, score_scale):
    scores = (
        jnp.einsum("rqhd,rkhd->rhqk", query_part, key_part, preferred_element_type=jnp.float32)
        * score_scale
    )
    return jnp.where(visible[:, None], scores, NEGATIVE)


def pair_grads(
    query_part, grad_part, total_part, delta_part, key_part, value_part, visible, score_scale
):
    scores = masked_scores(query_part, key_part, visible, score_scale)
    weights = jnp.exp(scores - total_part[..., None])
    grad_weights = jnp.einsum(
        "rqhd,rkhd->rhqk", grad_part, value_part, preferred_element_type=jnp.float32
    )
    grad_scores = (weights * (grad_weights - delta_part[..., None])).astype(jnp.bfloat16)
    return (grad_scores, weights.astype(jnp.bfloat16))


def on_device(
    tokens,
    doc_ids,
    routes,
    ln1_gain,
    ln1_bias,
    qkv_weight,
    qv_bias,
    out_weight,
    out_bias,
    ln2_gain,
    ln2_bias,
    centroids,
    up_weight,
    up_bias,
    down_weight,
    down_bias,
    cotangent,
):
    row_count, span_len, model_width = tokens.shape
    head_count = HEADS
    head_size = model_width // head_count
    score_scale = head_size ** (-0.5)
    blocks = lax.axis_size("blk")
    own_start = lax.axis_index("blk") * span_len
    token_count = row_count * span_len
    four_shape = (row_count, span_len, head_count, head_size)
    full_qkv, full_out = (
        lax.all_gather(qkv_weight, "expert", axis=0, tiled=True),
        lax.all_gather(out_weight, "expert", axis=0, tiled=True),
    )
    token_rows = tokens.astype(jnp.float32).reshape(token_count, model_width)
    normed_one, norm_back_one = jax.vjp(layer_norm, token_rows, ln1_gain, ln1_bias)
    normed_low = normed_one.astype(jnp.bfloat16)
    bias_row = jnp.concatenate([qv_bias[0], jnp.zeros((model_width,), jnp.float32), qv_bias[1]])
    projected = jnp.dot(normed_low, full_qkv, preferred_element_type=jnp.float32) + bias_row
    projected_low = projected.astype(jnp.bfloat16)
    query_low = projected_low[:, :model_width].reshape(row_count, span_len, model_width)
    key_low = projected_low[:, model_width : 2 * model_width].reshape(
        row_count, span_len, model_width
    )
    value_low = projected_low[:, 2 * model_width :].reshape(row_count, span_len, model_width)
    query_four = query_low.reshape(four_shape)
    key_all, value_all = (
        lax.all_gather(key_low, "blk", axis=1, tiled=True),
        lax.all_gather(value_low, "blk", axis=1, tiled=True),
    )
    query_ids = lax.dynamic_slice_in_dim(doc_ids, own_start, span_len, 1)
    query_pos = own_start + jnp.arange(span_len, dtype=jnp.int32)
    span_steps = jnp.arange(blocks, dtype=jnp.int32)

    def span_view(column):
        offset = column * span_len
        key_ids = lax.dynamic_slice_in_dim(doc_ids, offset, span_len, 1)
        key_pos = offset + jnp.arange(span_len, dtype=jnp.int32)
        visible = (query_ids[:, :, None] == key_ids[:, None, :]) & (
            key_pos[None, None, :] <= query_pos[None, :, None]
        )
        key_part = lax.dynamic_slice_in_dim(key_all, offset, span_len, 1).reshape(four_shape)
        value_part = lax.dynamic_slice_in_dim(value_all, offset, span_len, 1).reshape(four_shape)
        return (visible, key_part, value_part)

    def stats_step(running, column):
        visible, key_part, value_part = span_view(column)

        def stats_compute(running):
            running_max, running_sum = running
            scores = masked_scores(query_four, key_part, visible, score_scale)
            new_max = jnp.maximum(running_max, jnp.max(scores, axis=-1))
            weights = jnp.where(visible[:, None], jnp.exp(scores - new_max[..., None]), 0.0)
            return (
                new_max,
                running_sum * jnp.exp(running_max - new_max) + jnp.sum(weights, axis=-1),
            )

        return (lax.cond(jnp.any(visible), stats_compute, unchanged, running), None)

    start_max = jnp.full((row_count, head_count, span_len), NEGATIVE, jnp.float32)
    start_sum = jnp.zeros((row_count, head_count, span_len), jnp.float32)
    (row_max, row_sum), unused = lax.scan(stats_step, (start_max, start_sum), span_steps)
    log_total = row_max + jnp.log(row_sum)

    def output_step(totals, column):
        visible, key_part, value_part = span_view(column)

        def output_compute(totals):
            scores = masked_scores(query_four, key_part, visible, score_scale)
            weights_low = jnp.exp(scores - log_total[..., None]).astype(jnp.bfloat16)
            return totals + jnp.einsum(
                "rhqk,rkhd->rqhd", weights_low, value_part, preferred_element_type=jnp.float32
            )

        return (lax.cond(jnp.any(visible), output_compute, unchanged, totals), None)

    attended, unused = lax.scan(output_step, jnp.zeros(four_shape, jnp.float32), span_steps)
    attended_low = attended.reshape(token_count, model_width).astype(jnp.bfloat16)
    middle = (
        token_rows + jnp.dot(attended_low, full_out, preferred_element_type=jnp.float32) + out_bias
    )
    route_flat = routes.reshape(token_count)
    expert_count = centroids.shape[0]
    capacity = 2 * token_count // expert_count
    onehot = route_flat[:, None] == jnp.arange(expert_count, dtype=jnp.int32)[None, :]
    ranking = jnp.cumsum(onehot.astype(jnp.int32), axis=0) - 1
    slot_of = jnp.sum(jnp.where(onehot, ranking, 0), axis=1)
    normed_two, norm_back_two = jax.vjp(layer_norm, middle, ln2_gain, ln2_bias)
    expert_in = normed_two.astype(jnp.bfloat16)
    empty_slots = jnp.zeros((expert_count, capacity, model_width), jnp.bfloat16)
    outgoing = empty_slots.at[route_flat, slot_of].set(expert_in)
    centroid_rows = jnp.dot(
        onehot.astype(jnp.bfloat16), centroids, preferred_element_type=jnp.float32
    )
    gate_value = jax.nn.sigmoid(jnp.sum(normed_two * centroid_rows, axis=1))
    up_local = up_weight[0]
    down_local = down_weight[0]
    up_shift = up_bias[0]
    down_shift = down_bias[0]
    received = lax.all_to_all(outgoing, "expert", split_axis=0, concat_axis=0, tiled=True)
    flat_in = received.reshape(-1, model_width)
    hidden = jnp.dot(flat_in, up_local, preferred_element_type=jnp.float32) + up_shift
    active_low = gelu_exact(hidden).astype(jnp.bfloat16)
    produced = jnp.dot(active_low, down_local, preferred_element_type=jnp.float32) + down_shift
    produced_all = produced.astype(jnp.bfloat16).reshape(received.shape)
    returned = lax.all_to_all(produced_all, "expert", split_axis=0, concat_axis=0, tiled=True)
    expert_rows = returned[route_flat, slot_of].astype(jnp.float32)
    result = middle + gate_value[:, None] * expert_rows
    grad_out = cotangent.astype(jnp.float32).reshape(token_count, model_width)
    grad_expert = (grad_out * gate_value[:, None]).astype(jnp.bfloat16)
    grad_gate = jnp.sum(grad_out * expert_rows, axis=1)
    grad_logit = grad_gate * gate_value * (1.0 - gate_value)
    centroid_term = jnp.einsum(
        "te,td->ed",
        onehot.astype(jnp.float32),
        grad_logit[:, None] * normed_two,
        precision=lax.Precision.HIGHEST,
    )
    outgoing_grad = empty_slots.at[route_flat, slot_of].set(grad_expert)
    received_grad = lax.all_to_all(outgoing_grad, "expert", split_axis=0, concat_axis=0, tiled=True)
    flat_in = received.reshape(-1, model_width)
    flat_grad = received_grad.reshape(-1, model_width)
    hidden = jnp.dot(flat_in, up_local, preferred_element_type=jnp.float32) + up_shift
    active, gelu_back = jax.vjp(gelu_exact, hidden)
    active_low = active.astype(jnp.bfloat16)
    grad_active = jnp.einsum("sd,fd->sf", flat_grad, down_local, preferred_element_type=jnp.float32)
    (grad_hidden,) = gelu_back(grad_active)
    grad_hidden_low = grad_hidden.astype(jnp.bfloat16)
    down_term = jnp.einsum("sf,sd->fd", active_low, flat_grad, preferred_element_type=jnp.float32)
    down_shift_term = jnp.sum(flat_grad.astype(jnp.float32), axis=0)
    up_term = jnp.einsum("sd,sf->df", flat_in, grad_hidden_low, preferred_element_type=jnp.float32)
    up_shift_term = jnp.sum(grad_hidden_low.astype(jnp.float32), axis=0)
    grad_in = (
        jnp.einsum("sf,df->sd", grad_hidden_low, up_local, preferred_element_type=jnp.float32)
        .astype(jnp.bfloat16)
        .reshape(received.shape)
    )
    grad_back = lax.all_to_all(grad_in, "expert", split_axis=0, concat_axis=0, tiled=True)
    grad_from_expert = grad_back[route_flat, slot_of].astype(jnp.float32)
    up_sum, up_shift_sum, down_sum, down_shift_sum = (
        lax.psum_scatter(
            up_term.astype(jnp.bfloat16), "blk", scatter_dimension=0, tiled=True
        ).astype(jnp.float32),
        lax.psum_scatter(
            up_shift_term.astype(jnp.bfloat16), "blk", scatter_dimension=0, tiled=True
        ).astype(jnp.float32),
        lax.psum_scatter(
            down_term.astype(jnp.bfloat16), "blk", scatter_dimension=0, tiled=True
        ).astype(jnp.float32),
        lax.psum_scatter(
            down_shift_term.astype(jnp.bfloat16), "blk", scatter_dimension=0, tiled=True
        ).astype(jnp.float32),
    )
    grad_normed_two = grad_from_expert + grad_logit[:, None] * centroid_rows
    grad_middle_norm, ln2_gain_term, ln2_bias_term = norm_back_two(grad_normed_two)
    grad_middle = grad_out + grad_middle_norm
    out_shift_term = jnp.sum(grad_middle, axis=0)
    grad_middle_low = grad_middle.astype(jnp.bfloat16)
    out_term = jnp.einsum(
        "td,te->de", attended_low, grad_middle_low, preferred_element_type=jnp.float32
    )
    grad_attended = jnp.einsum(
        "te,de->td", grad_middle_low, full_out, preferred_element_type=jnp.float32
    ).astype(jnp.bfloat16)
    grad_four = grad_attended.reshape(four_shape)
    row_delta = jnp.sum(grad_four.astype(jnp.float32) * attended, axis=-1).transpose(0, 2, 1)
    zero_four = jnp.zeros(four_shape, jnp.float32)

    def grad_step(grad_query, column):
        visible, key_part, value_part = span_view(column)

        def grad_compute(grad_query):
            grad_scores, weights_low = pair_grads(
                query_four,
                grad_four,
                log_total,
                row_delta,
                key_part,
                value_part,
                visible,
                score_scale,
            )
            grad_query = (
                grad_query
                + jnp.einsum(
                    "rhqk,rkhd->rqhd", grad_scores, key_part, preferred_element_type=jnp.float32
                )
                * score_scale
            )
            key_term = (
                jnp.einsum(
                    "rhqk,rqhd->rkhd", grad_scores, query_four, preferred_element_type=jnp.float32
                )
                * score_scale
            )
            value_term = jnp.einsum(
                "rhqk,rqhd->rkhd", weights_low, grad_four, preferred_element_type=jnp.float32
            )
            return (
                grad_query,
                (
                    key_term.reshape(row_count, span_len, model_width),
                    value_term.reshape(row_count, span_len, model_width),
                ),
            )

        def skipped(grad_query):
            empty_term = jnp.zeros((row_count, span_len, model_width), jnp.float32)
            return (grad_query, (empty_term, empty_term))

        return lax.cond(jnp.any(visible), grad_compute, skipped, grad_query)

    grad_query, (key_stack, value_stack) = lax.scan(grad_step, zero_four, span_steps)
    grad_key, grad_value = (
        lax.psum_scatter(
            key_stack.astype(jnp.bfloat16), "blk", scatter_dimension=0, tiled=True
        ).astype(jnp.float32),
        lax.psum_scatter(
            value_stack.astype(jnp.bfloat16), "blk", scatter_dimension=0, tiled=True
        ).astype(jnp.float32),
    )
    grad_qkv_low = jnp.concatenate(
        [
            grad_query.reshape(token_count, model_width),
            grad_key.reshape(token_count, model_width),
            grad_value.reshape(token_count, model_width),
        ],
        axis=1,
    ).astype(jnp.bfloat16)
    qkv_term = jnp.einsum("td,te->de", normed_low, grad_qkv_low, preferred_element_type=jnp.float32)
    grad_qkv_wide = grad_qkv_low.astype(jnp.float32)
    qv_term = jnp.stack(
        [
            jnp.sum(grad_qkv_wide[:, :model_width], axis=0),
            jnp.sum(grad_qkv_wide[:, 2 * model_width :], axis=0),
        ]
    )
    grad_normed_one = jnp.einsum(
        "te,de->td", grad_qkv_low, full_qkv, preferred_element_type=jnp.float32
    )
    grad_tokens_norm, ln1_gain_term, ln1_bias_term = norm_back_one(grad_normed_one)
    grad_tokens = grad_middle + grad_tokens_norm
    (
        qkv_part,
        out_part,
        qv_part,
        shift_part,
        gain_one_part,
        bias_one_part,
        gain_two_part,
        bias_two_part,
        centroid_part,
    ) = (
        lax.psum_scatter(
            qkv_term.astype(jnp.bfloat16), "expert", scatter_dimension=0, tiled=True
        ).astype(jnp.float32),
        lax.psum_scatter(
            out_term.astype(jnp.bfloat16), "expert", scatter_dimension=0, tiled=True
        ).astype(jnp.float32),
        lax.psum_scatter(
            qv_term.astype(jnp.bfloat16), "expert", scatter_dimension=1, tiled=True
        ).astype(jnp.float32),
        lax.psum_scatter(
            out_shift_term.astype(jnp.bfloat16), "expert", scatter_dimension=0, tiled=True
        ).astype(jnp.float32),
        lax.psum_scatter(
            ln1_gain_term.astype(jnp.bfloat16), "expert", scatter_dimension=0, tiled=True
        ).astype(jnp.float32),
        lax.psum_scatter(
            ln1_bias_term.astype(jnp.bfloat16), "expert", scatter_dimension=0, tiled=True
        ).astype(jnp.float32),
        lax.psum_scatter(
            ln2_gain_term.astype(jnp.bfloat16), "expert", scatter_dimension=0, tiled=True
        ).astype(jnp.float32),
        lax.psum_scatter(
            ln2_bias_term.astype(jnp.bfloat16), "expert", scatter_dimension=0, tiled=True
        ).astype(jnp.float32),
        lax.psum_scatter(
            centroid_term.astype(jnp.bfloat16), "expert", scatter_dimension=1, tiled=True
        ).astype(jnp.float32),
    )
    (
        qkv_sum,
        out_sum,
        qv_sum,
        shift_sum,
        gain_one_sum,
        bias_one_sum,
        gain_two_sum,
        bias_two_sum,
        centroid_sum,
    ) = (
        lax.psum(qkv_part.astype(jnp.bfloat16), "blk").astype(jnp.float32),
        lax.psum(out_part.astype(jnp.bfloat16), "blk").astype(jnp.float32),
        lax.psum(qv_part.astype(jnp.bfloat16), "blk").astype(jnp.float32),
        lax.psum(shift_part.astype(jnp.bfloat16), "blk").astype(jnp.float32),
        lax.psum(gain_one_part.astype(jnp.bfloat16), "blk").astype(jnp.float32),
        lax.psum(bias_one_part.astype(jnp.bfloat16), "blk").astype(jnp.float32),
        lax.psum(gain_two_part.astype(jnp.bfloat16), "blk").astype(jnp.float32),
        lax.psum(bias_two_part.astype(jnp.bfloat16), "blk").astype(jnp.float32),
        lax.psum(centroid_part.astype(jnp.bfloat16), "blk").astype(jnp.float32),
    )
    return (
        result.reshape(row_count, span_len, model_width),
        grad_tokens.reshape(row_count, span_len, model_width),
        gain_one_sum,
        bias_one_sum,
        qkv_sum,
        qv_sum,
        out_sum,
        shift_sum,
        gain_two_sum,
        bias_two_sum,
        centroid_sum,
        up_sum[None],
        up_shift_sum[None],
        down_sum[None],
        down_shift_sum[None],
    )


def solution(mesh):
    return jax.shard_map(
        on_device,
        mesh=mesh,
        in_specs=(
            P("expert", "blk", None),
            P("expert", None),
            P("blk", "expert", None, None),
            P(),
            P(),
            P("expert", None),
            P(),
            P("expert", None),
            P(),
            P(),
            P(),
            P(),
            P("expert", None, None),
            P("expert", None),
            P("expert", None, None),
            P("expert", None),
            P("expert", "blk", None),
        ),
        out_specs=(
            P("expert", "blk", None),
            P("expert", "blk", None),
            P("expert"),
            P("expert"),
            P("expert", None),
            P(None, "expert"),
            P("expert", None),
            P("expert"),
            P("expert"),
            P("expert"),
            P(None, "expert"),
            P("expert", "blk", None),
            P("expert", "blk"),
            P("expert", "blk", None),
            P("expert", "blk"),
        ),
        check_vma=False,
    )
```

profile of v0, /device:TPU:0, one launch (start us, length us, event | category | flops | bytes accessed | tf_op | source)
XLA Modules:
  0.0 1687.8 jit_solution(6118853076410827704)
XLA Ops:
  13.0 33.6 %all-gather.5.cloned.1.call-done = bf16[768,2304]{1,0:T(8,128)(2,1)} async-done(((bf16[96,2304]{1,0:T(8,128)(2,1)}), bf16[768,2304]{1,0:T(8,128)(2,1)}) %all-gather.5.cloned.1.call-update) | async-done | bytes 3538960 | tf_op jit(solution)/shard_map/all_gather | solution.py:76
  69.0 103.3 %all-gather.7.cloned.1.call-done = bf16[2,2048,768]{1,2,0:T(8,128)(2,1)} async-done(((bf16[2,512,768]{1,2,0:T(8,128)(2,1)}), bf16[2,2048,768]{1,2,0:T(8,128)(2,1)}) %all-gather.7.cloned.1.call-update) | async-done | bytes 6291472 | tf_op jit(solution)/shard_map/all_gather | solution.py:92
  172.3 41.2 %while.45 = (s32[]{:T(128)}, f32[2,12,512]{2,1,0:T(8,128)S(1)}, f32[2,12,512]{2,1,0:T(8,128)S(1)}, s32[2,512]{1,0:T(2,128)S(1)}, s32[4]{0:T(128)S(1)}, /*index=5...) while((s32[]{:T(128)}, f32[2,12,512]{2,1,0:T(8,128)S(1)}, ...), condition=%wide.region_8.9_spmd.clone, body=%wide.region_2.8_spmd.clone.sunk | while | flops 857498624 | bytes 59384100 | solution.py:127
  176.4 24.8 %conditional.9 = ((f32[2,12,512]{2,1,0:T(8,128)S(1)}, f32[2,12,512]{2,1,0:T(8,128)S(1)})) conditional(s32[]{:T(128)} %convert_element_type.316, (f32[2,12,512]{2,1,0:T(8,128)S(1)}, f32[2,12,512]{2,1,0:T(8,128)S(1)}) %tuple.148, (pred[2,512,512]{1,2,0:T(8,128)(4,1)S(1)}, bf16[2,2048,768]{1,2,0:T(8,128)(2,1)}, s32[]{:T(128)}, ...), branch_computations={%region_4.4_spmd, %region_5.7_spmd} | conditional | flops 855662592 | bytes 58310684 | solution.py:123
  213.5 74.5 %all-gather.9.cloned.1.call-done = bf16[2,2048,768]{1,2,0:T(8,128)(2,1)} async-done(((bf16[2,512,768]{1,2,0:T(8,128)(2,1)}), bf16[2,2048,768]{1,2,0:T(8,128)(2,1)}) %all-gather.9.cloned.1.call-update) | async-done | bytes 6291472 | tf_op jit(solution)/shard_map/all_gather | solution.py:93
  290.1 35.8 %while.46 = (s32[]{:T(128)}, f32[2,512,12,64]{1,3,2,0:T(8,128)}, s32[2,512]{1,0:T(2,128)S(1)}, s32[4]{0:T(128)S(1)}, s32[2,2048]{1,0:T(2,128)}, /*index=5*/bf16[...) while((s32[]{:T(128)}, f32[2,512,12,64]{1,3,2,0:T(8,128)}, ...), condition=%wide.region_13.14_spmd.clone, body=%wide.region_9.13_spmd.clone.sunk | while | flops 1638401024 | bytes 18948372 | solution.py:142
  349.6 37.3 %all-to-all-done = bf16[8,256,768]{2,1,0:T(8,128)(2,1)S(1)} async-done(((bf16[8,256,768]{2,1,0:T(8,128)(2,1)}), bf16[8,256,768]{2,1,0:T(8,128)(2,1)S(1)}, u32[]{:S(2)}, u32[]{:S(2)}) %all-to-all-start) | async-done | bytes 3145760 | tf_op jit(solution)/shard_map/all_to_all | solution.py:165
  386.9 64.2 %multiply_convert_fusion = (bf16[2048,3072]{1,0:T(8,128)(2,1)S(1)}, f32[2048,3072]{1,0:T(8,128)}, f32[2048,3072]{1,0:T(8,128)}) fusion(f32[3072]{0:T(1024)S(1)} %bitcast.262, bf16[2048,768]{1,0:T(8,128)(2,1)S(1)} %bitcast.231, bf16[1,768,3072]{2,1,0:T(8,128)(2,1)} %param.41), kind=kOutput, calls=%fused_computation.58 | convolution fusion | flops 10078912512 | bytes 70791168 | tf_op jit(solution)/shard_map/dot_general | solution.py:167
  471.0 33.3 %all-to-all-done.1 = bf16[8,256,768]{2,1,0:T(8,128)(2,1)S(1)} async-done(((bf16[8,256,768]{2,1,0:T(8,128)(2,1)}), bf16[8,256,768]{2,1,0:T(8,128)(2,1)S(1)}, u32[]{:S(2)}, u32[]{:S(2)}) %all-to-all-start.1) | async-done | bytes 3145760 | tf_op jit(solution)/shard_map/all_to_all | solution.py:171
  528.5 41.6 %all_to_all.20 = bf16[8,256,768]{2,1,0:T(8,128)(2,1)S(1)} all-to-all(bf16[8,256,768]{2,1,0:T(8,128)(2,1)} %bitcast.223), channel_id=1, replica_groups=mesh['blk'=4,'expert'=8] {'expert'}, dimensions={0} | all-to-all | bytes 6291456 | tf_op jit(solution)/shard_map/all_to_all | solution.py:185
  570.1 29.1 %fusion.104 = (bf16[3072]{0:T(1024)(128)(2,1)}, bf16[2048,3072]{1,0:T(8,128)(2,1)}) fusion(f32[2048,3072]{1,0:T(8,128)} %get-tuple-element.694, bf16[2048,768]{1,0:T(8,128)(2,1)S(1)} %bitcast.220, bf16[1,3072,768]{2,1,0:T(8,128)(2,1)} %param.43, f32[2048,3072]{1,0:T(8,128)} %get-tuple-element.720, f32[3072]{0:T(1024)S(1)} %bitcast.263), kind=kOutput, calls=%fused_computation.194 | convolution fusion | flops 9764336640 | bytes 70797312 | tf_op jit(solution)/shard_map/sd,fd->sf/dot_general | solution.py:191
  618.4 37.7 %all-to-all-done.3 = bf16[8,256,768]{2,1,0:T(8,128)(2,1)S(1)} async-done(((bf16[8,256,768]{2,1,0:T(8,128)(2,1)}), bf16[8,256,768]{2,1,0:T(8,128)(2,1)S(1)}, u32[]{:S(2)}, u32[]{:S(2)}) %all-to-all-start.3) | async-done | bytes 3145760 | tf_op jit(solution)/shard_map/all_to_all | solution.py:203
  699.8 138.2 %while.47 = (s32[]{:T(128)}, f32[2,512,12,64]{1,3,2,0:T(8,128)S(1)}, bf16[4,2,512,768]{3,2,1,0:T(8,128)(2,1)}, bf16[4,2,512,768]{3,2,1,0:T(8,128)(2,1)}, s32[2,5...) while((s32[]{:T(128)}, ...), condition=%wide.region_30.31_spmd.clone, body=%wide.region_26.30_spmd.clone.sunk | while | flops 4094428160 | bytes 186295232 | solution.py:278
  715.4 64.4 %conditional.11 = (f32[2,512,12,64]{1,3,2,0:T(8,128)S(1)}, bf16[1,2,512,768]{2,3,1,0:T(8,128)(2,1)}, bf16[1,2,512,768]{2,3,1,0:T(8,128)(2,1)}) conditional(s32[]{:T(128)} %convert_element_type.318, f32[2,512,12,64]{1,3,2,0:T(8,128)S(1)} %get-tuple-element.1071, (pred[2,512,512]{1,2,0:T(8,128)(4,1)}, bf16[2,2048,768]{1,2,0:T(8,128)(2,1)}, ...), branch_computations={%region_28.28_spmd, %region_29.29_spmd} | conditional | flops 4092592128 | bytes 172638336 | solution.py:276
  882.3 296.2 %reduce-scatter.13.cloned.1.call-done = bf16[1,2,512,768]{3,2,1,0:T(8,128)(2,1)} async-done(((bf16[4,2,512,768]{3,2,1,0:T(8,128)(2,1)}), bf16[1,2,512,768]{3,2,1,0:T(8,128)(2,1)}) %reduce-scatter.13.cloned.1.call-update) | async-done | bytes 1572880 | tf_op jit(solution)/shard_map/reduce_scatter | solution.py:280
  1180.3 111.7 %reduce-scatter.15.cloned.1.call-done = bf16[1,2,512,768]{3,2,1,0:T(8,128)(2,1)} async-done(((bf16[4,2,512,768]{3,2,1,0:T(8,128)(2,1)}), bf16[1,2,512,768]{3,2,1,0:T(8,128)(2,1)}) %reduce-scatter.15.cloned.1.call-update) | async-done | bytes 1572880 | tf_op jit(solution)/shard_map/reduce_scatter | solution.py:283
  1305.9 23.7 %reduce-scatter.27.cloned.1.call-done = bf16[96,8]{1,0:T(8,128)(2,1)} async-done(((bf16[768,8]{1,0:T(8,128)(2,1)}), bf16[96,8]{1,0:T(8,128)(2,1)}) %reduce-scatter.27.cloned.1.call-update) | async-done | bytes 1552
  1331.0 86.4 %reduce-scatter.23.cloned.1.call-done = bf16[768,768]{1,0:T(8,128)(2,1)} async-done(((bf16[3072,768]{1,0:T(8,128)(2,1)}), bf16[768,768]{1,0:T(8,128)(2,1)}) %reduce-scatter.23.cloned.1.call-update) | async-done | bytes 1179664 | tf_op jit(solution)/shard_map/reduce_scatter | solution.py:212
  1420.2 85.4 %reduce-scatter.21.cloned.1.call-done = bf16[192,3072]{1,0:T(8,128)(2,1)} async-done(((bf16[768,3072]{1,0:T(8,128)(2,1)}), bf16[192,3072]{1,0:T(8,128)(2,1)}) %reduce-scatter.21.cloned.1.call-update) | async-done | bytes 1179664 | tf_op jit(solution)/shard_map/reduce_scatter | solution.py:206
  1523.7 24.2 %all-reduce.7 = (bf16[768]{0:T(1024)(128)(2,1)S(1)}, bf16[768]{0:T(1024)(128)(2,1)S(1)}, bf16[768]{0:T(1024)(128)(2,1)S(1)}, bf16[768]{0:T(1024)(128)(2,1)S(1)}, bf16[768]{0:T(1024)(128)(2,1)S(1)}) all-reduce(bf16[768]{0:T(1024)(128)(2,1)S(1)} %get-tuple-element.594, ...), channel_id=4, replica_groups=mesh['blk'=4,'expert'=8] {'expert'}, use_global_device_ids=true, to_apply=%region_36.37.clone | all-reduce | flops 3840 | bytes 15360
  1548.3 49.9 %reduce-scatter.17.cloned.1.call-done = bf16[96,2304]{1,0:T(8,128)(2,1)} async-done(((bf16[768,2304]{1,0:T(8,128)(2,1)}), bf16[96,2304]{1,0:T(8,128)(2,1)}) %reduce-scatter.17.cloned.1.call-update) | async-done | bytes 442384 | tf_op jit(solution)/shard_map/reduce_scatter | solution.py:319
  1602.8 32.3 %reduce-scatter.25.cloned.1.call-done = bf16[96,2]{1,0:T(8,128)(2,1)} async-done(((bf16[768,2]{1,0:T(8,128)(2,1)}), bf16[96,2]{1,0:T(8,128)(2,1)}) %reduce-scatter.25.cloned.1.call-update) | async-done | bytes 400
  1635.9 19.0 %all-reduce.8 = (bf16[96]{0:T(256)(128)(2,1)S(1)}, bf16[96]{0:T(256)(128)(2,1)S(1)}, bf16[2,96]{1,0:T(2,128)(2,1)S(1)}, bf16[96]{0:T(256)(128)(2,1)S(1)}, bf16[9...) all-reduce(bf16[96]{0:T(256)(128)(2,1)S(1)} %dynamic-slice.1, ...), channel_id=1, replica_groups=mesh['blk'=4,'expert'=8] {'blk'}, use_global_device_ids=true, to_apply=%region_37.38 | all-reduce | flops 5280 | bytes 21120 | tf_op jit(solution)/shard_map/psum | solution.py:362
  1659.9 17.6 %all-reduce.12.cloned.1.call-done = (bf16[96,2304]{1,0:T(8,128)(2,1)}, bf16[96,768]{1,0:T(8,128)(2,1)}) async-done(((bf16[96,2304]{1,0:T(8,128)(2,1)}, bf16[96,768]{1,0:T(8,128)(2,1)}), (bf16[96,2304]{1,0:T(8,128)(2,1)}, bf16[96,768]{1,0:T(8,128)(2,1)})) %all-reduce.12.cloned.1.call-update) | async-done | bytes 589840 | tf_op jit(solution)/shard_map/psum | solution.py:358
  (402 shorter events, 466.6 us)
Async XLA Ops:
  7.2 459.3 %copy-start = (bf16[8,768]{1,0:T(8,128)(2,1)S(1)}, bf16[8,768]{1,0:T(8,128)(2,1)}, u32[]{:S(2)}) copy-start(bf16[8,768]{1,0:T(8,128)(2,1)} %param.40) | copy-start | bytes 36868
  7.2 39.4 %all-gather.5.cloned.1.call-start = ((), (), s32[]{:S(2)}) async-start(), calls=%async_computation.12 | async-start | bytes 3981312 | tf_op jit(solution)/shard_map/all_gather | solution.py:76
  8.0 164.3 %all-gather.7.cloned.1.call-start = ((), (), s32[]{:S(2)}) async-start(), calls=%async_computation.13 | async-start | bytes 7864320 | tf_op jit(solution)/shard_map/all_gather | solution.py:92
  56.8 231.2 %all-gather.9.cloned.1.call-start = ((), (), s32[]{:S(2)}) async-start(), calls=%async_computation.14 | async-start | bytes 7864320 | tf_op jit(solution)/shard_map/all_gather | solution.py:93
  58.4 273.4 %all-gather.11.cloned.1.call-start = ((), (), s32[]{:S(2)}) async-start(), calls=%async_computation.15 | async-start | bytes 1327104 | tf_op jit(solution)/shard_map/all_gather | solution.py:77
  345.2 41.7 %all-to-all-start = ((bf16[8,256,768]{2,1,0:T(8,128)(2,1)}), bf16[8,256,768]{2,1,0:T(8,128)(2,1)S(1)}, u32[]{:S(2)}, u32[]{:S(2)}) async-start(bf16[8,256,768]{2,1,0:T(8,128)(2,1)} %bitcast.222), calls=%async_computation | async-start | bytes 6291456 | tf_op jit(solution)/shard_map/all_to_all | solution.py:165
  386.9 64.3 %copy-start.68 = (bf16[1,3072,768]{2,1,0:T(8,128)(2,1)S(1)}, bf16[1,3072,768]{2,1,0:T(8,128)(2,1)}, u32[]{:S(2)}) copy-start(bf16[1,3072,768]{2,1,0:T(8,128)(2,1)} %param.43) | copy-start | bytes 14155780
  462.5 41.8 %all-to-all-start.1 = ((bf16[8,256,768]{2,1,0:T(8,128)(2,1)}), bf16[8,256,768]{2,1,0:T(8,128)(2,1)S(1)}, u32[]{:S(2)}, u32[]{:S(2)}) async-start(bf16[8,256,768]{2,1,0:T(8,128)(2,1)} %bitcast.234), calls=%async_computation.1 | async-start | bytes 6291456 | tf_op jit(solution)/shard_map/all_to_all | solution.py:171
  520.7 154.5 %copy-start.49 = (f32[1024]{0:T(1024)}, f32[1024]{0:T(1024)S(1)}, u32[]{:S(2)}) copy-start(f32[1024]{0:T(1024)S(1)} %get-tuple-element.711) | copy-start | bytes 12292
  614.7 41.5 %all-to-all-start.3 = ((bf16[8,256,768]{2,1,0:T(8,128)(2,1)}), bf16[8,256,768]{2,1,0:T(8,128)(2,1)S(1)}, u32[]{:S(2)}, u32[]{:S(2)}) async-start(bf16[8,256,768]{2,1,0:T(8,128)(2,1)} %bitcast.233), calls=%async_computation.3 | async-start | bytes 6291456 | tf_op jit(solution)/shard_map/all_to_all | solution.py:203
  618.3 560.2 %reduce-scatter.13.cloned.1.call-start = ((), (), s32[]{:S(2)}) async-start(), calls=%async_computation.16 | async-start | bytes 7864320 | tf_op jit(solution)/shard_map/reduce_scatter | solution.py:280
  838.0 454.0 %reduce-scatter.15.cloned.1.call-start = ((), (), s32[]{:S(2)}) async-start(), calls=%async_computation.17 | async-start | bytes 7864320 | tf_op jit(solution)/shard_map/reduce_scatter | solution.py:283
  838.6 491.1 %reduce-scatter.27.cloned.1.call-start = ((), (), s32[]{:S(2)}) async-start(), calls=%async_computation.23 | async-start | bytes 221184
  843.3 574.1 %reduce-scatter.23.cloned.1.call-start = ((), (), s32[]{:S(2)}) async-start(), calls=%async_computation.21 | async-start | bytes 5898240 | tf_op jit(solution)/shard_map/reduce_scatter | solution.py:212
  859.2 646.4 %reduce-scatter.21.cloned.1.call-start = ((), (), s32[]{:S(2)}) async-start(), calls=%async_computation.20 | async-start | bytes 5898240 | tf_op jit(solution)/shard_map/reduce_scatter | solution.py:206
  874.7 673.5 %reduce-scatter.19.cloned.1.call-start = ((), (), s32[]{:S(2)}) async-start(), calls=%async_computation.19 | async-start | bytes 1327104 | tf_op jit(solution)/shard_map/reduce_scatter | solution.py:322
  880.0 718.2 %reduce-scatter.17.cloned.1.call-start = ((), (), s32[]{:S(2)}) async-start(), calls=%async_computation.18 | async-start | bytes 3981312 | tf_op jit(solution)/shard_map/reduce_scatter | solution.py:319
  882.3 412.3 %copy-start.20 = (bf16[96,8,2,512]{3,1,2,0:T(8,128)(2,1)}, bf16[96,8,2,512]{3,1,2,0:T(8,128)(2,1)S(1)}, u32[]{:S(2)}) copy-start(bf16[96,8,2,512]{3,1,2,0:T(8,128)(2,1)S(1)} %copy.135) | copy-start | bytes 4718596
  1180.3 114.4 %copy-start.22 = (bf16[1024,768]{0,1:T(8,128)(2,1)}, bf16[1024,768]{0,1:T(8,128)(2,1)S(1)}, u32[]{:S(2)}) copy-start(bf16[1024,768]{0,1:T(8,128)(2,1)S(1)} %copy.98) | copy-start | bytes 4718596
  1302.2 332.9 %reduce-scatter.25.cloned.1.call-start = ((), (), s32[]{:S(2)}) async-start(), calls=%async_computation.22 | async-start | bytes 221184
  1331.0 177.7 %copy-start.21 = (bf16[96,8,2,512]{3,1,2,0:T(8,128)(2,1)S(1)}, bf16[96,8,2,512]{3,1,2,0:T(8,128)(2,1)}, u32[]{:S(2)}) copy-start(bf16[96,8,2,512]{3,1,2,0:T(8,128)(2,1)} %copy-done.20) | copy-start | bytes 4718596
  1331.0 177.6 %copy-start.23 = (bf16[1024,768]{0,1:T(8,128)(2,1)S(1)}, bf16[1024,768]{0,1:T(8,128)(2,1)}, u32[]{:S(2)}) copy-start(bf16[1024,768]{0,1:T(8,128)(2,1)} %copy-done.22) | copy-start | bytes 4718596
  1520.5 157.0 %all-reduce.12.cloned.1.call-start = ((), (), s32[]{:S(2)}) async-start(), calls=%async_computation.24 | async-start | bytes 1179648 | tf_op jit(solution)/shard_map/psum | solution.py:358
  1598.2 82.9 %copy-start.1 = (bf16[8,768]{1,0:T(8,128)(2,1)S(1)}, bf16[8,768]{1,0:T(8,128)(2,1)}, u32[]{:S(2)}) copy-start(bf16[8,768]{1,0:T(8,128)(2,1)} %param.40) | copy-start | bytes 36868
  (67 other events, 562.5 us)
Sparse Core Ops, SparseCore 0:
  10.0 36.6 all-gather.4
  56.9 115.3 all-gather.6
  174.4 113.5 all-gather.8
  289.8 22.2 all-gather.10
  838.2 340.3 reduce-scatter.12
  1180.7 111.2 reduce-scatter.14
  1295.6 34.0 reduce-scatter.26
  1332.1 85.2 reduce-scatter.22
  1419.8 85.7 reduce-scatter.20
  1509.0 37.3 reduce-scatter.18
  1549.9 48.1 reduce-scatter.16
  1601.6 33.4 reduce-scatter.24
  1637.6 39.7 all-reduce.11
where the time goes:
time: 1690 us
  waiting for transfers between devices  1020 us (60%)
  matrix products  273 us (16%)
  local copies, waits for them, and re-layouts  150 us (9%)
  other arithmetic  98 us (6%)
  blocking collectives  84.8 us (5%)
  loops' own time  27.4 us (2%)
  between operations  17 us (1%)
    reduce_scatter x1, waiting for transfers between devices, on_device(): lax.psum_scatter(key_stack.astype(jnp.bfloat16), 'blk', scatter_dimension...  296 us
    reduce_scatter x1, waiting for transfers between devices, on_device(): lax.psum_scatter(value_stack.astype(jnp.bfloat16), 'blk', scatter_dimensi...  112 us
    all_gather x1, waiting for transfers between devices, on_device(): lax.all_gather(key_low, 'blk', axis=1, tiled=True)  103 us
    reduce_scatter x1, waiting for transfers between devices, on_device(): lax.psum_scatter(down_term.astype(jnp.bfloat16), 'blk', scatter_dimension...  86.4 us
    reduce_scatter x1, waiting for transfers between devices, on_device(): lax.psum_scatter(up_term.astype(jnp.bfloat16), 'blk', scatter_dimension=0...  85.4 us
    all_gather x1, waiting for transfers between devices, on_device(): lax.all_gather(value_low, 'blk', axis=1, tiled=True)  74.5 us
    dot_general x1, matrix products, on_device(): jnp.dot(flat_in, up_local, preferred_element_type=jnp.float32) + up_shift  64.2 us
    unnamed x15, waiting for transfers between devices  57.9 us
  transfers between devices with their start and end apart: 16, of which 14 were waited for; matrix products, arithmetic and copies ran while one was open for 11% of the time, Pallas kernels for 0%

commit v1 on v0

v1 whole, which is shorter than its diff:
```python
import functools

import jax
import jax.numpy as jnp
from jax import lax
from jax.experimental import pallas as pl
from jax.experimental.pallas import tpu as pltpu
from jax.sharding import PartitionSpec as P

HEADS = 12
SHORT = 256
NEGATIVE = -1e30
EPSILON = 1e-05
BF = jnp.bfloat16
F32 = jnp.float32


def dot_nn(a, b):
    return lax.dot_general(a, b, (((1,), (0,)), ((), ())), preferred_element_type=F32)


def dot_nt(a, b):
    return lax.dot_general(a, b, (((1,), (1,)), ((), ())), preferred_element_type=F32)


def norm_parts(values):
    average = jnp.mean(values, axis=-1, keepdims=True)
    centred = values - average
    variance = jnp.mean(centred * centred, axis=-1, keepdims=True)
    scale = lax.rsqrt(variance + EPSILON)
    return centred * scale, scale


def layer_norm(values, gain, bias):
    return norm_parts(values)[0] * gain + bias


def norm_back(upstream, normal, scale, gain):
    t = upstream * gain
    inner = (
        t
        - jnp.mean(t, axis=-1, keepdims=True)
        - normal * jnp.mean(t * normal, axis=-1, keepdims=True)
    )
    return inner * scale, jnp.sum(upstream * normal, axis=0), jnp.sum(upstream, axis=0)


def split_heads(qkv):
    size = qkv.shape[1] // 3
    scale = size ** (-0.5)
    return (
        (qkv[:, :size].astype(F32) * scale).astype(BF),
        qkv[:, size : 2 * size],
        qkv[:, 2 * size :],
    )


def causal(rows, columns, shift):
    row = lax.broadcasted_iota(jnp.int32, (rows, columns), 0)
    column = lax.broadcasted_iota(jnp.int32, (rows, columns), 1)
    return row <= column + shift


def long_forward(x_ref, w_ref, b_ref, qkv_ref, wide_ref, low_ref, total_ref, *, block):
    qkv = (dot_nn(x_ref[...], w_ref[0]) + b_ref[0]).astype(BF)
    qkv_ref[0] = qkv
    query, key, value = split_heads(qkv)
    value_t = value.T
    visible = causal(block, block, 0)
    for i in range(x_ref.shape[0] // block):
        lo, hi = i * block, (i + 1) * block
        own = query[lo:hi]
        near = jnp.where(visible, dot_nt(key[lo:hi], own), NEGATIVE)
        top = jnp.max(near, axis=0, keepdims=True)
        if i:
            far = dot_nt(key[:lo], own)
            top = jnp.maximum(top, jnp.max(far, axis=0, keepdims=True))
        near = jnp.exp(near - top)
        total = jnp.sum(near, axis=0, keepdims=True)
        out = dot_nn(value_t[:, lo:hi], near.astype(BF))
        if i:
            far = jnp.exp(far - top)
            total = total + jnp.sum(far, axis=0, keepdims=True)
            out = out + dot_nn(value_t[:, :lo], far.astype(BF))
        out = out / total
        wide_ref[:, lo:hi] = out
        low_ref[i] = out.astype(BF)
        total_ref[0, :, lo:hi] = top + jnp.log(total)


def long_backward(
    qkv_ref, grad_ref, wide_ref, total_ref, out_ref, key_acc, value_acc, *, block
):
    query, key, value = split_heads(qkv_ref[0])
    size = query.shape[1]
    scale = size ** (-0.5)
    key_t = key.T
    visible = causal(block, block, 0)
    count = query.shape[0] // block
    key_acc[...] = jnp.zeros_like(key_acc)
    value_acc[...] = jnp.zeros_like(value_acc)
    for i in range(count):
        lo, hi = i * block, (i + 1) * block
        own = query[lo:hi]
        grad_t = grad_ref[i]
        grad = grad_t.T
        delta = jnp.sum(grad_t.astype(F32) * wide_ref[:, lo:hi], axis=0, keepdims=True)
        total = total_ref[0, :, lo:hi]
        query_grad = None
        for start, stop in ((lo, hi), (0, lo)):
            if start == stop:
                continue
            weights = jnp.exp(dot_nt(key[start:stop], own) - total)
            if start == lo:
                weights = jnp.where(visible, weights, 0.0)
            scores = weights * (dot_nt(value[start:stop], grad) - delta)
            scores_low = scores.astype(BF)
            value_acc[start:stop] += dot_nn(weights.astype(BF), grad)
            key_acc[start:stop] += dot_nn(scores_low, own)
            part = dot_nn(key_t[:, start:stop], scores_low)
            query_grad = part if query_grad is None else query_grad + part
        out_ref[i, 0] = (query_grad * scale).astype(BF)
    key_grad = key_acc[...].T.astype(BF)
    value_grad = value_acc[...].T.astype(BF)
    for i in range(count):
        out_ref[i, 1] = key_grad[:, i * block : (i + 1) * block]
        out_ref[i, 2] = value_grad[:, i * block : (i + 1) * block]


def short_visible(key_ids, query_ids, i, block, halo):
    lo = i * block
    same = key_ids[lo : lo + halo + block] == query_ids[:, lo : lo + block]
    return same & causal(halo + block, block, halo)


def short_forward(
    x_ref, w_ref, b_ref, key_ids, query_ids, qkv_ref, wide_ref, low_ref, total_ref, *, block
):
    qkv = (dot_nn(x_ref[...], w_ref[0]) + b_ref[0]).astype(BF)
    qkv_ref[0] = qkv
    query, key, value = split_heads(qkv)
    value_t = value.T
    span = query_ids.shape[1]
    halo = x_ref.shape[0] - span
    for i in range(span // block):
        lo, hi = i * block, (i + 1) * block
        visible = short_visible(key_ids[...], query_ids[...], i, block, halo)
        scores = dot_nt(key[lo : hi + halo], query[lo + halo : hi + halo])
        scores = jnp.where(visible, scores, NEGATIVE)
        top = jnp.max(scores, axis=0, keepdims=True)
        scores = jnp.exp(scores - top)
        total = jnp.sum(scores, axis=0, keepdims=True)
        out = dot_nn(value_t[:, lo : hi + halo], scores.astype(BF)) / total
        wide_ref[:, lo:hi] = out
        low_ref[:, lo:hi] = out.astype(BF)
        total_ref[0, :, lo:hi] = top + jnp.log(total)


def short_backward(
    qkv_ref,
    grad_ref,
    wide_ref,
    total_ref,
    key_ids,
    query_ids,
    query_out,
    own_out,
    halo_out,
    key_acc,
    value_acc,
    *,
    block,
):
    query, key, value = split_heads(qkv_ref[0])
    scale = query.shape[1] ** (-0.5)
    key_t = key.T
    span = query_ids.shape[1]
    halo = query.shape[0] - span
    key_acc[...] = jnp.zeros_like(key_acc)
    value_acc[...] = jnp.zeros_like(value_acc)
    for i in range(span // block):
        lo, hi = i * block, (i + 1) * block
        visible = short_visible(key_ids[...], query_ids[...], i, block, halo)
        own = query[lo + halo : hi + halo]
        grad_t = grad_ref[:, lo:hi]
        grad = grad_t.T
        delta = jnp.sum(grad_t.astype(F32) * wide_ref[:, lo:hi], axis=0, keepdims=True)
        scores = dot_nt(key[lo : hi + halo], own)
        weights = jnp.exp(jnp.where(visible, scores, NEGATIVE) - total_ref[0, :, lo:hi])
        scores = weights * (dot_nt(value[lo : hi + halo], grad) - delta)
        scores_low = scores.astype(BF)
        value_acc[lo : hi + halo] += dot_nn(weights.astype(BF), grad)
        key_acc[lo : hi + halo] += dot_nn(scores_low, own)
        part = dot_nn(key_t[:, lo : hi + halo], scores_low)
        query_out[:, lo:hi] = (part * scale).astype(BF)
    for n, acc in enumerate((key_acc, value_acc)):
        whole = acc[...].T
        halo_out[n] = whole[:, :halo].astype(BF)
        own_out[n] = whole[:, halo:]


def whole_spec(shape):
    return pl.BlockSpec(shape, lambda *_: (0,) * len(shape))


def call(kernel, grid, ins, in_specs, outs, out_specs, scratch, flops, bytes_accessed, vmem=56 << 20):
    return pl.pallas_call(
        kernel,
        grid=grid,
        in_specs=in_specs,
        out_specs=out_specs,
        out_shape=outs,
        scratch_shapes=scratch,
        compiler_params=pltpu.CompilerParams(vmem_limit_bytes=vmem),
        cost_estimate=pl.CostEstimate(
            flops=int(flops), bytes_accessed=int(bytes_accessed), transcendentals=0
        ),
    )(*ins)


def gelu_parts(hidden):
    cdf = 0.5 * (1.0 + lax.erf(hidden * 0.7071067811865476))
    density = jnp.exp(-0.5 * hidden * hidden) * 0.3989422804014327
    return hidden * cdf, cdf + hidden * density


def expert_kernel(
    x_ref,
    cot_ref,
    up_ref,
    down_ref,
    up_shift_ref,
    down_shift_ref,
    centroid_ref,
    out_ref,
    grad_ref,
    up_out,
    down_out,
    up_shift_out,
    down_shift_out,
    gate_ref,
    low_ref,
    xt_ref,
    gt_ref,
    out_acc,
    grad_acc,
    *,
    chunk,
):
    step = pl.program_id(0)
    rows = x_ref.shape[0]

    @pl.when(step == 0)
    def _():
        for lo in range(0, rows, chunk):
            x = x_ref[lo : lo + chunk]
            logit = jnp.sum(x.astype(F32) * centroid_ref[...], axis=1, keepdims=True)
            gate = 1.0 / (1.0 + jnp.exp(-logit))
            gate_ref[lo : lo + chunk] = gate
            low = (cot_ref[lo : lo + chunk].astype(F32) * gate).astype(BF)
            low_ref[lo : lo + chunk] = low
            xt_ref[:, lo : lo + chunk] = x.T
            gt_ref[:, lo : lo + chunk] = low.T
            part = jnp.sum(low.astype(F32), axis=0, keepdims=True)
            if lo:
                down_shift_out[...] += part
            else:
                down_shift_out[...] = part
        out_acc[...] = jnp.zeros_like(out_acc)
        grad_acc[...] = jnp.zeros_like(grad_acc)

    up_total = None
    for lo in range(0, rows, chunk):
        x = x_ref[lo : lo + chunk]
        low = low_ref[lo : lo + chunk]
        hidden = dot_nn(x, up_ref[...]) + up_shift_ref[...]
        active, slope = gelu_parts(hidden)
        active = active.astype(BF)
        grad_hidden = dot_nt(low, down_ref[...]) * slope
        grad_low = grad_hidden.astype(BF)
        out_acc[lo : lo + chunk] += dot_nn(active, down_ref[...])
        grad_acc[lo : lo + chunk] += dot_nt(grad_low, up_ref[...])
        up_part = dot_nn(xt_ref[:, lo : lo + chunk], grad_low)
        down_part = dot_nn(gt_ref[:, lo : lo + chunk], active)
        shift_part = jnp.sum(grad_low.astype(F32), axis=0, keepdims=True)
        if up_total is None:
            up_total, down_total, shift_total = up_part, down_part, shift_part
        else:
            up_total, down_total, shift_total = (
                up_total + up_part,
                down_total + down_part,
                shift_total + shift_part,
            )
    up_out[...] = up_total.astype(BF)
    down_out[0] = down_total.astype(BF)
    up_shift_out[...] = shift_total

    @pl.when(step == pl.num_programs(0) - 1)
    def _():
        for lo in range(0, rows, chunk):
            gate = gate_ref[lo : lo + chunk]
            out = (out_acc[lo : lo + chunk] + down_shift_ref[...]).astype(BF)
            out_ref[lo : lo + chunk] = out
            inner = jnp.sum(
                cot_ref[lo : lo + chunk].astype(F32) * out.astype(F32), axis=1, keepdims=True
            )
            logit_grad = inner * gate * (1.0 - gate)
            grad_ref[lo : lo + chunk] = (
                grad_acc[lo : lo + chunk] + logit_grad * centroid_ref[...]
            ).astype(BF)


def run_expert(x, cot, up_weight, down_weight, up_shift, down_shift, centroid, slices):
    rows, width = x.shape
    hidden = up_weight.shape[1]
    block = hidden // 8
    per = hidden // slices // block
    chunk = min(512, rows)
    steps = hidden // block
    return call(
        functools.partial(expert_kernel, chunk=chunk),
        (steps,),
        (x, cot, up_weight, down_weight, up_shift, down_shift, centroid),
        [
            whole_spec((rows, width)),
            whole_spec((rows, width)),
            pl.BlockSpec((width, block), lambda f: (0, f)),
            pl.BlockSpec((block, width), lambda f: (f, 0)),
            pl.BlockSpec((1, block), lambda f: (0, f)),
            whole_spec((1, width)),
            whole_spec((1, width)),
        ],
        (
            jax.ShapeDtypeStruct((rows, width), BF),
            jax.ShapeDtypeStruct((rows, width), BF),
            jax.ShapeDtypeStruct((width, hidden), BF),
            jax.ShapeDtypeStruct((slices, width, hidden // slices), BF),
            jax.ShapeDtypeStruct((1, hidden), F32),
            jax.ShapeDtypeStruct((1, width), F32),
        ),
        (
            whole_spec((rows, width)),
            whole_spec((rows, width)),
            pl.BlockSpec((width, block), lambda f: (0, f)),
            pl.BlockSpec((1, width, block), lambda f: (f // per, 0, f % per)),
            pl.BlockSpec((1, block), lambda f: (0, f)),
            whole_spec((1, width)),
        ),
        [
            pltpu.VMEM((rows, 1), F32),
            pltpu.VMEM((rows, width), BF),
            pltpu.VMEM((width, rows), BF),
            pltpu.VMEM((width, rows), BF),
            pltpu.VMEM((rows, width), F32),
            pltpu.VMEM((rows, width), F32),
        ],
        12 * rows * width * hidden,
        8 * width * hidden + 8 * rows * width,
    )


def halving_scatter(parts, axis, count):
    me = lax.axis_index(axis)
    bit = 1
    held = parts
    while bit < count:
        pairs = [(i, i ^ bit) for i in range(count)]
        half = held.reshape((held.shape[0] // 2, 2) + held.shape[1:])
        mine = (me // bit) % 2
        keep = lax.dynamic_index_in_dim(half, mine, 1, keepdims=False)
        send = lax.dynamic_index_in_dim(half, 1 - mine, 1, keepdims=False)
        came = lax.ppermute(send, axis, pairs)
        held = keep.astype(F32) + came.astype(F32)
        bit *= 2
        if bit < count:
            held = held.astype(BF)
    return held[0]


def on_device(
    tokens,
    doc_ids,
    routes,
    ln1_gain,
    ln1_bias,
    qkv_weight,
    qv_bias,
    out_weight,
    out_bias,
    ln2_gain,
    ln2_bias,
    centroids,
    up_weight,
    up_bias,
    down_weight,
    down_bias,
    cotangent,
):
    rows, span, width = tokens.shape
    heads = HEADS
    size = width // heads
    blocks = lax.axis_size("blk")
    own = lax.axis_index("blk")
    count = rows * span
    length = blocks * span
    halo = min(SHORT, span)
    share = -(-heads // blocks)
    pad_heads = share * blocks - heads

    gathered = lax.all_gather(
        jnp.concatenate([qkv_weight, out_weight], axis=1), "expert", axis=0, tiled=True
    )
    full_qkv = gathered[:, : 3 * width]
    full_out = gathered[:, 3 * width :]
    head_weight = (
        full_qkv.reshape(width, 3, heads, size).transpose(2, 0, 1, 3).reshape(heads, width, 3 * size)
    )
    shift_row = jnp.stack([qv_bias[0], jnp.zeros((width,), F32), qv_bias[1]])
    head_shift = (
        shift_row.reshape(3, heads, size).transpose(1, 0, 2).reshape(heads, 1, 3 * size)
    )
    long_weight = lax.dynamic_slice_in_dim(
        jnp.pad(head_weight, ((0, pad_heads), (0, 0), (0, 0))), own * share, share, 0
    )
    long_shift = lax.dynamic_slice_in_dim(
        jnp.pad(head_shift, ((0, pad_heads), (0, 0), (0, 0))), own * share, share, 0
    )

    long_at = (doc_ids[0, -1] != 0).astype(jnp.int32)

    def pick(pair, at):
        return lax.dynamic_index_in_dim(pair, at, 0, keepdims=False)

    def in_order(long_part, short_part, axis):
        first = jnp.where(long_at == 0, long_part, short_part)
        second = jnp.where(long_at == 0, short_part, long_part)
        return jnp.concatenate([first, second], axis=axis)

    long_tokens = pick(tokens, long_at)
    short_tokens = pick(tokens, 1 - long_at)
    all_tokens = lax.all_gather(long_tokens, "blk", axis=0, tiled=True)
    halo_tokens = lax.ppermute(
        short_tokens[span - halo :], "blk", [(i, i + 1) for i in range(blocks - 1)]
    )
    short_ids = jnp.concatenate(
        [jnp.full((halo,), -1, jnp.int32), pick(doc_ids, 1 - long_at)]
    )
    short_ids = lax.dynamic_slice_in_dim(short_ids, own * span, halo + span, 0)
    key_ids = short_ids[:, None]
    query_ids = short_ids[None, halo:]

    def low_norm(part):
        return layer_norm(part.astype(F32), ln1_gain, ln1_bias).astype(BF)

    long_normed = low_norm(all_tokens)
    short_normed = low_norm(jnp.concatenate([halo_tokens, short_tokens], axis=0))

    long_qkv, long_wide, long_low, long_total = call(
        functools.partial(long_forward, block=span),
        (share,),
        (long_normed, long_weight, long_shift),
        [
            whole_spec((length, width)),
            pl.BlockSpec((1, width, 3 * size), lambda h: (h, 0, 0)),
            pl.BlockSpec((1, 1, 3 * size), lambda h: (h, 0, 0)),
        ],
        (
            jax.ShapeDtypeStruct((share, length, 3 * size), BF),
            jax.ShapeDtypeStruct((share * size, length), F32),
            jax.ShapeDtypeStruct((blocks, share * size, span), BF),
            jax.ShapeDtypeStruct((share, 1, length), F32),
        ),
        (
            pl.BlockSpec((1, length, 3 * size), lambda h: (h, 0, 0)),
            pl.BlockSpec((size, length), lambda h: (h, 0)),
            pl.BlockSpec((blocks, size, span), lambda h: (0, h, 0)),
            pl.BlockSpec((1, 1, length), lambda h: (h, 0, 0)),
        ),
        [],
        2 * share * length * (width * 3 * size + length * 256),
        6 * length * width,
    )
    long_attended = lax.all_to_all(long_low, "blk", 0, 0, tiled=True).reshape(-1, span)[:width]
    short_qkv, short_wide, short_low, short_total = call(
        functools.partial(short_forward, block=halo),
        (heads,),
        (short_normed, head_weight, head_shift, key_ids, query_ids),
        [
            whole_spec((halo + span, width)),
            pl.BlockSpec((1, width, 3 * size), lambda h: (h, 0, 0)),
            pl.BlockSpec((1, 1, 3 * size), lambda h: (h, 0, 0)),
            whole_spec((halo + span, 1)),
            whole_spec((1, span)),
        ],
        (
            jax.ShapeDtypeStruct((heads, halo + span, 3 * size), BF),
            jax.ShapeDtypeStruct((width, span), F32),
            jax.ShapeDtypeStruct((width, span), BF),
            jax.ShapeDtypeStruct((heads, 1, span), F32),
        ),
        (
            pl.BlockSpec((1, halo + span, 3 * size), lambda h: (h, 0, 0)),
            pl.BlockSpec((size, span), lambda h: (h, 0)),
            pl.BlockSpec((size, span), lambda h: (h, 0)),
            pl.BlockSpec((1, 1, span), lambda h: (h, 0, 0)),
        ),
        [],
        2 * heads * (halo + span) * (width * 3 * size + 2 * halo * 256),
        8 * span * width,
    )
    attended_t = in_order(long_attended, short_low, 1)

    expert_count = centroids.shape[0]
    capacity = 2 * count // expert_count
    slots = expert_count * capacity
    route_flat = routes.reshape(count)
    onehot = route_flat[:, None] == jnp.arange(expert_count, dtype=jnp.int32)[None, :]
    ranking = jnp.cumsum(onehot.astype(jnp.int32), axis=0) - 1
    slot_of = route_flat * capacity + jnp.sum(jnp.where(onehot, ranking, 0), axis=1)
    slot_line = jnp.arange(slots, dtype=jnp.int32)
    to_slots = (slot_line[:, None] == slot_of[None, :]).astype(BF)
    from_slots = (slot_of[:, None] == slot_line[None, :]).astype(BF)

    def exchange(flat):
        sent = flat.reshape(expert_count, capacity, width)
        return lax.all_to_all(sent, "expert", 0, 0, tiled=True).reshape(slots, width)

    grad_low = cotangent.reshape(count, width)
    received_cot = exchange(dot_nn(to_slots, grad_low).astype(BF))

    token_rows = tokens.astype(F32).reshape(count, width)
    middle = (
        token_rows
        + lax.dot_general(
            attended_t, full_out, (((0,), (0,)), ((), ())), preferred_element_type=F32
        )
        + out_bias
    )
    normal_two, scale_two = norm_parts(middle)
    normed_two = normal_two * ln2_gain + ln2_bias
    received = exchange(dot_nn(to_slots, normed_two.astype(BF)).astype(BF))
    centroid_rows = jnp.dot(onehot.astype(BF), centroids, preferred_element_type=F32)
    gate = jax.nn.sigmoid(jnp.sum(normed_two * centroid_rows, axis=1))

    own_centroid = lax.dynamic_index_in_dim(
        centroids.astype(F32), lax.axis_index("expert"), 0, keepdims=True
    )
    produced, slot_grad, up_term, down_term, up_shift_term, down_shift_term = run_expert(
        received,
        received_cot,
        up_weight[0],
        down_weight[0],
        up_bias,
        down_bias,
        own_centroid,
        blocks,
    )
    back_grad = exchange(slot_grad)
    back_out = exchange(produced)
    up_sum = halving_scatter(up_term.reshape(blocks, width // blocks, -1), "blk", blocks)
    down_sum = halving_scatter(down_term, "blk", blocks).T

    grad_normed_two = dot_nn(from_slots, back_grad)
    inner_two, ln2_gain_term, ln2_bias_term = norm_back(
        grad_normed_two, normal_two, scale_two, ln2_gain
    )
    grad_out = grad_low.astype(F32)
    grad_middle = grad_out + inner_two
    out_shift_term = jnp.sum(grad_middle, axis=0)
    grad_middle_low = grad_middle.astype(BF)
    grad_attended_t = lax.dot_general(
        full_out, grad_middle_low, (((1,), (1,)), ((), ())), preferred_element_type=F32
    ).astype(BF)
    grad_pair = grad_attended_t.reshape(width, rows, span)
    long_grad = lax.dynamic_index_in_dim(grad_pair, long_at, 1, keepdims=False)
    short_grad = lax.dynamic_index_in_dim(grad_pair, 1 - long_at, 1, keepdims=False)
    long_grad = jnp.pad(long_grad, ((0, pad_heads * size), (0, 0)))
    long_grad = lax.all_to_all(
        long_grad.reshape(blocks, share * size, span), "blk", 0, 0, tiled=True
    )
    out_term = lax.dot_general(
        attended_t, grad_middle_low, (((1,), (0,)), ((), ())), preferred_element_type=F32
    )

    long_back = call(
        functools.partial(long_backward, block=span),
        (share,),
        (long_qkv, long_grad, long_wide, long_total),
        [
            pl.BlockSpec((1, length, 3 * size), lambda h: (h, 0, 0)),
            pl.BlockSpec((blocks, size, span), lambda h: (0, h, 0)),
            pl.BlockSpec((size, length), lambda h: (h, 0)),
            pl.BlockSpec((1, 1, length), lambda h: (h, 0, 0)),
        ],
        jax.ShapeDtypeStruct((blocks, 3, share * size, span), BF),
        pl.BlockSpec((blocks, 3, size, span), lambda h: (0, 0, h, 0)),
        [pltpu.VMEM((length, size), F32), pltpu.VMEM((length, size), F32)],
        5 * share * length * length * 256,
        8 * length * width,
    )
    long_back = lax.all_to_all(long_back, "blk", 0, 0, tiled=True)
    long_back = long_back.transpose(1, 0, 2, 3).reshape(3, -1, span)[:, :width]
    query_back, own_back, halo_back = call(
        functools.partial(short_backward, block=halo),
        (heads,),
        (short_qkv, short_grad, short_wide, short_total, key_ids, query_ids),
        [
            pl.BlockSpec((1, halo + span, 3 * size), lambda h: (h, 0, 0)),
            pl.BlockSpec((size, span), lambda h: (h, 0)),
            pl.BlockSpec((size, span), lambda h: (h, 0)),
            pl.BlockSpec((1, 1, span), lambda h: (h, 0, 0)),
            whole_spec((halo + span, 1)),
            whole_spec((1, span)),
        ],
        (
            jax.ShapeDtypeStruct((width, span), BF),
            jax.ShapeDtypeStruct((2, width, span), F32),
            jax.ShapeDtypeStruct((2, width, halo), BF),
        ),
        (
            pl.BlockSpec((size, span), lambda h: (h, 0)),
            pl.BlockSpec((2, size, span), lambda h: (0, h, 0)),
            pl.BlockSpec((2, size, halo), lambda h: (0, h, 0)),
        ),
        [pltpu.VMEM((halo + span, size), F32), pltpu.VMEM((halo + span, size), F32)],
        5 * heads * span * 2 * 2 * halo * 256,
        16 * span * width,
    )
    halo_back = lax.ppermute(halo_back, "blk", [(i + 1, i) for i in range(blocks - 1)])
    own_back = own_back + jnp.pad(halo_back.astype(F32), ((0, 0), (0, 0), (span - halo, 0)))
    short_back = jnp.concatenate([query_back[None], own_back.astype(BF)], axis=0)
    back_t = in_order(
        long_back.reshape(3 * width, span), short_back.reshape(3 * width, span), 1
    )

    normal_one, scale_one = norm_parts(token_rows)
    normed_low = (normal_one * ln1_gain + ln1_bias).astype(BF)
    qkv_term = lax.dot_general(
        normed_low, back_t, (((0,), (1,)), ((), ())), preferred_element_type=F32
    )
    qv_sums = jnp.sum(back_t.astype(F32), axis=1)
    grad_normed_one = lax.dot_general(
        back_t, full_qkv, (((0,), (1,)), ((), ())), preferred_element_type=F32
    )
    inner_one, ln1_gain_term, ln1_bias_term = norm_back(
        grad_normed_one, normal_one, scale_one, ln1_gain
    )
    grad_tokens = grad_middle + inner_one

    expert_rows = dot_nn(from_slots, back_out)
    result = middle + gate[:, None] * expert_rows
    grad_logit = jnp.sum(grad_out * expert_rows, axis=1) * gate * (1.0 - gate)
    centroid_term = jnp.einsum(
        "te,td->de",
        onehot.astype(F32) * grad_logit[:, None],
        normed_two,
        precision=lax.Precision.HIGHEST,
    )

    small = jnp.stack(
        [
            qv_sums[:width],
            qv_sums[2 * width :],
            out_shift_term,
            ln1_gain_term,
            ln1_bias_term,
            ln2_gain_term,
            ln2_bias_term,
        ],
        axis=1,
    )
    n_small = small.shape[1]
    packed = jnp.concatenate([qkv_term, out_term, small, centroid_term], axis=1).astype(BF)
    packed = lax.psum_scatter(packed, "expert", scatter_dimension=0, tiled=True)
    packed = lax.psum(packed, "blk").astype(F32)
    qkv_sum = packed[:, : 3 * width]
    out_sum = packed[:, 3 * width : 4 * width]
    small_sum = packed[:, 4 * width : 4 * width + n_small]
    centroid_sum = packed[:, 4 * width + n_small :].T
    shift_sum = lax.psum_scatter(
        jnp.concatenate(
            [up_shift_term.reshape(blocks, -1), down_shift_term.reshape(blocks, -1)], axis=1
        ).astype(BF),
        "blk",
        scatter_dimension=0,
        tiled=True,
    ).astype(F32)
    up_shift_sum = shift_sum[:, : up_bias.shape[1] // blocks]
    down_shift_sum = shift_sum[:, up_bias.shape[1] // blocks :]
    return (
        result.reshape(rows, span, width),
        grad_tokens.reshape(rows, span, width),
        small_sum[:, 3],
        small_sum[:, 4],
        qkv_sum,
        small_sum[:, :2].T,
        out_sum,
        small_sum[:, 2],
        small_sum[:, 5],
        small_sum[:, 6],
        centroid_sum,
        up_sum[None],
        up_shift_sum,
        down_sum[None],
        down_shift_sum,
    )


def solution(mesh):
    return jax.shard_map(
        on_device,
        mesh=mesh,
        in_specs=(
            P("expert", "blk", None),
            P("expert", None),
            P("blk", "expert", None, None),
            P(),
            P(),
            P("expert", None),
            P(),
            P("expert", None),
            P(),
            P(),
            P(),
            P(),
            P("expert", None, None),
            P("expert", None),
            P("expert", None, None),
            P("expert", None),
            P("expert", "blk", None),
        ),
        out_specs=(
            P("expert", "blk", None),
            P("expert", "blk", None),
            P("expert"),
            P("expert"),
            P("expert", None),
            P(None, "expert"),
            P("expert", None),
            P("expert"),
            P("expert"),
            P("expert"),
            P(None, "expert"),
            P("expert", "blk", None),
            P("expert", "blk"),
            P("expert", "blk", None),
            P("expert", "blk"),
        ),
        check_vma=False,
    )
```

time: 1690 us -> 897 us (0.53)
  waiting for transfers between devices: 1020 us -> 373 us
  matrix products: 273 us -> 57.9 us
  Pallas kernels: 0 us -> 177 us
  local copies, waits for them, and re-layouts: 150 us -> 87.1 us
  other arithmetic: 98 us -> 39.7 us
  starting transfers between devices: 12.5 us -> 44.8 us
  loops' own time: 27.4 us -> 0 us
    reduce_scatter x6 -> x1, waiting for transfers between devices: 630 us -> 0.01 us  [on_device(): packed = lax.psum_scatter(packed, 'expert', scatter_dimension=0, tiled=True)]
    dot_general x21 -> x11, matrix products: 273 us -> 57.9 us  [the longest x4 29.5 us: dot_nn(): lax.dot_general(a, b, (((1,), (0,)), ((), ())), preferred_element_type=F32)]
    pallas_call x0 -> x5, Pallas kernels: none -> 177 us  [call(): pl.pallas_call(kernel, grid=grid, in_specs=in_specs, out_specs=out_specs,...]
    ppermute x0 -> x6, waiting for transfers between devices: none -> 157 us  [the longest x4 130 us: halving_scatter(): came = lax.ppermute(send, axis, pairs)]
    all_gather x4 -> x2, waiting for transfers between devices: 211 us -> 91.4 us  [the longest x1 54.2 us: on_device(): all_tokens = lax.all_gather(long_tokens, 'blk', axis=0, tiled=True)]
    unnamed x15 -> x4, waiting for transfers between devices: 57.9 us -> 0.07 us
    dynamic_update_slice x12 -> x0, local copies, waits for them, and re-layouts: 35.8 us -> none  [on_device(): lax.scan(grad_step, zero_four, span_steps)]
    reduce_sum x13 -> x10, other arithmetic: 38 us -> 7.97 us  [the longest x3 3.02 us: norm_parts(): average = jnp.mean(values, axis=-1, keepdims=True)]
  transfers between devices with their start and end apart: 16 -> 15, of which waited for: 14 -> 11; matrix products, arithmetic and copies ran while one was open for 11% -> 14% of each run, Pallas kernels for 0% -> 6%
where the time goes in v1:
time: 897 us; the launch traced here: 888 us
  waiting for transfers between devices  373 us (42%)
  Pallas kernels  177 us (20%)
  blocking collectives  93 us (10%)
  local copies, waits for them, and re-layouts  87.1 us (10%)
  matrix products  57.9 us (6%)
  starting transfers between devices  44.8 us (5%)
  other arithmetic  39.7 us (4%)
  between operations  15.6 us (2%)
    pallas_call x5, Pallas kernels, call(): pl.pallas_call(kernel, grid=grid, in_specs=in_specs, out_specs=out_specs,...  177 us
    ppermute x4, waiting for transfers between devices, halving_scatter(): came = lax.ppermute(send, axis, pairs)  130 us
    all_to_all x3, waiting for transfers between devices, exchange(): lax.all_to_all(sent, 'expert', 0, 0, tiled=True).reshape(slots, width)  67.3 us
    all_gather x1, waiting for transfers between devices, on_device(): all_tokens = lax.all_gather(long_tokens, 'blk', axis=0, tiled=True)  54.2 us
    psum x1, waiting for transfers between devices, on_device(): packed = lax.psum(packed, 'blk').astype(F32)  44.1 us
    all_to_all x1, blocking collectives, exchange(): lax.all_to_all(sent, 'expert', 0, 0, tiled=True).reshape(slots, width)  42.3 us
    all_gather x1, waiting for transfers between devices, on_device(): lax.all_gather(jnp.concatenate([qkv_weight, out_weight], axis=1), 'expert...  37.2 us
    unnamed x1, blocking collectives  30 us
  transfers between devices with their start and end apart: 15, of which 11 were waited for; matrix products, arithmetic and copies ran while one was open for 14% of the time, Pallas kernels for 6%

profile of v1, /device:TPU:0, one launch (start us, length us, event | category | flops | bytes accessed | tf_op | source)
XLA Modules:
  0.0 887.7 jit_solution(11958863872768343841)
XLA Ops:
  23.9 54.2 %all-gather.6.cloned.1.call-done = bf16[1,2048,768]{2,1,0:T(8,128)(2,1)} async-done(((bf16[1,512,768]{2,1,0:T(8,128)(2,1)}), bf16[1,2048,768]{2,1,0:T(8,128)(2,1)}) %all-gather.6.cloned.1.call-update) | async-done | bytes 3145744 | tf_op jit(solution)/shard_map/all_gather | solution.py:441
  84.5 37.2 %all-gather.4.cloned.1.call-done = bf16[768,3072]{1,0:T(8,128)(2,1)} async-done(((bf16[96,3072]{1,0:T(8,128)(2,1)}), bf16[768,3072]{1,0:T(8,128)(2,1)}) %all-gather.4.cloned.1.call-update) | async-done | bytes 4718608 | tf_op jit(solution)/shard_map/all_gather | solution.py:410
  135.7 6.3 copy.97.w_ref
  144.3 20.2 %shard_map.280 = (bf16[3,2048,192]{2,1,0:T(8,128)(2,1)}, f32[192,2048]{1,0:T(8,128)}, bf16[4,192,512]{2,1,0:T(8,128)(2,1)}, f32[3,1,2048]{2,1,0:T(1,128)}) custom-call(bf16[2048,768]{1,0:T(8,128)(2,1)} %fusion.10.x_ref, bf16[3,768,192]{2,1,0:T(8,128)(2,1)} %constant_dynamic-slice_fusion.9.w_ref, f32[3,1,192]{2,1,0:T(1,128)} %constant_dynamic-slice_fusion.8.b_ref), custom_call_target="tpu_custom_call" | custom-call | flops 8254390272 | bytes 9437184 | tf_op jit(solution)/shard_map/pallas_call | solution.py:207
  169.3 6.5 fusion.18
  177.2 12.6 %all-to-all-done = bf16[4,192,512]{2,1,0:T(8,128)(2,1)S(1)} async-done(((bf16[4,192,512]{2,1,0:T(8,128)(2,1)}), bf16[4,192,512]{2,1,0:T(8,128)(2,1)S(1)}, u32[]{:S(2)}, u32[]{:S(2)}) %all-to-all-start) | async-done | bytes 786464 | tf_op jit(solution)/shard_map/all_to_all | solution.py:483
  196.4 20.5 %shard_map.281 = (bf16[12,768,192]{2,1,0:T(8,128)(2,1)}, f32[768,512]{1,0:T(8,128)}, bf16[768,512]{1,0:T(8,128)(2,1)}, f32[12,1,512]{2,1,0:T(1,128)}) custom-call(bf16[768,768]{1,0:T(8,128)(2,1)} %fusion.43.x_ref, bf16[12,768,192]{2,1,0:T(8,128)(2,1)} %copy.97.w_ref, f32[12,1,192]{2,1,0:T(1,128)} %copy-done.21, s32[768,1]{1,0:T(8,128)} %broadcast_in_dim.17.key_ids, ...), custom_call_target="tpu_custom_call" | custom-call | flops 5133828096 | bytes 3145728 | tf_op jit(solution)/shard_map/pallas_call | solution.py:207
  237.3 37.3 %all-to-all-done.1 = bf16[8,256,768]{2,1,0:T(8,128)(2,1)} async-done(((bf16[8,256,768]{2,1,0:T(8,128)(2,1)}), bf16[8,256,768]{2,1,0:T(8,128)(2,1)}, u32[]{:S(2)}, u32[]{:S(2)}) %all-to-all-start.1) | async-done | bytes 3145760 | tf_op jit(solution)/shard_map/all_to_all | solution.py:526
  274.6 96.9 %shard_map.282 = (bf16[2048,768]{1,0:T(8,128)(2,1)}, bf16[2048,768]{1,0:T(8,128)(2,1)}, bf16[768,3072]{1,0:T(8,128)(2,1)}, bf16[4,768,768]{2,1,0:T(8,128)(2,1)}, f32[1,3072]{1,0:T(1,128)}, /*index=5*/f32[1,768]{1,0:T(1,128)}) custom-call(bf16[2048,768]{1,0:T(8,128)(2,1)} %bitcast.16.x_ref, bf16[2048,768]{1,0:T(8,128)(2,1)} %bitcast.19.cot_ref, ...), custom_call_target="tpu_custom_call" | custom-call | flops 57982058496 | bytes 31457280 | tf_op jit(solution)/shard_map/pallas_call | solution.py:207
  371.5 42.3 %all_to_all.35 = bf16[8,256,768]{2,1,0:T(8,128)(2,1)} all-to-all(bf16[8,256,768]{2,1,0:T(8,128)(2,1)} %bitcast.158), channel_id=1, replica_groups=mesh['blk'=4,'expert'=8] {'expert'}, dimensions={0} | all-to-all | bytes 6291456 | tf_op jit(solution)/shard_map/all_to_all | solution.py:526
  421.4 7.8 multiply_reduce_fusion
  429.1 27.0 %all-to-all-done.3 = bf16[8,256,768]{2,1,0:T(8,128)(2,1)} async-done(((bf16[8,256,768]{2,1,0:T(8,128)(2,1)}), bf16[8,256,768]{2,1,0:T(8,128)(2,1)}, u32[]{:S(2)}, u32[]{:S(2)}) %all-to-all-start.3) | async-done | bytes 3145760 | tf_op jit(solution)/shard_map/all_to_all | solution.py:526
  456.1 9.3 %fusion.19 = (f32[1024]{0:T(1024)S(1)}, f32[1024,768]{1,0:T(8,128)}, bf16[768]{0:T(1024)(128)(2,1)S(1)}, f32[1024,768]{1,0:T(8,128)S(1)}) fusion(bf16[2,512,768]{2,1,0:T(8,128)(2,1)S(1)} %copy-done.32, f32[1024,768]{1,0:T(8,128)} %copy-done.2, f32[1024]{0:T(1024)S(1)} %add_divide_fusion, f32[1024]{0:T(1024)S(1)} %get-tuple-element.153, ...), kind=kOutput, calls=%fused_computation.29 | convolution fusion | flops 3234330880 | bytes 17334784 | tf_op jit(solution)/shard_map/dot_general | solution.py:19
  478.5 20.7 %all_to_all.36.grad_ref = bf16[4,192,512]{2,1,0:T(8,128)(2,1)} all-to-all(bf16[4,192,512]{2,1,0:T(8,128)(2,1)S(1)} %bitcast.159), channel_id=1, replica_groups=mesh['blk'=4,'expert'=8] {'blk'}, dimensions={0} | all-to-all | bytes 1572864 | tf_op jit(solution)/shard_map/all_to_all | solution.py:578
  499.2 23.9 %shard_map.283 = bf16[4,3,192,512]{3,2,1,0:T(8,128)(2,1)} custom-call(bf16[3,2048,192]{2,1,0:T(8,128)(2,1)} %get-tuple-element.36.qkv_ref, bf16[4,192,512]{2,1,0:T(8,128)(2,1)} %all_to_all.36.grad_ref, f32[192,2048]{1,0:T(8,128)} %get-tuple-element.37.wide_ref, f32[3,1,2048]{2,1,0:T(1,128)} %get-tuple-element.38.total_ref), custom_call_target="tpu_custom_call" | custom-call | flops 16106127360 | bytes 12582912 | tf_op jit(solution)/shard_map/pallas_call | solution.py:207
  529.7 15.6 %shard_map.284 = (bf16[768,512]{1,0:T(8,128)(2,1)}, f32[2,768,512]{2,1,0:T(8,128)}, bf16[2,768,256]{2,1,0:T(8,128)(2,1)}) custom-call(bf16[12,768,192]{2,1,0:T(8,128)(2,1)} %get-tuple-element.39.qkv_ref, bf16[768,512]{1,0:T(8,128)(2,1)} %bitcast.165, f32[768,512]{1,0:T(8,128)} %get-tuple-element.40.wide_ref, f32[12,1,512]{2,1,0:T(1,128)} %get-tuple-element.41.total_ref, ...), custom_call_target="tpu_custom_call" | custom-call | flops 8053063680 | bytes 6291456 | tf_op jit(solution)/shard_map/pallas_call | solution.py:207
  555.8 27.4 %collective-permute-done.1 = bf16[2,768,256]{2,1,0:T(8,128)(2,1)} collective-permute-done((bf16[2,768,256]{2,1,0:T(8,128)(2,1)}, bf16[2,768,256]{2,1,0:T(8,128)(2,1)}, u32[]{:S(2)}, u32[]{:S(2)}) %collective-permute-start.1) | collective-permute-done | bytes 786464 | tf_op jit(solution)/shard_map/ppermute | solution.py:629
  606.4 9.1 %concatenate.32 = bf16[768,3087]{1,0:T(8,128)(2,1)} concatenate(bf16[768,2304]{1,0:T(8,128)(2,1)} %convolution_convert_fusion, bf16[768,768]{1,0:T(8,128)(2,1)S(1)} %convolution_convert_fusion.2, bf16[768,1]{1,0:T(8,128)(2,1)} %stack.39, bf16[768,1]{1,0:T(8,128)(2,1)} %stack.40, bf16[768,1]{1,0:T(8,128)(2,1)S(1)} %copy-done.15, bf16[768,1]{1,0:T(8,128)(2,1)} %stack.42, ...), dimensions={1} | concatenate | bytes 9483264 | tf_op jit(solution)/shard_map/concatenate | solution.py:673
  624.8 14.2 %collective-permute-start.4 = (bf16[2,768,768]{1,2,0:T(8,128)(2,1)}, bf16[2,768,768]{1,2,0:T(8,128)(2,1)}, u32[]{:S(2)}, u32[]{:S(2)}) collective-permute-start(bf16[2,768,768]{1,2,0:T(8,128)(2,1)} %bitcast.163), channel_id=1, source_target_pairs={{0,8},{8,0},{16,24},{24,16},{1,9},{9,1},{17,25},{25,17},{2,10},{10... | collective-permute-start | bytes 7077896 | tf_op jit(solution)/shard_map/ppermute | solution.py:372
  647.0 44.4 %collective-permute-done.4 = bf16[2,768,768]{1,2,0:T(8,128)(2,1)} collective-permute-done((bf16[2,768,768]{1,2,0:T(8,128)(2,1)}, bf16[2,768,768]{1,2,0:T(8,128)(2,1)}, u32[]{:S(2)}, u32[]{:S(2)}) %collective-permute-start.4) | collective-permute-done | bytes 2359328 | tf_op jit(solution)/shard_map/ppermute | solution.py:372
  696.5 69.0 %collective-permute-done.2 = bf16[2,192,3072]{2,1,0:T(8,128)(2,1)} collective-permute-done((bf16[2,192,3072]{2,1,0:T(8,128)(2,1)}, bf16[2,192,3072]{2,1,0:T(8,128)(2,1)}, u32[]{:S(2)}, u32[]{:S(2)}) %collective-permute-start.2) | collective-permute-done | bytes 2359328 | tf_op jit(solution)/shard_map/ppermute | solution.py:372
  770.7 30.0 %all-reduce.2 = bf16[4,960]{1,0:T(4,128)(2,1)S(1)} all-reduce(bf16[4,960]{1,0:T(4,128)(2,1)S(1)} %pad_maximum_fusion.10), channel_id=4, replica_groups=mesh['blk'=4,'expert'=8] {'blk'}, use_global_device_ids=true, to_apply=%region_25.26.clone | all-reduce | flops 3840 | bytes 15360
  805.5 16.5 %collective-permute-done.3 = bf16[1,192,3072]{2,1,0:T(8,128)(2,1)} collective-permute-done((bf16[1,192,3072]{2,1,0:T(8,128)(2,1)}, bf16[1,192,3072]{2,1,0:T(8,128)(2,1)}, u32[]{:S(2)}, u32[]{:S(2)}) %collective-permute-start.3) | collective-permute-done | bytes 1179680 | tf_op jit(solution)/shard_map/ppermute | solution.py:372
  829.7 44.1 %all-reduce.5.cloned.1.call-done = bf16[96,3087]{1,0:T(8,128)(2,1)} async-done(((bf16[96,3087]{1,0:T(8,128)(2,1)}), bf16[96,3087]{1,0:T(8,128)(2,1)}) %all-reduce.5.cloned.1.call-update) | async-done | bytes 592720 | tf_op jit(solution)/shard_map/psum | solution.py:675
  (209 shorter events, 179.3 us)
Async XLA Ops:
  7.2 70.9 %all-gather.6.cloned.1.call-start = ((), (), s32[]{:S(2)}) async-start(), calls=%async_computation.11 | async-start | bytes 3932160 | tf_op jit(solution)/shard_map/all_gather | solution.py:441
  11.7 109.9 %all-gather.4.cloned.1.call-start = ((), (), s32[]{:S(2)}) async-start(), calls=%async_computation.8 | async-start | bytes 5308416 | tf_op jit(solution)/shard_map/all_gather | solution.py:410
  13.5 162.3 %collective-permute-start = (bf16[256,768]{1,0:T(8,128)(2,1)}, bf16[256,768]{1,0:T(8,128)(2,1)S(1)}, u32[]{:S(2)}, u32[]{:S(2)}) collective-permute-start(bf16[256,768]{1,0:T(8,128)(2,1)} %dynamic-slice_bitcast_fusion.2), channel_id=1, source_target_pairs={{0,8},{8,16},{16,24},{1,9},{9,17},{17,25},{2,10},{10,18},{18,26},{... | collective-permute-start | bytes 1179656 | tf_op jit(solution)/shard_map/ppermute | solution.py:442
  20.4 61.6 %copy-start.21 = (f32[12,1,192]{2,1,0:T(1,128)}, f32[12,1,192]{2,1,0:T(1,128)S(1)}, u32[]{:S(2)}) copy-start(f32[12,1,192]{2,1,0:T(1,128)S(1)} %reshape.267.b_ref) | copy-start | bytes 27652
  23.9 145.4 %copy-start.27 = (s32[1024]{0:T(1024)}, s32[1024]{0:T(1024)S(1)}, u32[]{:S(2)}) copy-start(s32[1024]{0:T(1024)S(1)} %multiply_add_fusion.5) | copy-start | bytes 12292
  23.9 58.2 %copy-start.20 = (f32[768]{0:T(1024)S(1)}, f32[768]{0:T(1024)}, u32[]{:S(2)}) copy-start(f32[768]{0:T(1024)} %param.20) | copy-start | bytes 9220
  164.5 25.3 %all-to-all-start = ((bf16[4,192,512]{2,1,0:T(8,128)(2,1)}), bf16[4,192,512]{2,1,0:T(8,128)(2,1)S(1)}, u32[]{:S(2)}, u32[]{:S(2)}) async-start(bf16[4,192,512]{2,1,0:T(8,128)(2,1)} %get-tuple-element.32), calls=%async_computation | async-start | bytes 1572864 | tf_op jit(solution)/shard_map/all_to_all | solution.py:483
  189.8 42.3 %all-to-all-start.2 = ((bf16[8,256,768]{2,1,0:T(8,128)(2,1)}), bf16[8,256,768]{2,1,0:T(8,128)(2,1)}, u32[]{:S(2)}, u32[]{:S(2)}) async-start(bf16[8,256,768]{2,1,0:T(8,128)(2,1)} %bitcast.154), calls=%async_computation.2 | async-start | bytes 6291456 | tf_op jit(solution)/shard_map/all_to_all | solution.py:526
  232.1 42.5 %all-to-all-start.1 = ((bf16[8,256,768]{2,1,0:T(8,128)(2,1)}), bf16[8,256,768]{2,1,0:T(8,128)(2,1)}, u32[]{:S(2)}, u32[]{:S(2)}) async-start(bf16[8,256,768]{2,1,0:T(8,128)(2,1)} %bitcast.156), calls=%async_computation.1 | async-start | bytes 6291456 | tf_op jit(solution)/shard_map/all_to_all | solution.py:526
  413.8 42.3 %all-to-all-start.3 = ((bf16[8,256,768]{2,1,0:T(8,128)(2,1)}), bf16[8,256,768]{2,1,0:T(8,128)(2,1)}, u32[]{:S(2)}, u32[]{:S(2)}) async-start(bf16[8,256,768]{2,1,0:T(8,128)(2,1)} %bitcast.155), calls=%async_computation.3 | async-start | bytes 6291456 | tf_op jit(solution)/shard_map/all_to_all | solution.py:526
  523.0 63.4 %all-to-all-start.6 = ((bf16[4,3,192,512]{3,2,1,0:T(8,128)(2,1)}), bf16[4,3,192,512]{3,2,1,0:T(8,128)(2,1)}, u32[]{:S(2)}, u32[]{:S(2)}) async-start(bf16[4,3,192,512]{3,2,1,0:T(8,128)(2,1)} %shard_map.283), calls=%async_computation.6 | async-start | bytes 4718592 | tf_op jit(solution)/shard_map/all_to_all | solution.py:601
  527.7 297.4 %reduce-scatter.2.cloned.1.call-start = ((), (), s32[]{:S(2)}) async-start(), calls=%async_computation.9 | async-start | bytes 5529600 | tf_op jit(solution)/shard_map/reduce_scatter | solution.py:674
  545.4 37.8 %collective-permute-start.1 = (bf16[2,768,256]{2,1,0:T(8,128)(2,1)}, bf16[2,768,256]{2,1,0:T(8,128)(2,1)}, u32[]{:S(2)}, u32[]{:S(2)}) collective-permute-start(bf16[2,768,256]{2,1,0:T(8,128)(2,1)} %get-tuple-element.44), channel_id=1, source_target_pairs={{8,0},{16,8},{24,16},{9,1},{17,9},{25,17},{10,2},{18,10},{26,18},{... | collective-permute-start | bytes 2359304 | tf_op jit(solution)/shard_map/ppermute | solution.py:629
  615.5 258.3 %all-reduce.5.cloned.1.call-start = ((), (), s32[]{:S(2)}) async-start(), calls=%async_computation.10 | async-start | bytes 1228800 | tf_op jit(solution)/shard_map/psum | solution.py:675
  624.8 66.7 %collective-permute-start.4 = (bf16[2,768,768]{1,2,0:T(8,128)(2,1)}, bf16[2,768,768]{1,2,0:T(8,128)(2,1)}, u32[]{:S(2)}, u32[]{:S(2)}) collective-permute-start(bf16[2,768,768]{1,2,0:T(8,128)(2,1)} %bitcast.163), channel_id=1, source_target_pairs={{0,8},{8,0},{16,24},{24,16},{1,9},{9,1},{17,25},{25,17},{2,10},{10... | collective-permute-start | bytes 7077896 | tf_op jit(solution)/shard_map/ppermute | solution.py:372
  642.4 123.1 %collective-permute-start.2 = (bf16[2,192,3072]{2,1,0:T(8,128)(2,1)}, bf16[2,192,3072]{2,1,0:T(8,128)(2,1)}, u32[]{:S(2)}, u32[]{:S(2)}) collective-permute-start(bf16[2,192,3072]{2,1,0:T(8,128)(2,1)} %dynamic-slice_bitcast_fusion), channel_id=1, source_target_pairs={{0,8},{8,0},{16,24},{24,16},{1,9},{9,1},{17,25},{25,17},{2,10},{10... | collective-permute-start | bytes 7077896 | tf_op jit(solution)/shard_map/ppermute | solution.py:372
  642.6 123.0 %slice-start = ((s8[4718592]{0:T(1024)(128)(4,1)}), s8[524288]{0:T(1024)(128)(4,1)S(1)}, s32[]{:S(2)}) async-start(s8[4718592]{0:T(1024)(128)(4,1)} %bitcast.150), calls=%async_computation.12 | async-start | bytes 1048576
  647.0 118.5 %slice-start.1 = ((s8[4718592]{0:T(1024)(128)(4,1)}), s8[4194304]{0:T(1024)(128)(4,1)S(1)}, s32[]{:S(2)}) async-start(s8[4718592]{0:T(1024)(128)(4,1)} %bitcast.150), calls=%async_computation.13 | async-start | bytes 8388608
  694.4 73.7 %copy-start.5 = (bf16[2,768,768]{1,2,0:T(8,128)(2,1)}, bf16[2,768,768]{1,2,0:T(8,128)(2,1)S(1)}, u32[]{:S(2)}) copy-start(bf16[2,768,768]{1,2,0:T(8,128)(2,1)S(1)} %fusion.11) | copy-start | bytes 7077892
  695.6 74.3 %copy-start.34 = (u32[32]{0:T(128)S(1)}, u32[32]{0:T(128)}, u32[]{:S(2)}) copy-start(u32[32]{0:T(128)} %constant.164) | copy-start | bytes 388
  695.6 74.9 %copy-start.23 = (f32[1,3072]{1,0:T(1,128)S(1)}, f32[1,3072]{1,0:T(1,128)}, u32[]{:S(2)}) copy-start(f32[1,3072]{1,0:T(1,128)} %get-tuple-element.46) | copy-start | bytes 36868
  695.6 75.0 %copy-start.30 = (f32[1,768]{1,0:T(1,128)S(1)}, f32[1,768]{1,0:T(1,128)}, u32[]{:S(2)}) copy-start(f32[1,768]{1,0:T(1,128)} %get-tuple-element.47) | copy-start | bytes 9220
  695.6 107.1 %collective-permute-start.5 = (bf16[1,768,768]{1,2,0:T(8,128)(2,1)}, bf16[1,768,768]{1,2,0:T(8,128)(2,1)S(1)}, u32[]{:S(2)}, u32[]{:S(2)}) collective-permute-start(bf16[1,768,768]{1,2,0:T(8,128)(2,1)} %constant_dynamic-slice_fusion), channel_id=1, source_target_pairs={{0,16},{8,24},{16,0},{24,8},{1,17},{9,25},{17,1},{25,9},{2,18},{10... | collective-permute-start | bytes 3538952 | tf_op jit(solution)/shard_map/ppermute | solution.py:372
  769.9 52.1 %collective-permute-start.3 = (bf16[1,192,3072]{2,1,0:T(8,128)(2,1)}, bf16[1,192,3072]{2,1,0:T(8,128)(2,1)}, u32[]{:S(2)}, u32[]{:S(2)}) collective-permute-start(bf16[1,192,3072]{2,1,0:T(8,128)(2,1)} %constant_dynamic-slice_fusion.3), channel_id=1, source_target_pairs={{0,16},{8,24},{16,0},{24,8},{1,17},{9,25},{17,1},{25,9},{2,18},{10... | collective-permute-start | bytes 3538952 | tf_op jit(solution)/shard_map/ppermute | solution.py:372
  (30 other events, 301.0 us)
Sparse Core Ops, SparseCore 0:
  11.9 66.2 all-gather.5
  80.6 41.0 all-gather.3
  615.6 69.2 reduce-scatter.1
  825.2 48.5 all-reduce.4

commit v2 on v1

--- a/solution.py
+++ b/solution.py
@@ -45,26 +45,66 @@
     return inner * scale, jnp.sum(upstream * normal, axis=0), jnp.sum(upstream, axis=0)
 
 
-def split_heads(qkv):
-    size = qkv.shape[1] // 3
-    scale = size ** (-0.5)
-    return (
-        (qkv[:, :size].astype(F32) * scale).astype(BF),
-        qkv[:, size : 2 * size],
-        qkv[:, 2 * size :],
-    )
-
-
 def causal(rows, columns, shift):
     row = lax.broadcasted_iota(jnp.int32, (rows, columns), 0)
     column = lax.broadcasted_iota(jnp.int32, (rows, columns), 1)
     return row <= column + shift
 
 
-def long_forward(x_ref, w_ref, b_ref, qkv_ref, wide_ref, low_ref, total_ref, *, block):
-    qkv = (dot_nn(x_ref[...], w_ref[0]) + b_ref[0]).astype(BF)
-    qkv_ref[0] = qkv
-    query, key, value = split_heads(qkv)
+def norm_low(values, gain, bias):
+    return layer_norm(values.astype(F32), gain, bias).astype(BF)
+
+
+def project(x_ref, gain_ref, bias_ref, weights, shifts, stores, size, chunk):
+    rows = x_ref.shape[0]
+    for lo in range(0, rows, chunk):
+        low = norm_low(x_ref[lo : lo + chunk], gain_ref[...], bias_ref[...])
+        for kind, (weight, shift) in enumerate(zip(weights, shifts)):
+            part = dot_nn(low, weight[...])
+            if shift is not None:
+                part = part + shift[...]
+            part = part.astype(BF)
+            for head in range(part.shape[1] // size):
+                stores[kind, head, lo : lo + chunk] = part[:, head * size : (head + 1) * size]
+
+
+def scaled(query):
+    return (query.astype(F32) * query.shape[-1] ** (-0.5)).astype(BF)
+
+
+def long_forward(
+    x_ref,
+    gain_ref,
+    bias_ref,
+    query_weight,
+    key_weight,
+    value_weight,
+    query_shift,
+    value_shift,
+    qkv_ref,
+    wide_ref,
+    low_ref,
+    total_ref,
+    *,
+    block,
+):
+    head = pl.program_id(0)
+    size = qkv_ref.shape[3]
+
+    @pl.when(head == 0)
+    def _():
+        project(
+            x_ref,
+            gain_ref,
+            bias_ref,
+            (query_weight, key_weight, value_weight),
+            (query_shift, None, value_shift),
+            qkv_ref,
+            size,
+            block,
+        )
+
+    query, key, value = scaled(qkv_ref[0, head]), qkv_ref[1, head], qkv_ref[2, head]
     value_t = value.T
     visible = causal(block, block, 0)
     for i in range(x_ref.shape[0] // block):
@@ -91,9 +131,8 @@
 def long_backward(
     qkv_ref, grad_ref, wide_ref, total_ref, out_ref, key_acc, value_acc, *, block
 ):
-    query, key, value = split_heads(qkv_ref[0])
-    size = query.shape[1]
-    scale = size ** (-0.5)
+    query, key, value = scaled(qkv_ref[0, 0]), qkv_ref[1, 0], qkv_ref[2, 0]
+    scale = query.shape[1] ** (-0.5)
     key_t = key.T
     visible = causal(block, block, 0)
     count = query.shape[0] // block
@@ -134,11 +173,38 @@
 
 
 def short_forward(
-    x_ref, w_ref, b_ref, key_ids, query_ids, qkv_ref, wide_ref, low_ref, total_ref, *, block
+    x_ref,
+    gain_ref,
+    bias_ref,
+    weight_ref,
+    shift_ref,
+    key_ids,
+    query_ids,
+    qkv_ref,
+    wide_ref,
+    low_ref,
+    total_ref,
+    *,
+    block,
 ):
-    qkv = (dot_nn(x_ref[...], w_ref[0]) + b_ref[0]).astype(BF)
-    qkv_ref[0] = qkv
-    query, key, value = split_heads(qkv)
+    head = pl.program_id(0)
+    width = x_ref.shape[1]
+
+    @pl.when(head == 0)
+    def _():
+        kinds = [slice(n * width, (n + 1) * width) for n in range(3)]
+        project(
+            x_ref,
+            gain_ref,
+            bias_ref,
+            [weight_ref.at[:, kind] for kind in kinds],
+            (shift_ref.at[0:1], None, shift_ref.at[1:2]),
+            qkv_ref,
+            qkv_ref.shape[3],
+            block,
+        )
+
+    query, key, value = scaled(qkv_ref[0, head]), qkv_ref[1, head], qkv_ref[2, head]
     value_t = value.T
     span = query_ids.shape[1]
     halo = x_ref.shape[0] - span
@@ -171,7 +237,7 @@
     *,
     block,
 ):
-    query, key, value = split_heads(qkv_ref[0])
+    query, key, value = scaled(qkv_ref[0, 0]), qkv_ref[1, 0], qkv_ref[2, 0]
     scale = query.shape[1] ** (-0.5)
     key_t = key.T
     span = query_ids.shape[1]
@@ -218,6 +284,188 @@
     )(*ins)
 
 
+MESH = pl.DeviceIdType.MESH
+
+
+def gather_kernel(
+    experts,
+    blocks,
+    qkv_ref,
+    out_ref,
+    row_ref,
+    edge_ref,
+    full_qkv,
+    full_out,
+    all_rows,
+    halo_ref,
+    shard_send,
+    shard_recv,
+    row_send,
+    row_recv,
+    edge_sem,
+    local_sem,
+):
+    me, z = lax.axis_index("expert"), lax.axis_index("blk")
+    mate = me + 1 - 2 * lax.rem(me, 2)
+    peers = [lax.rem(me + 2 * d, experts) for d in range(1, experts // 2)]
+    barrier = pltpu.get_barrier_semaphore()
+    for peer in [mate] + peers:
+        pl.semaphore_signal(barrier, inc=1, device_id={"expert": peer}, device_id_type=MESH)
+    for d in range(1, blocks):
+        pl.semaphore_signal(
+            barrier, inc=1, device_id={"blk": lax.rem(z + d, blocks)}, device_id_type=MESH
+        )
+    pl.semaphore_wait(barrier, len(peers) + blocks)
+
+    arrays = ((qkv_ref, full_qkv), (out_ref, full_out))
+
+    def shard(n, source, slot, turn, target):
+        return pltpu.make_async_remote_copy(
+            src_ref=source,
+            dst_ref=arrays[n][1].at[slot],
+            send_sem=shard_send.at[n, turn],
+            recv_sem=shard_recv.at[n, slot],
+            device_id={"expert": target},
+            device_id_type=MESH,
+        )
+
+    def row(source, slot, turn, target):
+        return pltpu.make_async_remote_copy(
+            src_ref=source,
+            dst_ref=all_rows.at[slot],
+            send_sem=row_send.at[turn],
+            recv_sem=row_recv.at[slot],
+            device_id={"blk": target},
+            device_id_type=MESH,
+        )
+
+    to_right, to_left = z + 1 < blocks, z > 0
+    right, left = lax.rem(z + 1, blocks), lax.rem(z + blocks - 1, blocks)
+    edge = pltpu.make_async_remote_copy(
+        src_ref=edge_ref,
+        dst_ref=halo_ref,
+        send_sem=edge_sem.at[0],
+        recv_sem=edge_sem.at[1],
+        device_id={"blk": right},
+        device_id_type=MESH,
+    )
+    no_edge = pltpu.make_async_copy(edge_ref, halo_ref, edge_sem.at[1])
+
+    @pl.when(to_right)
+    def _():
+        row(row_ref, z, 0, right).start()
+        edge.start()
+
+    @pl.when(to_left)
+    def _():
+        row(row_ref, z, 1, left).start()
+
+    @pl.when(jnp.logical_not(to_left))
+    def _():
+        no_edge.start()
+
+    sent = []
+    for n in range(2):
+        for turn, peer in enumerate(peers):
+            sent.append(shard(n, arrays[n][0], me, turn, peer))
+        sent.append(shard(n, arrays[n][0], me, len(peers), mate))
+    for copy in sent:
+        copy.start()
+    local = [
+        pltpu.make_async_copy(qkv_ref, full_qkv.at[me], local_sem.at[0]),
+        pltpu.make_async_copy(out_ref, full_out.at[me], local_sem.at[1]),
+        pltpu.make_async_copy(row_ref, all_rows.at[z], local_sem.at[2]),
+    ]
+    for copy in local:
+        copy.start()
+
+    def hand_on(k):
+        @pl.when(z - k >= 0)
+        def _():
+            slot = jnp.maximum(z - k, 0)
+            row(all_rows.at[slot], slot, 2 * k, right).wait_recv()
+
+            @pl.when(to_right)
+            def _():
+                row(all_rows.at[slot], slot, 2 * k, right).start()
+
+        @pl.when(z + k < blocks)
+        def _():
+            slot = jnp.minimum(z + k, blocks - 1)
+            row(all_rows.at[slot], slot, 2 * k + 1, left).wait_recv()
+
+            @pl.when(to_left)
+            def _():
+                row(all_rows.at[slot], slot, 2 * k + 1, left).start()
+
+    hand_on(1)
+    for turn, peer in enumerate(peers):
+        for n in range(2):
+            copy = shard(n, arrays[n][1].at[peer], peer, len(peers) + 1 + turn, mate)
+            copy.wait_recv()
+            copy.start()
+            sent.append(copy)
+    for k in range(2, blocks):
+        hand_on(k)
+    for turn in range(experts // 2):
+        slot = lax.rem(mate + 2 * turn, experts)
+        for n in range(2):
+            shard(n, arrays[n][1].at[slot], slot, 0, mate).wait_recv()
+    for copy in sent:
+        copy.wait_send()
+    for copy in local:
+        copy.wait()
+
+    @pl.when(to_right)
+    def _():
+        row(row_ref, z, 0, right).wait_send()
+        edge.wait_send()
+
+    @pl.when(to_left)
+    def _():
+        row(row_ref, z, 1, left).wait_send()
+        edge.wait_recv()
+
+    @pl.when(jnp.logical_not(to_left))
+    def _():
+        no_edge.wait()
+
+    for k in range(1, blocks):
+        @pl.when((z - k >= 0) & to_right)
+        def _(k=k):
+            slot = jnp.maximum(z - k, 0)
+            row(all_rows.at[slot], slot, 2 * k, right).wait_send()
+
+        @pl.when((z + k < blocks) & to_left)
+        def _(k=k):
+            slot = jnp.minimum(z + k, blocks - 1)
+            row(all_rows.at[slot], slot, 2 * k + 1, left).wait_send()
+
+
+def gather(qkv_weight, out_weight, row, edge, experts, blocks):
+    any_spec = pl.BlockSpec(memory_space=pl.ANY)
+    return pl.pallas_call(
+        functools.partial(gather_kernel, experts, blocks),
+        in_specs=[any_spec] * 4,
+        out_specs=(any_spec,) * 4,
+        out_shape=(
+            jax.ShapeDtypeStruct((experts,) + qkv_weight.shape, BF),
+            jax.ShapeDtypeStruct((experts,) + out_weight.shape, BF),
+            jax.ShapeDtypeStruct((blocks,) + row.shape, BF),
+            jax.ShapeDtypeStruct(edge.shape, BF),
+        ),
+        scratch_shapes=[
+            pltpu.SemaphoreType.DMA((2, experts)),
+            pltpu.SemaphoreType.DMA((2, experts)),
+            pltpu.SemaphoreType.DMA((2 * blocks,)),
+            pltpu.SemaphoreType.DMA((blocks,)),
+            pltpu.SemaphoreType.DMA((2,)),
+            pltpu.SemaphoreType.DMA((3,)),
+        ],
+        compiler_params=pltpu.CompilerParams(collective_id=0, has_side_effects=True),
+    )(qkv_weight, out_weight, row, edge)
+
+
 def gelu_parts(hidden):
     cdf = 0.5 * (1.0 + lax.erf(hidden * 0.7071067811865476))
     density = jnp.exp(-0.5 * hidden * hidden) * 0.3989422804014327
@@ -225,40 +473,147 @@
 
 
 def expert_kernel(
-    x_ref,
-    cot_ref,
-    up_ref,
-    down_ref,
-    up_shift_ref,
-    down_shift_ref,
-    centroid_ref,
-    out_ref,
-    grad_ref,
-    up_out,
-    down_out,
-    up_shift_out,
-    down_shift_out,
-    gate_ref,
-    low_ref,
-    xt_ref,
-    gt_ref,
-    out_acc,
-    grad_acc,
-    *,
+    experts,
+    blocks,
+    steps,
     chunk,
+    x_hbm,
+    cot_hbm,
+    *refs,
 ):
+    ups, refs = refs[:blocks], refs[blocks:]
+    downs, refs = refs[:blocks], refs[blocks:]
+    up_shifts, refs = refs[:blocks], refs[blocks:]
+    (
+        down_shift_ref,
+        centroid_ref,
+        back_grad,
+        back_out,
+        up_sum,
+        down_sum,
+        up_shift_out,
+        down_shift_out,
+        x_buf,
+        low_buf,
+        xt_ref,
+        gt_ref,
+        out_acc,
+        grad_acc,
+        gate_ref,
+        x_send,
+        x_recv,
+        back_send,
+        back_recv,
+        local_sem,
+        *refs,
+    ) = refs
+    rounds = (blocks - 1).bit_length()
+    up_held, down_held = refs[: rounds + 1], refs[rounds + 1 : 2 * rounds + 2]
+    part_send, part_recv = refs[2 * rounds + 2 :]
     step = pl.program_id(0)
-    rows = x_ref.shape[0]
+    me, z = lax.axis_index("expert"), lax.axis_index("blk")
+    capacity, width = x_buf.shape[1:]
+    rows = experts * capacity
+    lanes = 128
+
+    def x_copy(d):
+        target = lax.rem(me + d, experts)
+        return pltpu.make_async_remote_copy(
+            src_ref=x_hbm.at[target],
+            dst_ref=x_buf.at[me],
+            send_sem=x_send.at[d],
+            recv_sem=x_recv.at[d],
+            device_id={"expert": target},
+            device_id_type=MESH,
+        )
+
+    def back_copy(n, d):
+        target = lax.rem(me + d, experts)
+        return pltpu.make_async_remote_copy(
+            src_ref=(low_buf, x_buf)[n].at[target],
+            dst_ref=(back_grad, back_out)[n].at[me],
+            send_sem=back_send.at[n, d],
+            recv_sem=back_recv.at[n, d],
+            device_id={"expert": target},
+            device_id_type=MESH,
+        )
+
+    def back_local(n):
+        return pltpu.make_async_copy(
+            (low_buf, x_buf)[n].at[me], (back_grad, back_out)[n].at[me], local_sem.at[n]
+        )
+
+    def part_copies(r, p):
+        bit = 1 << r
+        mine = lax.rem(z // bit, 2)
+        partner = z + bit - 2 * bit * mine
+        copies = []
+        for k in range((blocks >> r) // 2):
+            for n, held in enumerate((up_held, down_held)):
+                copies.append(
+                    pltpu.make_async_remote_copy(
+                        src_ref=held[r].at[p, 2 * k + 1 - mine],
+                        dst_ref=held[r + 1].at[p, k],
+                        send_sem=part_send.at[r, n, p, k],
+                        recv_sem=part_recv.at[r, n, p, k],
+                        device_id={"blk": partner},
+                        device_id_type=MESH,
+                    )
+                )
+        return copies
+
+    def add_parts(r, p):
+        mine = lax.rem(z // (1 << r), 2)
+        for copy in part_copies(r, p):
+            copy.wait_recv()
+        for k in range((blocks >> r) // 2):
+            up = up_held[r][p, 2 * k + mine].astype(F32) + up_held[r + 1][p, k].astype(F32)
+            down = down_held[r][p, 2 * k + mine].astype(F32) + down_held[r + 1][p, k].astype(F32)
+            if r + 1 < rounds:
+                up_held[r + 1][p, k] = up.astype(BF)
+                down_held[r + 1][p, k] = down.astype(BF)
+            else:
+                for j in range(blocks):
+                    at = j * steps * lanes + p * lanes
+                    up_sum[:, at : at + lanes] = up[:, j * lanes : (j + 1) * lanes]
+                down_sum[p * lanes : (p + 1) * lanes, :] = down.T
+        if r + 1 < rounds:
+            for copy in part_copies(r + 1, p):
+                copy.start()
+
+    cot_copy = pltpu.make_async_copy(cot_hbm, low_buf, local_sem.at[2])
+    own_copy = pltpu.make_async_copy(x_hbm.at[me], x_buf.at[me], local_sem.at[3])
+    x_flat, low_flat = x_buf.reshape(rows, width), low_buf.reshape(rows, width)
 
     @pl.when(step == 0)
     def _():
+        barrier = pltpu.get_barrier_semaphore()
+        for d in range(1, experts):
+            pl.semaphore_signal(
+                barrier, inc=1, device_id={"expert": lax.rem(me + d, experts)}, device_id_type=MESH
+            )
+        for r in range(rounds):
+            bit = 1 << r
+            partner = z + bit - 2 * bit * lax.rem(z // bit, 2)
+            pl.semaphore_signal(barrier, inc=1, device_id={"blk": partner}, device_id_type=MESH)
+        cot_copy.start()
+        own_copy.start()
+        pl.semaphore_wait(barrier, experts - 1 + rounds)
+        for d in range(1, experts):
+            x_copy(d).start()
+        out_acc[...] = jnp.zeros_like(out_acc)
+        grad_acc[...] = jnp.zeros_like(grad_acc)
+        cot_copy.wait()
+        own_copy.wait()
+        for d in range(1, experts):
+            x_copy(d).wait_recv()
         for lo in range(0, rows, chunk):
-            x = x_ref[lo : lo + chunk]
+            x = x_flat[lo : lo + chunk]
             logit = jnp.sum(x.astype(F32) * centroid_ref[...], axis=1, keepdims=True)
             gate = 1.0 / (1.0 + jnp.exp(-logit))
             gate_ref[lo : lo + chunk] = gate
-            low = (cot_ref[lo : lo + chunk].astype(F32) * gate).astype(BF)
-            low_ref[lo : lo + chunk] = low
+            low = (low_flat[lo : lo + chunk].astype(F32) * gate).astype(BF)
+            low_flat[lo : lo + chunk] = low
             xt_ref[:, lo : lo + chunk] = x.T
             gt_ref[:, lo : lo + chunk] = low.T
             part = jnp.sum(low.astype(F32), axis=0, keepdims=True)
@@ -266,115 +621,164 @@
                 down_shift_out[...] += part
             else:
                 down_shift_out[...] = part
-        out_acc[...] = jnp.zeros_like(out_acc)
-        grad_acc[...] = jnp.zeros_like(grad_acc)
-
-    up_total = None
+
+    up = jnp.concatenate([ref[...] for ref in ups], axis=1)
+    down = jnp.concatenate([ref[...] for ref in downs], axis=0)
+    up_shift = jnp.concatenate([ref[...] for ref in up_shifts], axis=1)
+    totals = None
     for lo in range(0, rows, chunk):
-        x = x_ref[lo : lo + chunk]
-        low = low_ref[lo : lo + chunk]
-        hidden = dot_nn(x, up_ref[...]) + up_shift_ref[...]
+        x = x_flat[lo : lo + chunk]
+        low = low_flat[lo : lo + chunk]
+        hidden = dot_nn(x, up) + up_shift
         active, slope = gelu_parts(hidden)
         active = active.astype(BF)
-        grad_hidden = dot_nt(low, down_ref[...]) * slope
-        grad_low = grad_hidden.astype(BF)
-        out_acc[lo : lo + chunk] += dot_nn(active, down_ref[...])
-        grad_acc[lo : lo + chunk] += dot_nt(grad_low, up_ref[...])
-        up_part = dot_nn(xt_ref[:, lo : lo + chunk], grad_low)
-        down_part = dot_nn(gt_ref[:, lo : lo + chunk], active)
-        shift_part = jnp.sum(grad_low.astype(F32), axis=0, keepdims=True)
-        if up_total is None:
-            up_total, down_total, shift_total = up_part, down_part, shift_part
-        else:
-            up_total, down_total, shift_total = (
-                up_total + up_part,
-                down_total + down_part,
-                shift_total + shift_part,
-            )
-    up_out[...] = up_total.astype(BF)
-    down_out[0] = down_total.astype(BF)
-    up_shift_out[...] = shift_total
-
-    @pl.when(step == pl.num_programs(0) - 1)
+        grad_low = (dot_nt(low, down) * slope).astype(BF)
+        out_acc[lo : lo + chunk] += dot_nn(active, down)
+        grad_acc[lo : lo + chunk] += dot_nt(grad_low, up)
+        parts = (
+            dot_nn(xt_ref[:, lo : lo + chunk], grad_low),
+            dot_nn(gt_ref[:, lo : lo + chunk], active),
+            jnp.sum(grad_low.astype(F32), axis=0, keepdims=True),
+        )
+        totals = parts if totals is None else tuple(a + b for a, b in zip(totals, parts))
+    up_total, down_total, shift_total = totals
+    up_total = up_total.astype(BF)
+    depth = width // blocks
+    for j in range(blocks):
+        up_held[0][step, j] = up_total[j * depth : (j + 1) * depth]
+        down_held[0][step, j] = down_total[:, j * lanes : (j + 1) * lanes].astype(BF)
+        up_shift_out[j] = shift_total[:, j * lanes : (j + 1) * lanes]
+    for copy in part_copies(0, step):
+        copy.start()
+
+    tasks = sorted(
+        ((r, p) for p in range(steps) for r in range(rounds)), key=lambda task: (sum(task), task[0])
+    )
+    early = [[] for _ in range(steps)]
+    for turn, task in enumerate(tasks):
+        at = 2 * (task[1] + 1) + 2 * task[0]
+        if at < steps - 1:
+            early[at].append(task)
+    for at in range(steps):
+        if early[at]:
+
+            @pl.when(step == at)
+            def _(at=at):
+                for r, p in early[at]:
+                    add_parts(r, p)
+
+    @pl.when(step == steps - 1)
     def _():
+        for d in range(1, experts):
+            x_copy(d).wait_send()
         for lo in range(0, rows, chunk):
             gate = gate_ref[lo : lo + chunk]
             out = (out_acc[lo : lo + chunk] + down_shift_ref[...]).astype(BF)
-            out_ref[lo : lo + chunk] = out
             inner = jnp.sum(
-                cot_ref[lo : lo + chunk].astype(F32) * out.astype(F32), axis=1, keepdims=True
+                low_flat[lo : lo + chunk].astype(F32) * out.astype(F32), axis=1, keepdims=True
             )
-            logit_grad = inner * gate * (1.0 - gate)
-            grad_ref[lo : lo + chunk] = (
-                grad_acc[lo : lo + chunk] + logit_grad * centroid_ref[...]
+            x_flat[lo : lo + chunk] = out
+            low_flat[lo : lo + chunk] = (
+                grad_acc[lo : lo + chunk] + inner * (1.0 - gate) * centroid_ref[...]
             ).astype(BF)
-
-
-def run_expert(x, cot, up_weight, down_weight, up_shift, down_shift, centroid, slices):
-    rows, width = x.shape
+        back_local(0).start()
+        for d in range(1, experts):
+            back_copy(0, d).start()
+        back_local(1).start()
+        left = [task for task in tasks if all(task not in done for done in early)]
+        half = len(left) // 2
+        for r, p in left[:half]:
+            add_parts(r, p)
+        for d in range(1, experts):
+            back_copy(0, d).wait_send()
+            back_copy(1, d).start()
+        for r, p in left[half:]:
+            add_parts(r, p)
+        for n in range(2):
+            back_local(n).wait()
+            for d in range(1, experts):
+                back_copy(n, d).wait_recv()
+        for d in range(1, experts):
+            back_copy(1, d).wait_send()
+        for p in range(steps):
+            for r in range(rounds):
+                for copy in part_copies(r, p):
+                    copy.wait_send()
+
+
+def run_expert(x, cot, up_weight, down_weight, up_shift, down_shift, centroid, blocks):
+    experts, capacity, width = x.shape
+    rows = experts * capacity
     hidden = up_weight.shape[1]
-    block = hidden // 8
-    per = hidden // slices // block
+    lanes = 128
+    steps = hidden // blocks // lanes
+    rounds = (blocks - 1).bit_length()
     chunk = min(512, rows)
-    steps = hidden // block
-    return call(
-        functools.partial(expert_kernel, chunk=chunk),
-        (steps,),
-        (x, cot, up_weight, down_weight, up_shift, down_shift, centroid),
-        [
-            whole_spec((rows, width)),
-            whole_spec((rows, width)),
-            pl.BlockSpec((width, block), lambda f: (0, f)),
-            pl.BlockSpec((block, width), lambda f: (f, 0)),
-            pl.BlockSpec((1, block), lambda f: (0, f)),
-            whole_spec((1, width)),
-            whole_spec((1, width)),
-        ],
-        (
-            jax.ShapeDtypeStruct((rows, width), BF),
-            jax.ShapeDtypeStruct((rows, width), BF),
-            jax.ShapeDtypeStruct((width, hidden), BF),
-            jax.ShapeDtypeStruct((slices, width, hidden // slices), BF),
-            jax.ShapeDtypeStruct((1, hidden), F32),
+    depth = width // blocks
+    any_spec = pl.BlockSpec(memory_space=pl.ANY)
+
+    def once(shape):
+        return pl.BlockSpec(shape, lambda f: (0,) * len(shape), pipeline_mode=pl.Buffered(1))
+
+    return pl.pallas_call(
+        functools.partial(expert_kernel, experts, blocks, steps, chunk),
+        grid=(steps,),
+        in_specs=[any_spec] * 2
+        + [pl.BlockSpec((width, lanes), lambda f, j=j: (0, j * steps + f)) for j in range(blocks)]
+        + [pl.BlockSpec((lanes, width), lambda f, j=j: (j * steps + f, 0)) for j in range(blocks)]
+        + [pl.BlockSpec((1, lanes), lambda f, j=j: (0, j * steps + f)) for j in range(blocks)]
+        + [once((1, width))] * 2,
+        out_specs=(
+            any_spec,
+            any_spec,
+            once((depth, hidden)),
+            once((hidden // blocks, width)),
+            pl.BlockSpec((blocks, 1, lanes), lambda f: (0, 0, f)),
+            once((1, width)),
+        ),
+        out_shape=(
+            jax.ShapeDtypeStruct(x.shape, BF),
+            jax.ShapeDtypeStruct(x.shape, BF),
+            jax.ShapeDtypeStruct((depth, hidden), F32),
+            jax.ShapeDtypeStruct((hidden // blocks, width), F32),
+            jax.ShapeDtypeStruct((blocks, 1, hidden // blocks), F32),
             jax.ShapeDtypeStruct((1, width), F32),
         ),
-        (
-            whole_spec((rows, width)),
-            whole_spec((rows, width)),
-            pl.BlockSpec((width, block), lambda f: (0, f)),
-            pl.BlockSpec((1, width, block), lambda f: (f // per, 0, f % per)),
-            pl.BlockSpec((1, block), lambda f: (0, f)),
-            whole_spec((1, width)),
-        ),
-        [
-            pltpu.VMEM((rows, 1), F32),
-            pltpu.VMEM((rows, width), BF),
+        scratch_shapes=[
+            pltpu.VMEM(x.shape, BF),
+            pltpu.VMEM(x.shape, BF),
             pltpu.VMEM((width, rows), BF),
             pltpu.VMEM((width, rows), BF),
             pltpu.VMEM((rows, width), F32),
             pltpu.VMEM((rows, width), F32),
+            pltpu.VMEM((rows, 1), F32),
+            pltpu.SemaphoreType.DMA((experts,)),
+            pltpu.SemaphoreType.DMA((experts,)),
+            pltpu.SemaphoreType.DMA((2, experts)),
+            pltpu.SemaphoreType.DMA((2, experts)),
+            pltpu.SemaphoreType.DMA((4,)),
+        ]
+        + [pltpu.VMEM((steps, blocks >> r, depth, blocks * lanes), BF) for r in range(rounds + 1)]
+        + [pltpu.VMEM((steps, blocks >> r, width, lanes), BF) for r in range(rounds + 1)]
+        + [
+            pltpu.SemaphoreType.DMA((rounds, 2, steps, blocks // 2)),
+            pltpu.SemaphoreType.DMA((rounds, 2, steps, blocks // 2)),
         ],
-        12 * rows * width * hidden,
-        8 * width * hidden + 8 * rows * width,
-    )
-
-
-def halving_scatter(parts, axis, count):
-    me = lax.axis_index(axis)
-    bit = 1
-    held = parts
-    while bit < count:
-        pairs = [(i, i ^ bit) for i in range(count)]
-        half = held.reshape((held.shape[0] // 2, 2) + held.shape[1:])
-        mine = (me // bit) % 2
-        keep = lax.dynamic_index_in_dim(half, mine, 1, keepdims=False)
-        send = lax.dynamic_index_in_dim(half, 1 - mine, 1, keepdims=False)
-        came = lax.ppermute(send, axis, pairs)
-        held = keep.astype(F32) + came.astype(F32)
-        bit *= 2
-        if bit < count:
-            held = held.astype(BF)
-    return held[0]
+        compiler_params=pltpu.CompilerParams(
+            collective_id=1, has_side_effects=True, vmem_limit_bytes=62 << 20
+        ),
+        cost_estimate=pl.CostEstimate(
+            flops=12 * rows * width * hidden, bytes_accessed=40 << 20, transcendentals=0
+        ),
+    )(
+        x,
+        cot,
+        *([up_weight] * blocks),
+        *([down_weight] * blocks),
+        *([up_shift] * blocks),
+        down_shift,
+        centroid,
+    )
 
 
 def on_device(
@@ -407,25 +811,6 @@
     share = -(-heads // blocks)
     pad_heads = share * blocks - heads
 
-    gathered = lax.all_gather(
-        jnp.concatenate([qkv_weight, out_weight], axis=1), "expert", axis=0, tiled=True
-    )
-    full_qkv = gathered[:, : 3 * width]
-    full_out = gathered[:, 3 * width :]
-    head_weight = (
-        full_qkv.reshape(width, 3, heads, size).transpose(2, 0, 1, 3).reshape(heads, width, 3 * size)
-    )
-    shift_row = jnp.stack([qv_bias[0], jnp.zeros((width,), F32), qv_bias[1]])
-    head_shift = (
-        shift_row.reshape(3, heads, size).transpose(1, 0, 2).reshape(heads, 1, 3 * size)
-    )
-    long_weight = lax.dynamic_slice_in_dim(
-        jnp.pad(head_weight, ((0, pad_heads), (0, 0), (0, 0))), own * share, share, 0
-    )
-    long_shift = lax.dynamic_slice_in_dim(
-        jnp.pad(head_shift, ((0, pad_heads), (0, 0), (0, 0))), own * share, share, 0
-    )
-
     long_at = (doc_ids[0, -1] != 0).astype(jnp.int32)
 
     def pick(pair, at):
@@ -438,10 +823,25 @@
 
     long_tokens = pick(tokens, long_at)
     short_tokens = pick(tokens, 1 - long_at)
-    all_tokens = lax.all_gather(long_tokens, "blk", axis=0, tiled=True)
-    halo_tokens = lax.ppermute(
-        short_tokens[span - halo :], "blk", [(i, i + 1) for i in range(blocks - 1)]
-    )
+    full_qkv, full_out, all_tokens, halo_tokens = gather(
+        qkv_weight,
+        out_weight,
+        long_tokens,
+        short_tokens[span - halo :],
+        lax.axis_size("expert"),
+        blocks,
+    )
+    full_qkv = full_qkv.reshape(width, 3 * width)
+    full_out = full_out.reshape(width, width)
+    all_tokens = all_tokens.reshape(length, width)
+    ln1_rows = (ln1_gain[None], ln1_bias[None])
+
+    def own_heads(matrix):
+        padded = jnp.pad(matrix, ((0, 0), (0, pad_heads * size)))
+        return lax.dynamic_slice_in_dim(padded, own * share * size, share * size, 1)
+
+    long_weights = [own_heads(full_qkv[:, n * width : (n + 1) * width]) for n in range(3)]
+    long_shifts = [own_heads(qv_bias[n][None]) for n in range(2)]
     short_ids = jnp.concatenate(
         [jnp.full((halo,), -1, jnp.int32), pick(doc_ids, 1 - long_at)]
     )
@@ -449,29 +849,23 @@
     key_ids = short_ids[:, None]
     query_ids = short_ids[None, halo:]
 
-    def low_norm(part):
-        return layer_norm(part.astype(F32), ln1_gain, ln1_bias).astype(BF)
-
-    long_normed = low_norm(all_tokens)
-    short_normed = low_norm(jnp.concatenate([halo_tokens, short_tokens], axis=0))
-
+    part = share * size
     long_qkv, long_wide, long_low, long_total = call(
         functools.partial(long_forward, block=span),
         (share,),
-        (long_normed, long_weight, long_shift),
-        [
-            whole_spec((length, width)),
-            pl.BlockSpec((1, width, 3 * size), lambda h: (h, 0, 0)),
-            pl.BlockSpec((1, 1, 3 * size), lambda h: (h, 0, 0)),
-        ],
+        (all_tokens, *ln1_rows, *long_weights, *long_shifts),
+        [whole_spec((length, width))]
+        + [whole_spec((1, width))] * 2
+        + [whole_spec((width, part))] * 3
+        + [whole_spec((1, part))] * 2,
         (
-            jax.ShapeDtypeStruct((share, length, 3 * size), BF),
+            jax.ShapeDtypeStruct((3, share, length, size), BF),
             jax.ShapeDtypeStruct((share * size, length), F32),
             jax.ShapeDtypeStruct((blocks, share * size, span), BF),
             jax.ShapeDtypeStruct((share, 1, length), F32),
         ),
         (
-            pl.BlockSpec((1, length, 3 * size), lambda h: (h, 0, 0)),
+            whole_spec((3, share, length, size)),
             pl.BlockSpec((size, length), lambda h: (h, 0)),
             pl.BlockSpec((blocks, size, span), lambda h: (0, h, 0)),
             pl.BlockSpec((1, 1, length), lambda h: (h, 0, 0)),
@@ -484,22 +878,31 @@
     short_qkv, short_wide, short_low, short_total = call(
         functools.partial(short_forward, block=halo),
         (heads,),
-        (short_normed, head_weight, head_shift, key_ids, query_ids),
+        (
+            jnp.concatenate([halo_tokens, short_tokens], axis=0),
+            *ln1_rows,
+            full_qkv,
+            qv_bias,
+            key_ids,
+            query_ids,
+        ),
         [
             whole_spec((halo + span, width)),
-            pl.BlockSpec((1, width, 3 * size), lambda h: (h, 0, 0)),
-            pl.BlockSpec((1, 1, 3 * size), lambda h: (h, 0, 0)),
+            whole_spec((1, width)),
+            whole_spec((1, width)),
+            whole_spec((width, 3 * width)),
+            whole_spec((2, width)),
             whole_spec((halo + span, 1)),
             whole_spec((1, span)),
         ],
         (
-            jax.ShapeDtypeStruct((heads, halo + span, 3 * size), BF),
+            jax.ShapeDtypeStruct((3, heads, halo + span, size), BF),
             jax.ShapeDtypeStruct((width, span), F32),
             jax.ShapeDtypeStruct((width, span), BF),
             jax.ShapeDtypeStruct((heads, 1, span), F32),
         ),
         (
-            pl.BlockSpec((1, halo + span, 3 * size), lambda h: (h, 0, 0)),
+            whole_spec((3, heads, halo + span, size)),
             pl.BlockSpec((size, span), lambda h: (h, 0)),
             pl.BlockSpec((size, span), lambda h: (h, 0)),
             pl.BlockSpec((1, 1, span), lambda h: (h, 0, 0)),
@@ -521,12 +924,11 @@
     to_slots = (slot_line[:, None] == slot_of[None, :]).astype(BF)
     from_slots = (slot_of[:, None] == slot_line[None, :]).astype(BF)
 
-    def exchange(flat):
-        sent = flat.reshape(expert_count, capacity, width)
-        return lax.all_to_all(sent, "expert", 0, 0, tiled=True).reshape(slots, width)
+    def to_experts(flat):
+        return dot_nn(to_slots, flat).astype(BF).reshape(expert_count, capacity, width)
 
     grad_low = cotangent.reshape(count, width)
-    received_cot = exchange(dot_nn(to_slots, grad_low).astype(BF))
+    received_cot = lax.all_to_all(to_experts(grad_low), "expert", 0, 0, tiled=True)
 
     token_rows = tokens.astype(F32).reshape(count, width)
     middle = (
@@ -538,15 +940,15 @@
     )
     normal_two, scale_two = norm_parts(middle)
     normed_two = normal_two * ln2_gain + ln2_bias
-    received = exchange(dot_nn(to_slots, normed_two.astype(BF)).astype(BF))
+    outgoing = to_experts(normed_two.astype(BF))
     centroid_rows = jnp.dot(onehot.astype(BF), centroids, preferred_element_type=F32)
     gate = jax.nn.sigmoid(jnp.sum(normed_two * centroid_rows, axis=1))
 
     own_centroid = lax.dynamic_index_in_dim(
         centroids.astype(F32), lax.axis_index("expert"), 0, keepdims=True
     )
-    produced, slot_grad, up_term, down_term, up_shift_term, down_shift_term = run_expert(
-        received,
+    back_grad, back_out, up_sum, down_sum, up_shift_term, down_shift_term = run_expert(
+        outgoing,
         received_cot,
         up_weight[0],
         down_weight[0],
@@ -555,10 +957,8 @@
         own_centroid,
         blocks,
     )
-    back_grad = exchange(slot_grad)
-    back_out = exchange(produced)
-    up_sum = halving_scatter(up_term.reshape(blocks, width // blocks, -1), "blk", blocks)
-    down_sum = halving_scatter(down_term, "blk", blocks).T
+    back_grad = back_grad.reshape(slots, width)
+    back_out = back_out.reshape(slots, width)
 
     grad_normed_two = dot_nn(from_slots, back_grad)
     inner_two, ln2_gain_term, ln2_bias_term = norm_back(
@@ -587,7 +987,7 @@
         (share,),
         (long_qkv, long_grad, long_wide, long_total),
         [
-            pl.BlockSpec((1, length, 3 * size), lambda h: (h, 0, 0)),
+            pl.BlockSpec((3, 1, length, size), lambda h: (0, h, 0, 0)),
             pl.BlockSpec((blocks, size, span), lambda h: (0, h, 0)),
             pl.BlockSpec((size, length), lambda h: (h, 0)),
             pl.BlockSpec((1, 1, length), lambda h: (h, 0, 0)),
@@ -605,7 +1005,7 @@
         (heads,),
         (short_qkv, short_grad, short_wide, short_total, key_ids, query_ids),
         [
-            pl.BlockSpec((1, halo + span, 3 * size), lambda h: (h, 0, 0)),
+            pl.BlockSpec((3, 1, halo + span, size), lambda h: (0, h, 0, 0)),
             pl.BlockSpec((size, span), lambda h: (h, 0)),
             pl.BlockSpec((size, span), lambda h: (h, 0)),
             pl.BlockSpec((1, 1, span), lambda h: (h, 0, 0)),

time: 897 us -> 713 us (0.79)
  waiting for transfers between devices: 373 us -> 133 us
  Pallas kernels: 177 us -> 361 us
  blocking collectives: 93 us -> 46.9 us
  local copies, waits for them, and re-layouts: 87.1 us -> 60 us
  starting transfers between devices: 44.8 us -> 21 us
  other arithmetic: 39.7 us -> 19 us
    pallas_call x0 -> x2, Pallas kernels: none -> 282 us  [the longest x1 222 us: run_expert(): pl.pallas_call(functools.partial(expert_kernel, experts, blocks, steps, c...]
    ppermute x5 -> x0, waiting for transfers between devices: 130 us -> none  [the longest x4 130 us: halving_scatter(): came = lax.ppermute(send, axis, pairs)]
    pallas_call x5 -> x4, Pallas kernels: 177 us -> 78.5 us  [call(): pl.pallas_call(kernel, grid=grid, in_specs=in_specs, out_specs=out_specs,...]
    all_gather x2 -> x0, waiting for transfers between devices: 91.4 us -> none  [the longest x1 54.2 us: on_device(): all_tokens = lax.all_gather(long_tokens, 'blk', axis=0, tiled=True)]
    all_to_all x1 -> x0, blocking collectives: 42.3 us -> none  [exchange(): lax.all_to_all(sent, 'expert', 0, 0, tiled=True).reshape(slots, width)]
    all_to_all x3 -> x1, waiting for transfers between devices: 67.3 us -> 26.6 us  [on_device(): lax.all_to_all(to_experts(grad_low), 'expert', 0, 0, tiled=True)]
    reduce_scatter x1, waiting for transfers between devices: 0.01 us -> 40.1 us  [on_device(): packed = lax.psum_scatter(packed, 'expert', scatter_dimension=0, tiled=True)]
    ppermute x5 -> x0, starting transfers between devices: 20.2 us -> none  [the longest x4 15.3 us: halving_scatter(): came = lax.ppermute(send, axis, pairs)]
  transfers between devices with their start and end apart: 15 -> 6, of which waited for: 11 -> 4; matrix products, arithmetic and copies ran while one was open for 14% -> 6% of each run, Pallas kernels for 6% -> 5%
where the time goes in v2:
time: 713 us; the launch traced here: 705 us
  Pallas kernels  361 us (51%)
  waiting for transfers between devices  133 us (19%)
  local copies, waits for them, and re-layouts  60 us (8%)
  matrix products  49.3 us (7%)
  blocking collectives  46.9 us (7%)
  starting transfers between devices  21 us (3%)
  other arithmetic  19 us (3%)
  between operations  15.5 us (2%)
    pallas_call x1, Pallas kernels, run_expert(): pl.pallas_call(functools.partial(expert_kernel, experts, blocks, steps, c...  222 us
    pallas_call x4, Pallas kernels, call(): pl.pallas_call(kernel, grid=grid, in_specs=in_specs, out_specs=out_specs,...  78.5 us
    pallas_call x1, Pallas kernels, gather(): pl.pallas_call(functools.partial(gather_kernel, experts, blocks), in_spec...  60.2 us
    reduce_scatter x1, waiting for transfers between devices, on_device(): packed = lax.psum_scatter(packed, 'expert', scatter_dimension=0, tiled=True)  40.1 us
    psum x1, waiting for transfers between devices, on_device(): packed = lax.psum(packed, 'blk').astype(F32)  37.5 us
    ppermute x1, waiting for transfers between devices, on_device(): lax.ppermute(halo_back, 'blk', [(i + 1, i) for i in range(blocks - 1)])  28.6 us
    all_to_all x1, waiting for transfers between devices, on_device(): lax.all_to_all(to_experts(grad_low), 'expert', 0, 0, tiled=True)  26.6 us
    dot_general x4, matrix products, dot_nn(): lax.dot_general(a, b, (((1,), (0,)), ((), ())), preferred_element_type=F32)  25.3 us
  transfers between devices with their start and end apart: 6, of which 4 were waited for; matrix products, arithmetic and copies ran while one was open for 6% of the time, Pallas kernels for 5%

profile of v2, /device:TPU:0, one launch (start us, length us, event | category | flops | bytes accessed | tf_op | source)
XLA Modules:
  0.0 705.4 jit_solution(17988658914129675906)
XLA Ops:
  16.5 60.2 %shard_map.280 = (bf16[8,96,2304]{2,1,0:T(8,128)(2,1)}, bf16[8,96,768]{2,1,0:T(8,128)(2,1)}, bf16[4,512,768]{2,1,0:T(8,128)(2,1)}, bf16[256,768]{1,0:T(8,128)(2,1)}) custom-call(bf16[96,2304]{1,0:T(8,128)(2,1)} %qkv_ref.1, bf16[96,768]{1,0:T(8,128)(2,1)} %out_ref.1, bf16[512,768]{1,0:T(8,128)(2,1)} %get-tuple-element.151.row_ref, ...), custom_call_target="tpu_custom_call" | custom-call | tf_op jit(solution)/shard_map/pallas_call | solution.py:447
  83.8 19.0 %shard_map.281 = (bf16[3,3,2048,64]{3,2,1,0:T(8,128)(2,1)}, f32[192,2048]{1,0:T(8,128)}, bf16[4,192,512]{2,1,0:T(8,128)(2,1)}, f32[3,1,2048]{2,1,0:T(1,128)}) custom-call(bf16[2048,768]{1,0:T(8,128)(2,1)} %bitcast.144, f32[1,768]{1,0:T(1,128)} %broadcast_in_dim.18.gain_ref, f32[1,768]{1,0:T(1,128)} %broadcast_in_dim.19.bias_ref, ...), custom_call_target="tpu_custom_call" | custom-call | flops 8254390272 | bytes 9437184 | tf_op jit(solution)/shard_map/pallas_call | solution.py:273
  102.8 10.5 %all-to-all-start = ((bf16[4,192,512]{2,1,0:T(8,128)(2,1)}), bf16[4,192,512]{2,1,0:T(8,128)(2,1)S(1)}, u32[]{:S(2)}, u32[]{:S(2)}) async-start(bf16[4,192,512]{2,1,0:T(8,128)(2,1)} %get-tuple-element.38), calls=%async_computation | async-start | bytes 1572864 | tf_op jit(solution)/shard_map/all_to_all | solution.py:877
  119.5 19.8 %shard_map.282 = (bf16[3,12,768,64]{3,2,1,0:T(8,128)(2,1)}, f32[768,512]{1,0:T(8,128)}, bf16[768,512]{1,0:T(8,128)(2,1)}, f32[12,1,512]{2,1,0:T(1,128)}) custom-call(bf16[768,768]{1,0:T(8,128)(2,1)} %pad_maximum_fusion.5.x_ref, f32[1,768]{1,0:T(1,128)} %broadcast_in_dim.18.gain_ref, f32[1,768]{1,0:T(1,128)} %broadcast_in_dim.19.bias_ref, ...), custom_call_target="tpu_custom_call" | custom-call | flops 5133828096 | bytes 3145728 | tf_op jit(solution)/shard_map/pallas_call | solution.py:273
  139.2 5.1 fusion.9
  145.2 4.5 all-to-all-start.1
  155.1 5.9 fusion.8
  161.0 26.6 %all-to-all-done.1.cot_hbm = bf16[8,256,768]{2,1,0:T(8,128)(2,1)} async-done(((bf16[8,256,768]{2,1,0:T(8,128)(2,1)}), bf16[8,256,768]{2,1,0:T(8,128)(2,1)}, u32[]{:S(2)}, u32[]{:S(2)}) %all-to-all-start.1) | async-done | bytes 3145760 | tf_op jit(solution)/shard_map/all_to_all | solution.py:931
  187.6 222.3 %shard_map.283 = (bf16[8,256,768]{2,1,0:T(8,128)(2,1)}, bf16[8,256,768]{2,1,0:T(8,128)(2,1)}, f32[192,3072]{1,0:T(8,128)}, f32[768,768]{1,0:T(8,128)}, f32[4,1,768]{2,1,0:T(1,128)}, /*index=5*/f32[1,768]{1,0:T(1,128)}) custom-call(bf16[8,256,768]{2,1,0:T(8,128)(2,1)} %bitcast.151, bf16[8,256,768]{2,1,0:T(8,128)(2,1)} %all-to-all-done.1.cot_hbm, ...), custom_call_target="tpu_custom_call" | custom-call | flops 57982058496 | bytes 41943040 | tf_op jit(solution)/shard_map/pallas_call | solution.py:723
  409.8 7.4 %multiply_reduce_fusion = (bf16[768]{0:T(1024)(128)(2,1)S(1)}, f32[1024]{0:T(1024)S(1)}, f32[1024]{0:T(1024)S(1)}, bf16[768]{0:T(1024)(128)(2,1)S(1)}, f32[1024,768]{1,0:T(8,128)S(1)}) fusion(f32[1024]{0:T(1024)S(1)} %add_rsqrt_fusion, f32[1024,768]{1,0:T(8,128)} %copy-done.1, f32[1024]{0:T(1024)S(1)} %broadcast_multiply_fusion.5, f32[768]{0:T(1024)S(1)} %copy-done.21, ...), kind=kOutput, calls=%fused_computation.36 | convolution fusion | flops 3230396928 | bytes 9463808 | tf_op jit(solution)/shard_map/dot_general | solution.py:19
  417.3 6.9 fusion.10
  432.3 6.3 constant_dynamic-slice_fusion
  438.8 24.2 %all_to_all.20.grad_ref = bf16[4,192,512]{2,1,0:T(8,128)(2,1)} all-to-all(bf16[4,192,512]{2,1,0:T(8,128)(2,1)S(1)} %bitcast.116), channel_id=1, replica_groups=mesh['blk'=4,'expert'=8] {'blk'}, dimensions={0} | all-to-all | bytes 1572864 | tf_op jit(solution)/shard_map/all_to_all | solution.py:978
  463.0 23.9 %shard_map.284 = bf16[4,3,192,512]{3,2,1,0:T(8,128)(2,1)} custom-call(bf16[3,3,2048,64]{3,2,1,0:T(8,128)(2,1)} %get-tuple-element.44.qkv_ref, bf16[4,192,512]{2,1,0:T(8,128)(2,1)} %all_to_all.20.grad_ref, f32[192,2048]{1,0:T(8,128)} %get-tuple-element.45.wide_ref, f32[3,1,2048]{2,1,0:T(1,128)} %get-tuple-element.46.total_ref), custom_call_target="tpu_custom_call" | custom-call | flops 16106127360 | bytes 12582912 | tf_op jit(solution)/shard_map/pallas_call | solution.py:273
  486.9 4.5 all-to-all-start.3
  494.9 15.8 %shard_map.285 = (bf16[768,512]{1,0:T(8,128)(2,1)}, f32[2,768,512]{2,1,0:T(8,128)}, bf16[2,768,256]{2,1,0:T(8,128)(2,1)}) custom-call(bf16[3,12,768,64]{3,2,1,0:T(8,128)(2,1)} %get-tuple-element.47.qkv_ref, bf16[768,512]{1,0:T(8,128)(2,1)} %bitcast.121, f32[768,512]{1,0:T(8,128)} %get-tuple-element.48.wide_ref, f32[12,1,512]{2,1,0:T(1,128)} %get-tuple-element.49.total_ref, ...), custom_call_target="tpu_custom_call" | custom-call | flops 8053063680 | bytes 6291456 | tf_op jit(solution)/shard_map/pallas_call | solution.py:273
  519.7 28.6 %collective-permute-done = bf16[2,768,256]{2,1,0:T(8,128)(2,1)} collective-permute-done((bf16[2,768,256]{2,1,0:T(8,128)(2,1)}, bf16[2,768,256]{2,1,0:T(8,128)(2,1)}, u32[]{:S(2)}, u32[]{:S(2)}) %collective-permute-start) | collective-permute-done | bytes 786464 | tf_op jit(solution)/shard_map/ppermute | solution.py:1029
  557.9 7.3 %fusion.25 = (bf16[768]{0:T(1024)(128)(2,1)S(1)}, f32[1024]{0:T(1024)S(1)}, f32[1024]{0:T(1024)S(1)}, bf16[768]{0:T(1024)(128)(2,1)S(1)}, bf16[1024,768]{1,0:T(8,128)(2,1)S(1)}, /*index=5*/f32[1024,768]{1,0:T(8,128)}) fusion(bf16[2,512,768]{2,1,0:T(8,128)(2,1)S(1)} %copy-done, f32[1024]{0:T(1024)S(1)} %bitcast.131, f32[1024]{0:T(1024)S(1)} %bitcast.129, ...), kind=kOutput, calls=%fused_computation.35 | convolution fusion | flops 3643535872 | bytes 14574592 | tf_op jit(solution)/shard_map/dot_general | solution.py:1042
  565.2 5.4 convolution_convert_fusion
  572.3 9.1 %concatenate.28 = bf16[768,3087]{1,0:T(8,128)(2,1)} concatenate(bf16[768,2304]{1,0:T(8,128)(2,1)} %convolution_convert_fusion, bf16[768,768]{1,0:T(8,128)(2,1)S(1)} %convolution_convert_fusion.2, bf16[768,1]{1,0:T(8,128)(2,1)} %stack.35, bf16[768,1]{1,0:T(8,128)(2,1)} %stack.36, bf16[768,1]{1,0:T(8,128)(2,1)S(1)} %stack.37, bf16[768,1]{1,0:T(8,128)(2,1)} %stack.38, ...), dimensions={1} | concatenate | bytes 9483264 | tf_op jit(solution)/shard_map/concatenate | solution.py:1073
  582.8 22.7 %all-reduce.2 = bf16[4,960]{1,0:T(4,128)(2,1)S(1)} all-reduce(bf16[4,960]{1,0:T(4,128)(2,1)S(1)} %pad_maximum_fusion.8), channel_id=3, replica_groups=mesh['blk'=4,'expert'=8] {'blk'}, use_global_device_ids=true, to_apply=%region_21.22.clone | all-reduce | flops 3840 | bytes 15360
  607.3 40.1 %reduce-scatter.2.cloned.1.call-done = bf16[96,3087]{1,0:T(8,128)(2,1)} async-done(((bf16[768,3087]{1,0:T(8,128)(2,1)}), bf16[96,3087]{1,0:T(8,128)(2,1)}) %reduce-scatter.2.cloned.1.call-update) | async-done | bytes 592720 | tf_op jit(solution)/shard_map/reduce_scatter | solution.py:1074
  647.4 4.6 fusion.22
  652.0 37.5 %all-reduce.5.cloned.1.call-done = bf16[96,3087]{1,0:T(8,128)(2,1)} async-done(((bf16[96,3087]{1,0:T(8,128)(2,1)}), bf16[96,3087]{1,0:T(8,128)(2,1)}) %all-reduce.5.cloned.1.call-update) | async-done | bytes 592720 | tf_op jit(solution)/shard_map/psum | solution.py:1075
  (153 shorter events, 71.9 us)
Async XLA Ops:
  83.8 29.6 %copy-start.23 = (s32[2,2048]{1,0:T(2,128)S(1)}, s32[2,2048]{1,0:T(2,128)}, u32[]{:S(2)}) copy-start(s32[2,2048]{1,0:T(2,128)} %param.18) | copy-start | bytes 49156
  83.8 29.6 %copy-start.17 = (s32[1,2,512,1]{2,3,1,0:T(1,128)S(1)}, s32[1,2,512,1]{2,3,1,0:T(1,128)}, u32[]{:S(2)}) copy-start(s32[1,2,512,1]{2,3,1,0:T(1,128)} %param.19) | copy-start | bytes 12292
  83.8 32.5 %copy-start.16 = (bf16[256,768]{1,0:T(8,128)(2,1)S(1)}, bf16[256,768]{1,0:T(8,128)(2,1)}, u32[]{:S(2)}) copy-start(bf16[256,768]{1,0:T(8,128)(2,1)} %get-tuple-element.39) | copy-start | bytes 1179652
  102.8 14.6 %copy-start.25 = (bf16[8,768]{1,0:T(8,128)(2,1)S(1)}, bf16[8,768]{1,0:T(8,128)(2,1)}, u32[]{:S(2)}) copy-start(bf16[8,768]{1,0:T(8,128)(2,1)} %param.28) | copy-start | bytes 36868
  102.8 41.5 %all-to-all-start = ((bf16[4,192,512]{2,1,0:T(8,128)(2,1)}), bf16[4,192,512]{2,1,0:T(8,128)(2,1)S(1)}, u32[]{:S(2)}, u32[]{:S(2)}) async-start(bf16[4,192,512]{2,1,0:T(8,128)(2,1)} %get-tuple-element.38), calls=%async_computation | async-start | bytes 1572864 | tf_op jit(solution)/shard_map/all_to_all | solution.py:877
  119.5 19.8 %copy-start.26 = (bf16[2,512,768]{2,1,0:T(8,128)(2,1)S(1)}, bf16[2,512,768]{2,1,0:T(8,128)(2,1)}, u32[]{:S(2)}) copy-start(bf16[2,512,768]{2,1,0:T(8,128)(2,1)} %param.33) | copy-start | bytes 4718596
  144.3 5.4 copy-start.15
  145.2 42.4 %all-to-all-start.1 = ((bf16[8,256,768]{2,1,0:T(8,128)(2,1)}), bf16[8,256,768]{2,1,0:T(8,128)(2,1)}, u32[]{:S(2)}, u32[]{:S(2)}) async-start(bf16[8,256,768]{2,1,0:T(8,128)(2,1)} %bitcast.16), calls=%async_computation.1 | async-start | bytes 6291456 | tf_op jit(solution)/shard_map/all_to_all | solution.py:931
  409.8 7.5 %copy-start.2 = (f32[1024,768]{1,0:T(8,128)S(1)}, f32[1024,768]{1,0:T(8,128)}, u32[]{:S(2)}) copy-start(f32[1024,768]{1,0:T(8,128)} %copy-done.1) | copy-start | bytes 9437188
  409.8 7.5 %copy-start.27 = (bf16[2,512,768]{2,1,0:T(8,128)(2,1)S(1)}, bf16[2,512,768]{2,1,0:T(8,128)(2,1)}, u32[]{:S(2)}) copy-start(bf16[2,512,768]{2,1,0:T(8,128)(2,1)} %param.33) | copy-start | bytes 4718596
  409.8 7.5 %copy-start.31 = (bf16[8,256,768]{2,1,0:T(8,128)(2,1)S(1)}, bf16[8,256,768]{2,1,0:T(8,128)(2,1)}, u32[]{:S(2)}) copy-start(bf16[8,256,768]{2,1,0:T(8,128)(2,1)} %get-tuple-element.42) | copy-start | bytes 9437188
  417.3 8.6 %copy-start.29 = (bf16[8,96,768]{2,1,0:T(8,128)(2,1)S(1)}, bf16[8,96,768]{2,1,0:T(8,128)(2,1)}, u32[]{:S(2)}) copy-start(bf16[8,96,768]{2,1,0:T(8,128)(2,1)} %get-tuple-element.41) | copy-start | bytes 3538948
  486.9 64.6 %all-to-all-start.3 = ((bf16[4,3,192,512]{3,2,1,0:T(8,128)(2,1)}), bf16[4,3,192,512]{3,2,1,0:T(8,128)(2,1)}, u32[]{:S(2)}, u32[]{:S(2)}) async-start(bf16[4,3,192,512]{3,2,1,0:T(8,128)(2,1)} %shard_map.284), calls=%async_computation.3 | async-start | bytes 4718592 | tf_op jit(solution)/shard_map/all_to_all | solution.py:1001
  491.4 155.9 %reduce-scatter.2.cloned.1.call-start = ((), (), s32[]{:S(2)}) async-start(), calls=%async_computation.5 | async-start | bytes 5529600 | tf_op jit(solution)/shard_map/reduce_scatter | solution.py:1074
  494.9 17.3 %copy-start.3 = (f32[1024,768]{1,0:T(8,128)S(1)}, f32[1024,768]{1,0:T(8,128)}, u32[]{:S(2)}) copy-start(f32[1024,768]{1,0:T(8,128)} %copy-done.1) | copy-start | bytes 9437188
  510.7 37.6 %collective-permute-start = (bf16[2,768,256]{2,1,0:T(8,128)(2,1)}, bf16[2,768,256]{2,1,0:T(8,128)(2,1)}, u32[]{:S(2)}, u32[]{:S(2)}) collective-permute-start(bf16[2,768,256]{2,1,0:T(8,128)(2,1)} %get-tuple-element.52), channel_id=1, source_target_pairs={{8,0},{16,8},{24,16},{9,1},{17,9},{25,17},{10,2},{18,10},{26,18},{... | collective-permute-start | bytes 2359304 | tf_op jit(solution)/shard_map/ppermute | solution.py:1029
  515.8 32.5 %copy-start.8 = (f32[2,768,512]{2,1,0:T(8,128)S(1)}, f32[2,768,512]{2,1,0:T(8,128)}, u32[]{:S(2)}) copy-start(f32[2,768,512]{2,1,0:T(8,128)} %get-tuple-element.51) | copy-start | bytes 9437188
  519.7 30.2 %copy-start.12 = (bf16[768,512]{1,0:T(8,128)(2,1)S(1)}, bf16[768,512]{1,0:T(8,128)(2,1)}, u32[]{:S(2)}) copy-start(bf16[768,512]{1,0:T(8,128)(2,1)} %get-tuple-element.50) | copy-start | bytes 2359300
  553.9 4.0 copy-start.6
  553.9 4.0 copy-start.18
  553.9 4.0 copy-start.22
  581.4 108.0 %all-reduce.5.cloned.1.call-start = ((), (), s32[]{:S(2)}) async-start(), calls=%async_computation.6 | async-start | bytes 1228800 | tf_op jit(solution)/shard_map/psum | solution.py:1075
  652.0 43.5 %copy-start.11 = (f32[192,3072]{1,0:T(8,128)S(1)}, f32[192,3072]{1,0:T(8,128)}, u32[]{:S(2)}) copy-start(f32[192,3072]{1,0:T(8,128)} %get-tuple-element.53) | copy-start | bytes 7077892
  689.4 5.1 copy-start.5
  (15 other events, 23.7 us)
Sparse Core Ops, SparseCore 0:
  581.5 65.7 reduce-scatter.1
  649.8 39.5 all-reduce.4

commit v3 on v2

--- a/solution.py
+++ b/solution.py
@@ -55,77 +55,8 @@
     return layer_norm(values.astype(F32), gain, bias).astype(BF)
 
 
-def project(x_ref, gain_ref, bias_ref, weights, shifts, stores, size, chunk):
-    rows = x_ref.shape[0]
-    for lo in range(0, rows, chunk):
-        low = norm_low(x_ref[lo : lo + chunk], gain_ref[...], bias_ref[...])
-        for kind, (weight, shift) in enumerate(zip(weights, shifts)):
-            part = dot_nn(low, weight[...])
-            if shift is not None:
-                part = part + shift[...]
-            part = part.astype(BF)
-            for head in range(part.shape[1] // size):
-                stores[kind, head, lo : lo + chunk] = part[:, head * size : (head + 1) * size]
-
-
 def scaled(query):
     return (query.astype(F32) * query.shape[-1] ** (-0.5)).astype(BF)
-
-
-def long_forward(
-    x_ref,
-    gain_ref,
-    bias_ref,
-    query_weight,
-    key_weight,
-    value_weight,
-    query_shift,
-    value_shift,
-    qkv_ref,
-    wide_ref,
-    low_ref,
-    total_ref,
-    *,
-    block,
-):
-    head = pl.program_id(0)
-    size = qkv_ref.shape[3]
-
-    @pl.when(head == 0)
-    def _():
-        project(
-            x_ref,
-            gain_ref,
-            bias_ref,
-            (query_weight, key_weight, value_weight),
-            (query_shift, None, value_shift),
-            qkv_ref,
-            size,
-            block,
-        )
-
-    query, key, value = scaled(qkv_ref[0, head]), qkv_ref[1, head], qkv_ref[2, head]
-    value_t = value.T
-    visible = causal(block, block, 0)
-    for i in range(x_ref.shape[0] // block):
-        lo, hi = i * block, (i + 1) * block
-        own = query[lo:hi]
-        near = jnp.where(visible, dot_nt(key[lo:hi], own), NEGATIVE)
-        top = jnp.max(near, axis=0, keepdims=True)
-        if i:
-            far = dot_nt(key[:lo], own)
-            top = jnp.maximum(top, jnp.max(far, axis=0, keepdims=True))
-        near = jnp.exp(near - top)
-        total = jnp.sum(near, axis=0, keepdims=True)
-        out = dot_nn(value_t[:, lo:hi], near.astype(BF))
-        if i:
-            far = jnp.exp(far - top)
-            total = total + jnp.sum(far, axis=0, keepdims=True)
-            out = out + dot_nn(value_t[:, :lo], far.astype(BF))
-        out = out / total
-        wide_ref[:, lo:hi] = out
-        low_ref[i] = out.astype(BF)
-        total_ref[0, :, lo:hi] = top + jnp.log(total)
 
 
 def long_backward(
@@ -170,56 +101,6 @@
     lo = i * block
     same = key_ids[lo : lo + halo + block] == query_ids[:, lo : lo + block]
     return same & causal(halo + block, block, halo)
-
-
-def short_forward(
-    x_ref,
-    gain_ref,
-    bias_ref,
-    weight_ref,
-    shift_ref,
-    key_ids,
-    query_ids,
-    qkv_ref,
-    wide_ref,
-    low_ref,
-    total_ref,
-    *,
-    block,
-):
-    head = pl.program_id(0)
-    width = x_ref.shape[1]
-
-    @pl.when(head == 0)
-    def _():
-        kinds = [slice(n * width, (n + 1) * width) for n in range(3)]
-        project(
-            x_ref,
-            gain_ref,
-            bias_ref,
-            [weight_ref.at[:, kind] for kind in kinds],
-            (shift_ref.at[0:1], None, shift_ref.at[1:2]),
-            qkv_ref,
-            qkv_ref.shape[3],
-            block,
-        )
-
-    query, key, value = scaled(qkv_ref[0, head]), qkv_ref[1, head], qkv_ref[2, head]
-    value_t = value.T
-    span = query_ids.shape[1]
-    halo = x_ref.shape[0] - span
-    for i in range(span // block):
-        lo, hi = i * block, (i + 1) * block
-        visible = short_visible(key_ids[...], query_ids[...], i, block, halo)
-        scores = dot_nt(key[lo : hi + halo], query[lo + halo : hi + halo])
-        scores = jnp.where(visible, scores, NEGATIVE)
-        top = jnp.max(scores, axis=0, keepdims=True)
-        scores = jnp.exp(scores - top)
-        total = jnp.sum(scores, axis=0, keepdims=True)
-        out = dot_nn(value_t[:, lo : hi + halo], scores.astype(BF)) / total
-        wide_ref[:, lo:hi] = out
-        low_ref[:, lo:hi] = out.astype(BF)
-        total_ref[0, :, lo:hi] = top + jnp.log(total)
 
 
 def short_backward(
@@ -287,183 +168,439 @@
 MESH = pl.DeviceIdType.MESH
 
 
-def gather_kernel(
+def remote(source, target, send_sem, recv_sem, device):
+    return pltpu.make_async_remote_copy(
+        src_ref=source,
+        dst_ref=target,
+        send_sem=send_sem,
+        recv_sem=recv_sem,
+        device_id=device,
+        device_id_type=MESH,
+    )
+
+
+def greet(experts, blocks):
+    me, z = lax.axis_index("expert"), lax.axis_index("blk")
+    barrier = pltpu.get_barrier_semaphore()
+    for d in range(1, experts):
+        pl.semaphore_signal(
+            barrier, inc=1, device_id={"expert": lax.rem(me + d, experts)}, device_id_type=MESH
+        )
+    for d in range(1, blocks):
+        pl.semaphore_signal(
+            barrier, inc=1, device_id={"blk": lax.rem(z + d, blocks)}, device_id_type=MESH
+        )
+    pl.semaphore_wait(barrier, experts + blocks - 2)
+
+
+def front_kernel(
     experts,
     blocks,
+    heads,
+    gathers,
+    block,
+    short_block,
     qkv_ref,
     out_ref,
     row_ref,
-    edge_ref,
-    full_qkv,
-    full_out,
-    all_rows,
-    halo_ref,
-    shard_send,
-    shard_recv,
-    row_send,
-    row_recv,
-    edge_sem,
-    local_sem,
+    short_ref,
+    cot_ref,
+    gain_ref,
+    bias_ref,
+    shift_ref,
+    key_ids,
+    query_ids,
+    *refs,
 ):
+    if gathers:
+        (full_qkv, full_out), refs = refs[:2], refs[2:]
+    else:
+        full_qkv = qkv_ref
+    (
+        received_cot,
+        attended,
+        long_qkv,
+        long_wide,
+        long_total,
+        short_qkv,
+        short_wide,
+        short_low,
+        short_total,
+        weights,
+        rows_buf,
+        short_buf,
+        long_store,
+        short_store,
+        low_stage,
+        shard_send,
+        shard_recv,
+        row_send,
+        row_recv,
+        edge_sem,
+        local_sem,
+        cot_send,
+        cot_recv,
+        low_send,
+        low_recv,
+    ) = refs
     me, z = lax.axis_index("expert"), lax.axis_index("blk")
+    step = pl.program_id(0)
     mate = me + 1 - 2 * lax.rem(me, 2)
     peers = [lax.rem(me + 2 * d, experts) for d in range(1, experts // 2)]
-    barrier = pltpu.get_barrier_semaphore()
-    for peer in [mate] + peers:
-        pl.semaphore_signal(barrier, inc=1, device_id={"expert": peer}, device_id_type=MESH)
-    for d in range(1, blocks):
-        pl.semaphore_signal(
-            barrier, inc=1, device_id={"blk": lax.rem(z + d, blocks)}, device_id_type=MESH
-        )
-    pl.semaphore_wait(barrier, len(peers) + blocks)
-
-    arrays = ((qkv_ref, full_qkv), (out_ref, full_out))
-
-    def shard(n, source, slot, turn, target):
-        return pltpu.make_async_remote_copy(
-            src_ref=source,
-            dst_ref=arrays[n][1].at[slot],
-            send_sem=shard_send.at[n, turn],
-            recv_sem=shard_recv.at[n, slot],
-            device_id={"expert": target},
-            device_id_type=MESH,
-        )
-
-    def row(source, slot, turn, target):
-        return pltpu.make_async_remote_copy(
-            src_ref=source,
-            dst_ref=all_rows.at[slot],
-            send_sem=row_send.at[turn],
-            recv_sem=row_recv.at[slot],
-            device_id={"blk": target},
-            device_id_type=MESH,
+    share, size = long_store.shape[1], long_store.shape[3]
+    length = blocks * block
+    span = block
+    halo = short_buf.shape[0] - span
+    shard_rows = qkv_ref.shape[1]
+
+    def qkv_part(slot):
+        return full_qkv.at[:, pl.ds(pl.multiple_of(slot * shard_rows, shard_rows), shard_rows)]
+
+    def shard(n, own, slot, turn, target):
+        part = (qkv_part(slot), full_out.at[slot])[n]
+        source = (qkv_ref, out_ref)[n] if own else part
+        return remote(
+            source, part, shard_send.at[n, turn], shard_recv.at[n, slot], {"expert": target}
+        )
+
+    def row(slot, turn, target):
+        return remote(
+            rows_buf.at[slot],
+            rows_buf.at[slot],
+            row_send.at[turn],
+            row_recv.at[slot],
+            {"blk": target},
+        )
+
+    def own_row(turn, target):
+        return remote(
+            row_ref, rows_buf.at[z], row_send.at[turn], row_recv.at[z], {"blk": target}
         )
 
     to_right, to_left = z + 1 < blocks, z > 0
     right, left = lax.rem(z + 1, blocks), lax.rem(z + blocks - 1, blocks)
-    edge = pltpu.make_async_remote_copy(
-        src_ref=edge_ref,
-        dst_ref=halo_ref,
-        send_sem=edge_sem.at[0],
-        recv_sem=edge_sem.at[1],
-        device_id={"blk": right},
-        device_id_type=MESH,
-    )
-    no_edge = pltpu.make_async_copy(edge_ref, halo_ref, edge_sem.at[1])
-
-    @pl.when(to_right)
-    def _():
-        row(row_ref, z, 0, right).start()
-        edge.start()
-
-    @pl.when(to_left)
-    def _():
-        row(row_ref, z, 1, left).start()
-
-    @pl.when(jnp.logical_not(to_left))
-    def _():
-        no_edge.start()
-
+    last_rows = short_ref.at[pl.ds(span - halo, halo)]
+    halo_rows = short_buf.at[pl.ds(0, halo)]
+    edge = remote(last_rows, halo_rows, edge_sem.at[0], edge_sem.at[1], {"blk": right})
+    no_edge = pltpu.make_async_copy(last_rows, halo_rows, edge_sem.at[1])
+    local = [
+        pltpu.make_async_copy(row_ref, rows_buf.at[z], local_sem.at[0]),
+        pltpu.make_async_copy(short_ref, short_buf.at[pl.ds(halo, span)], local_sem.at[1]),
+    ]
+    own_cot = pltpu.make_async_copy(cot_ref.at[me], received_cot.at[me], local_sem.at[2])
+    load_weights = pltpu.make_async_copy(full_qkv, weights, local_sem.at[3])
+    own_shards = []
     sent = []
-    for n in range(2):
-        for turn, peer in enumerate(peers):
-            sent.append(shard(n, arrays[n][0], me, turn, peer))
-        sent.append(shard(n, arrays[n][0], me, len(peers), mate))
-    for copy in sent:
-        copy.start()
-    local = [
-        pltpu.make_async_copy(qkv_ref, full_qkv.at[me], local_sem.at[0]),
-        pltpu.make_async_copy(out_ref, full_out.at[me], local_sem.at[1]),
-        pltpu.make_async_copy(row_ref, all_rows.at[z], local_sem.at[2]),
-    ]
-    for copy in local:
-        copy.start()
+    handed = []
+    if gathers:
+        own_shards = [
+            pltpu.make_async_copy(qkv_ref, qkv_part(me), local_sem.at[4]),
+            pltpu.make_async_copy(out_ref, full_out.at[me], local_sem.at[5]),
+        ]
+        for n in range(2):
+            for turn, peer in enumerate(peers):
+                sent.append(shard(n, True, me, turn, peer))
+            sent.append(shard(n, True, me, len(peers), mate))
+            for turn, peer in enumerate(peers):
+                handed.append(shard(n, False, peer, len(peers) + 1 + turn, mate))
+
+    def cot_copy(d):
+        target = lax.rem(me + d, experts)
+        return remote(
+            cot_ref.at[target],
+            received_cot.at[me],
+            cot_send.at[d],
+            cot_recv.at[d],
+            {"expert": target},
+        )
+
+    def low_copy(head, d):
+        target = lax.rem(z + d, blocks)
+        return remote(
+            low_stage.at[target, head],
+            attended.at[z, head],
+            low_send.at[head, d],
+            low_recv.at[head, d],
+            {"blk": target},
+        )
+
+    def low_local(head):
+        return pltpu.make_async_copy(
+            low_stage.at[z, head], attended.at[z, head], low_send.at[head, 0]
+        )
 
     def hand_on(k):
         @pl.when(z - k >= 0)
         def _():
             slot = jnp.maximum(z - k, 0)
-            row(all_rows.at[slot], slot, 2 * k, right).wait_recv()
+            row(slot, 2 * k, right).wait_recv()
 
             @pl.when(to_right)
             def _():
-                row(all_rows.at[slot], slot, 2 * k, right).start()
+                row(slot, 2 * k, right).start()
 
         @pl.when(z + k < blocks)
         def _():
             slot = jnp.minimum(z + k, blocks - 1)
-            row(all_rows.at[slot], slot, 2 * k + 1, left).wait_recv()
+            row(slot, 2 * k + 1, left).wait_recv()
 
             @pl.when(to_left)
             def _():
-                row(all_rows.at[slot], slot, 2 * k + 1, left).start()
-
-    hand_on(1)
-    for turn, peer in enumerate(peers):
-        for n in range(2):
-            copy = shard(n, arrays[n][1].at[peer], peer, len(peers) + 1 + turn, mate)
+                row(slot, 2 * k + 1, left).start()
+
+    def project(source, lo, count, groups, store):
+        low = norm_low(source, gain_ref[...], bias_ref[...])
+        for n, group in enumerate(groups):
+            part = (dot_nn(low, weights[group]) + shift_ref[group]).astype(BF)
+            for kind in range(3):
+                for head in range(share):
+                    at = (kind * share + head) * size
+                    if n * share + head < store.shape[1]:
+                        store[kind, n * share + head, lo : lo + count] = part[:, at : at + size]
+
+    @pl.when(step == 0)
+    def _():
+        for copy in local + own_shards:
+            copy.start()
+        greet(experts, blocks)
+
+        @pl.when(to_right)
+        def _():
+            own_row(0, right).start()
+            edge.start()
+
+        @pl.when(to_left)
+        def _():
+            own_row(1, left).start()
+
+        @pl.when(jnp.logical_not(to_left))
+        def _():
+            no_edge.start()
+
+        for copy in sent:
+            copy.start()
+        hand_on(1)
+        for copy in handed:
             copy.wait_recv()
             copy.start()
-            sent.append(copy)
+        if gathers:
+            for turn in range(experts // 2):
+                for n in range(2):
+                    shard(n, False, lax.rem(mate + 2 * turn, experts), 0, mate).wait_recv()
+        for copy in own_shards:
+            copy.wait()
+        load_weights.start()
+        own_cot.start()
+        for d in range(1, experts):
+            cot_copy(d).start()
+
+        @pl.when(to_left)
+        def _():
+            edge.wait_recv()
+
+        @pl.when(jnp.logical_not(to_left))
+        def _():
+            no_edge.wait()
+
+        for copy in local:
+            copy.wait()
+        load_weights.wait()
+        for lo in range(0, halo + span, short_block):
+            project(short_buf[lo : lo + short_block], lo, short_block, range(blocks), short_store)
+
     for k in range(2, blocks):
-        hand_on(k)
-    for turn in range(experts // 2):
-        slot = lax.rem(mate + 2 * turn, experts)
-        for n in range(2):
-            shard(n, arrays[n][1].at[slot], slot, 0, mate).wait_recv()
-    for copy in sent:
-        copy.wait_send()
-    for copy in local:
-        copy.wait()
-
-    @pl.when(to_right)
+
+        @pl.when(step == (k - 1) * heads // (blocks - 1))
+        def _(k=k):
+            hand_on(k)
+
+    @pl.when(step < heads)
     def _():
-        row(row_ref, z, 0, right).wait_send()
-        edge.wait_send()
-
-    @pl.when(to_left)
+        query, key, value = (short_store[kind, step] for kind in range(3))
+        for kind, part in enumerate((query, key, value)):
+            short_qkv[kind, 0] = part
+        query = scaled(query)
+        value_t = value.T
+        for i in range(span // short_block):
+            lo, hi = i * short_block, (i + 1) * short_block
+            visible = short_visible(key_ids[...], query_ids[...], i, short_block, halo)
+            scores = dot_nt(key[lo : hi + halo], query[lo + halo : hi + halo])
+            scores = jnp.where(visible, scores, NEGATIVE)
+            top = jnp.max(scores, axis=0, keepdims=True)
+            scores = jnp.exp(scores - top)
+            total = jnp.sum(scores, axis=0, keepdims=True)
+            out = dot_nn(value_t[:, lo : hi + halo], scores.astype(BF)) / total
+            short_wide[:, lo:hi] = out
+            short_low[:, lo:hi] = out.astype(BF)
+            short_total[0, :, lo:hi] = top + jnp.log(total)
+
+    @pl.when(step == heads)
     def _():
-        row(row_ref, z, 1, left).wait_send()
-        edge.wait_recv()
-
-    @pl.when(jnp.logical_not(to_left))
+        for slot in range(blocks):
+            project(rows_buf[slot], slot * block, block, [z], long_store)
+
+    @pl.when(step >= heads)
     def _():
-        no_edge.wait()
-
-    for k in range(1, blocks):
-        @pl.when((z - k >= 0) & to_right)
-        def _(k=k):
-            slot = jnp.maximum(z - k, 0)
-            row(all_rows.at[slot], slot, 2 * k, right).wait_send()
-
-        @pl.when((z + k < blocks) & to_left)
-        def _(k=k):
-            slot = jnp.minimum(z + k, blocks - 1)
-            row(all_rows.at[slot], slot, 2 * k + 1, left).wait_send()
-
-
-def gather(qkv_weight, out_weight, row, edge, experts, blocks):
+        head = step - heads
+        query, key, value = (long_store[kind, head] for kind in range(3))
+        for kind, part in enumerate((query, key, value)):
+            long_qkv[kind, 0] = part
+        query = scaled(query)
+        value_t = value.T
+        visible = causal(block, block, 0)
+        for i in range(blocks):
+            lo, hi = i * block, (i + 1) * block
+            own = query[lo:hi]
+            near = jnp.where(visible, dot_nt(key[lo:hi], own), NEGATIVE)
+            top = jnp.max(near, axis=0, keepdims=True)
+            if i:
+                far = dot_nt(key[:lo], own)
+                top = jnp.maximum(top, jnp.max(far, axis=0, keepdims=True))
+            near = jnp.exp(near - top)
+            total = jnp.sum(near, axis=0, keepdims=True)
+            out = dot_nn(value_t[:, lo:hi], near.astype(BF))
+            if i:
+                far = jnp.exp(far - top)
+                total = total + jnp.sum(far, axis=0, keepdims=True)
+                out = out + dot_nn(value_t[:, :lo], far.astype(BF))
+            out = out / total
+            long_wide[:, lo:hi] = out
+            low_stage[i, head] = out.astype(BF)
+            long_total[0, :, lo:hi] = top + jnp.log(total)
+        low_local(head).start()
+        for d in range(1, blocks):
+            low_copy(head, d).start()
+
+    @pl.when(step == heads + share - 1)
+    def _():
+        for head in range(share):
+            low_local(head).wait()
+            for d in range(1, blocks):
+                low_copy(head, d).wait()
+        own_cot.wait()
+        for d in range(1, experts):
+            cot_copy(d).wait()
+        for copy in sent + handed:
+            copy.wait_send()
+
+        @pl.when(to_right)
+        def _():
+            own_row(0, right).wait_send()
+            edge.wait_send()
+
+        @pl.when(to_left)
+        def _():
+            own_row(1, left).wait_send()
+
+        for k in range(1, blocks):
+
+            @pl.when((z - k >= 0) & to_right)
+            def _(k=k):
+                row(jnp.maximum(z - k, 0), 2 * k, right).wait_send()
+
+            @pl.when((z + k < blocks) & to_left)
+            def _(k=k):
+                row(jnp.minimum(z + k, blocks - 1), 2 * k + 1, left).wait_send()
+
+
+def run_front(
+    qkv_shard, out_shard, row, short_row, cot, gain, bias, shifts, key_ids, query_ids, experts, blocks
+):
+    span, width = row.shape
+    size = width // HEADS
+    halo = key_ids.shape[0] - span
+    part = qkv_shard.shape[2]
+    share = part // size // 3
+    length = blocks * span
+    gathers = qkv_shard.shape[1] % 16 == 0
+    if not gathers:
+        qkv_shard = lax.all_gather(qkv_shard, "expert", axis=1, tiled=True)
+        full_out = lax.all_gather(out_shard, "expert", axis=0, tiled=True)
     any_spec = pl.BlockSpec(memory_space=pl.ANY)
-    return pl.pallas_call(
-        functools.partial(gather_kernel, experts, blocks),
-        in_specs=[any_spec] * 4,
-        out_specs=(any_spec,) * 4,
-        out_shape=(
-            jax.ShapeDtypeStruct((experts,) + qkv_weight.shape, BF),
-            jax.ShapeDtypeStruct((experts,) + out_weight.shape, BF),
-            jax.ShapeDtypeStruct((blocks,) + row.shape, BF),
-            jax.ShapeDtypeStruct(edge.shape, BF),
+    dma = pltpu.SemaphoreType.DMA
+
+    def whole(shape):
+        return pl.BlockSpec(shape, lambda f: (0,) * len(shape), pipeline_mode=pl.Buffered(1))
+
+    def short_head(*shape):
+        return pl.BlockSpec(
+            shape, lambda f: (0,) * (len(shape) - 3) + (jnp.minimum(f, HEADS - 1), 0, 0)
+        )
+
+    def long_head(*shape):
+        return pl.BlockSpec(
+            shape, lambda f: (0,) * (len(shape) - 3) + (jnp.maximum(f - HEADS, 0), 0, 0)
+        )
+
+    def flat_short(*shape):
+        return pl.BlockSpec(shape, lambda f: (jnp.minimum(f, HEADS - 1), 0))
+
+    gathered_shapes = (
+        jax.ShapeDtypeStruct((blocks, width, part), BF),
+        jax.ShapeDtypeStruct((experts,) + out_shard.shape, BF),
+    )
+    results = pl.pallas_call(
+        functools.partial(
+            front_kernel, experts, blocks, HEADS, gathers, span, min(SHORT, span)
+        ),
+        grid=(HEADS + share,),
+        in_specs=[any_spec] * 5
+        + [
+            whole((1, width)),
+            whole((1, width)),
+            whole((blocks, 1, part)),
+            whole((halo + span, 1)),
+            whole((1, span)),
+        ],
+        out_specs=((any_spec,) * 2 if gathers else ())
+        + (
+            any_spec,
+            any_spec,
+            long_head(3, 1, length, size),
+            pl.BlockSpec((size, length), lambda f: (jnp.maximum(f - HEADS, 0), 0)),
+            long_head(1, 1, length),
+            short_head(3, 1, halo + span, size),
+            flat_short(size, span),
+            flat_short(size, span),
+            short_head(1, 1, span),
+        ),
+        out_shape=(gathered_shapes if gathers else ())
+        + (
+            jax.ShapeDtypeStruct(cot.shape, BF),
+            jax.ShapeDtypeStruct((blocks, share, size, span), BF),
+            jax.ShapeDtypeStruct((3, share, length, size), BF),
+            jax.ShapeDtypeStruct((share * size, length), F32),
+            jax.ShapeDtypeStruct((share, 1, length), F32),
+            jax.ShapeDtypeStruct((3, HEADS, halo + span, size), BF),
+            jax.ShapeDtypeStruct((width, span), F32),
+            jax.ShapeDtypeStruct((width, span), BF),
+            jax.ShapeDtypeStruct((HEADS, 1, span), F32),
         ),
         scratch_shapes=[
-            pltpu.SemaphoreType.DMA((2, experts)),
-            pltpu.SemaphoreType.DMA((2, experts)),
-            pltpu.SemaphoreType.DMA((2 * blocks,)),
-            pltpu.SemaphoreType.DMA((blocks,)),
-            pltpu.SemaphoreType.DMA((2,)),
-            pltpu.SemaphoreType.DMA((3,)),
+            pltpu.VMEM((blocks, width, part), BF),
+            pltpu.VMEM((blocks, span, width), BF),
+            pltpu.VMEM((halo + span, width), BF),
+            pltpu.VMEM((3, share, length, size), BF),
+            pltpu.VMEM((3, HEADS, halo + span, size), BF),
+            pltpu.VMEM((blocks, share, size, span), BF),
+            dma((2, experts)),
+            dma((2, experts)),
+            dma((2 * blocks,)),
+            dma((blocks,)),
+            dma((2,)),
+            dma((6,)),
+            dma((experts,)),
+            dma((experts,)),
+            dma((share, blocks)),
+            dma((share, blocks)),
         ],
-        compiler_params=pltpu.CompilerParams(collective_id=0, has_side_effects=True),
-    )(qkv_weight, out_weight, row, edge)
+        compiler_params=pltpu.CompilerParams(
+            collective_id=0, has_side_effects=True, vmem_limit_bytes=56 << 20
+        ),
+    )(qkv_shard, out_shard, row, short_row, cot, gain, bias, shifts, key_ids, query_ids)
+    if gathers:
+        return results[0], results[1].reshape(-1, out_shard.shape[1]), results[2:]
+    return qkv_shard, full_out, results
 
 
 def gelu_parts(hidden):
@@ -781,6 +918,225 @@
     )
 
 
+def reduce_kernel(experts, blocks, parts, *refs):
+    arrays = 1 + max(piece[0] for part in parts for piece in part)
+    ins, refs = refs[:arrays], refs[arrays:]
+    outs, refs = refs[:arrays], refs[arrays:]
+    number = len(parts)
+    from_mate, refs = refs[:number], refs[number:]
+    pair_sum, refs = refs[:number], refs[number:]
+    from_chips, refs = refs[:number], refs[number:]
+    group_sum, refs = refs[:number], refs[number:]
+    from_line, refs = refs[:number], refs[number:]
+    whole, refs = refs[:number], refs[number:]
+    mate_send, mate_recv, chip_send, chip_recv, line_send, line_recv, back_send, back_recv = refs
+    rounds = (blocks - 1).bit_length()
+    chips = experts // 2
+    me, z = lax.axis_index("expert"), lax.axis_index("blk")
+    core = lax.rem(me, 2)
+    chip = me // 2
+    mate = me + 1 - 2 * core
+
+    def line_partner(r):
+        bit = 1 << r
+        return z + bit - 2 * bit * lax.rem(z // bit, 2)
+
+    barrier = pltpu.get_barrier_semaphore()
+    pl.semaphore_signal(barrier, inc=1, device_id={"expert": mate}, device_id_type=MESH)
+    for d in range(1, chips):
+        peer = lax.rem(me + 2 * d, experts)
+        pl.semaphore_signal(barrier, inc=1, device_id={"expert": peer}, device_id_type=MESH)
+    for r in range(rounds):
+        pl.semaphore_signal(
+            barrier, inc=1, device_id={"blk": line_partner(r)}, device_id_type=MESH
+        )
+    pl.semaphore_wait(barrier, chips + rounds)
+
+    def send(source, target, send_sem, recv_sem, device):
+        return pltpu.make_async_remote_copy(
+            src_ref=source,
+            dst_ref=target,
+            send_sem=send_sem,
+            recv_sem=recv_sem,
+            device_id=device,
+            device_id_type=MESH,
+        )
+
+    def mate_copies(p):
+        at = 0
+        copies = []
+        for n, (array, first, columns) in enumerate(parts[p]):
+            copies.append(
+                send(
+                    ins[array].at[:, 1 - core, :, pl.ds(first, columns)],
+                    from_mate[p].at[:, :, pl.ds(at, columns)],
+                    mate_send.at[p, n],
+                    mate_recv.at[p, n],
+                    {"expert": mate},
+                )
+            )
+            at += columns
+        return copies
+
+    def chip_copies(p):
+        copies = []
+        for d in range(1, chips):
+            there = lax.rem(chip + d, chips)
+            copies.append(
+                send(
+                    pair_sum[p].at[there],
+                    from_chips[p].at[d - 1],
+                    chip_send.at[p, d],
+                    chip_recv.at[p, d],
+                    {"expert": 2 * there + core},
+                )
+            )
+        return copies
+
+    def segment(p, r):
+        groups = whole[p].shape[0]
+        start = 0
+        for n in range(r):
+            start = start + lax.rem(z // (1 << n), 2) * (groups >> (n + 1))
+        return start, groups >> r
+
+    def line_copy(p, r):
+        start, groups = segment(p, r)
+        half = groups // 2
+        mine = lax.rem(z // (1 << r), 2)
+        return send(
+            group_sum[p].at[pl.ds(start + (1 - mine) * half, half)],
+            from_line[p].at[r, pl.ds(0, half)],
+            line_send.at[p, r],
+            line_recv.at[p, r],
+            {"blk": line_partner(r)},
+        )
+
+    def back_copy(p, r):
+        start, groups = segment(p, r + 1)
+        return send(
+            whole[p].at[pl.ds(start, groups)],
+            whole[p].at[pl.ds(start, groups)],
+            back_send.at[p, r],
+            back_recv.at[p, r],
+            {"blk": line_partner(r)},
+        )
+
+    def back_arrival(p, r):
+        start, groups = segment(p, r)
+        mine = lax.rem(z // (1 << r), 2)
+        start = start + (1 - mine) * (groups // 2)
+        return send(
+            whole[p].at[pl.ds(start, groups // 2)],
+            whole[p].at[pl.ds(start, groups // 2)],
+            back_send.at[p, r],
+            back_recv.at[p, r],
+            {"blk": line_partner(r)},
+        )
+
+    def run(p, stage):
+        if stage == 0:
+            for copy in mate_copies(p):
+                copy.start()
+        elif stage == 1:
+            for copy in mate_copies(p):
+                copy.wait_recv()
+            for k in range(chips):
+                at = 0
+                for array, first, columns in parts[p]:
+                    own = ins[array][k, core, :, first : first + columns]
+                    came = from_mate[p][k, :, at : at + columns]
+                    pair_sum[p][k, :, at : at + columns] = (
+                        own.astype(F32) + came.astype(F32)
+                    ).astype(BF)
+                    at += columns
+            for copy in chip_copies(p):
+                copy.start()
+        elif stage == 2:
+            for copy in chip_copies(p):
+                copy.wait_recv()
+            total = pair_sum[p][chip].astype(F32)
+            for d in range(1, chips):
+                total = total + from_chips[p][d - 1].astype(F32)
+            low = total.astype(BF)
+            used = low.shape[1] // 128
+            for g in range(group_sum[p].shape[0]):
+                if g < used:
+                    group_sum[p][g] = low[:, g * 128 : (g + 1) * 128]
+                else:
+                    group_sum[p][g] = jnp.zeros(group_sum[p].shape[1:], BF)
+            line_copy(p, 0).start()
+        elif stage < 2 + rounds:
+            add_line(p, stage - 3)
+            line_copy(p, stage - 2).start()
+        elif stage == 2 + rounds:
+            r = rounds - 1
+            add_line(p, r)
+            start, groups = segment(p, rounds)
+            whole[p][pl.ds(start, groups)] = group_sum[p][pl.ds(start, groups)]
+            back_copy(p, r).start()
+        else:
+            r = rounds - 1 - (stage - 3 - rounds)
+            back_arrival(p, r).wait_recv()
+            if r:
+                back_copy(p, r - 1).start()
+            else:
+                at = 0
+                for array, first, columns in parts[p]:
+                    for c in range(0, columns, 128):
+                        outs[array][:, first + c : first + c + 128] = whole[p][
+                            (at + c) // 128
+                        ].astype(F32)
+                    at += columns
+
+    def add_line(p, r):
+        line_copy(p, r).wait_recv()
+        start, groups = segment(p, r + 1)
+        held = group_sum[p][pl.ds(start, groups)].astype(F32)
+        group_sum[p][pl.ds(start, groups)] = (
+            held + from_line[p][r, pl.ds(0, groups)].astype(F32)
+        ).astype(BF)
+
+    stages = 3 + 2 * rounds
+    for turn in range(number + stages - 1):
+        for p in range(number):
+            if 0 <= turn - p < stages:
+                run(p, turn - p)
+    for p in range(number):
+        for copy in mate_copies(p) + chip_copies(p):
+            copy.wait_send()
+        for r in range(rounds):
+            line_copy(p, r).wait_send()
+            back_copy(p, r).wait_send()
+
+
+def reduce_all(arrays, parts, experts, blocks):
+    rows = arrays[0].shape[0] // experts
+    chips = experts // 2
+    rounds = (blocks - 1).bit_length()
+    number = len(parts)
+    widths = [sum(piece[2] for piece in part) for part in parts]
+    groups = [-(-width // 128 // blocks) * blocks for width in widths]
+    dma = pltpu.SemaphoreType.DMA
+    return pl.pallas_call(
+        functools.partial(reduce_kernel, experts, blocks, parts),
+        in_specs=[pl.BlockSpec(memory_space=pltpu.VMEM)] * len(arrays),
+        out_specs=tuple(pl.BlockSpec(memory_space=pltpu.VMEM) for _ in arrays),
+        out_shape=tuple(jax.ShapeDtypeStruct((rows, a.shape[1]), F32) for a in arrays),
+        scratch_shapes=[pltpu.VMEM((chips, rows, w), BF) for w in widths]
+        + [pltpu.VMEM((chips, rows, w), BF) for w in widths]
+        + [pltpu.VMEM((chips - 1, rows, w), BF) for w in widths]
+        + [pltpu.VMEM((g, rows, 128), BF) for g in groups]
+        + [pltpu.VMEM((rounds, g // 2, rows, 128), BF) for g in groups]
+        + [pltpu.VMEM((g, rows, 128), BF) for g in groups]
+        + [dma((number, 3)), dma((number, 3)), dma((number, chips)), dma((number, chips))]
+        + [dma((number, rounds))] * 4,
+        compiler_params=pltpu.CompilerParams(
+            collective_id=2, has_side_effects=True, vmem_limit_bytes=40 << 20
+        ),
+    )(*[a.reshape(chips, 2, rows, a.shape[1]) for a in arrays])
+
+
 def on_device(
     tokens,
     doc_ids,
@@ -811,109 +1167,19 @@
     share = -(-heads // blocks)
     pad_heads = share * blocks - heads
 
+    expert_count = centroids.shape[0]
+
     long_at = (doc_ids[0, -1] != 0).astype(jnp.int32)
 
-    def pick(pair, at):
-        return lax.dynamic_index_in_dim(pair, at, 0, keepdims=False)
-
-    def in_order(long_part, short_part, axis):
-        first = jnp.where(long_at == 0, long_part, short_part)
-        second = jnp.where(long_at == 0, short_part, long_part)
-        return jnp.concatenate([first, second], axis=axis)
-
-    long_tokens = pick(tokens, long_at)
-    short_tokens = pick(tokens, 1 - long_at)
-    full_qkv, full_out, all_tokens, halo_tokens = gather(
-        qkv_weight,
-        out_weight,
-        long_tokens,
-        short_tokens[span - halo :],
-        lax.axis_size("expert"),
-        blocks,
-    )
-    full_qkv = full_qkv.reshape(width, 3 * width)
-    full_out = full_out.reshape(width, width)
-    all_tokens = all_tokens.reshape(length, width)
-    ln1_rows = (ln1_gain[None], ln1_bias[None])
-
-    def own_heads(matrix):
-        padded = jnp.pad(matrix, ((0, 0), (0, pad_heads * size)))
-        return lax.dynamic_slice_in_dim(padded, own * share * size, share * size, 1)
-
-    long_weights = [own_heads(full_qkv[:, n * width : (n + 1) * width]) for n in range(3)]
-    long_shifts = [own_heads(qv_bias[n][None]) for n in range(2)]
-    short_ids = jnp.concatenate(
-        [jnp.full((halo,), -1, jnp.int32), pick(doc_ids, 1 - long_at)]
-    )
-    short_ids = lax.dynamic_slice_in_dim(short_ids, own * span, halo + span, 0)
-    key_ids = short_ids[:, None]
-    query_ids = short_ids[None, halo:]
-
-    part = share * size
-    long_qkv, long_wide, long_low, long_total = call(
-        functools.partial(long_forward, block=span),
-        (share,),
-        (all_tokens, *ln1_rows, *long_weights, *long_shifts),
-        [whole_spec((length, width))]
-        + [whole_spec((1, width))] * 2
-        + [whole_spec((width, part))] * 3
-        + [whole_spec((1, part))] * 2,
-        (
-            jax.ShapeDtypeStruct((3, share, length, size), BF),
-            jax.ShapeDtypeStruct((share * size, length), F32),
-            jax.ShapeDtypeStruct((blocks, share * size, span), BF),
-            jax.ShapeDtypeStruct((share, 1, length), F32),
-        ),
-        (
-            whole_spec((3, share, length, size)),
-            pl.BlockSpec((size, length), lambda h: (h, 0)),
-            pl.BlockSpec((blocks, size, span), lambda h: (0, h, 0)),
-            pl.BlockSpec((1, 1, length), lambda h: (h, 0, 0)),
-        ),
-        [],
-        2 * share * length * (width * 3 * size + length * 256),
-        6 * length * width,
-    )
-    long_attended = lax.all_to_all(long_low, "blk", 0, 0, tiled=True).reshape(-1, span)[:width]
-    short_qkv, short_wide, short_low, short_total = call(
-        functools.partial(short_forward, block=halo),
-        (heads,),
-        (
-            jnp.concatenate([halo_tokens, short_tokens], axis=0),
-            *ln1_rows,
-            full_qkv,
-            qv_bias,
-            key_ids,
-            query_ids,
-        ),
-        [
-            whole_spec((halo + span, width)),
-            whole_spec((1, width)),
-            whole_spec((1, width)),
-            whole_spec((width, 3 * width)),
-            whole_spec((2, width)),
-            whole_spec((halo + span, 1)),
-            whole_spec((1, span)),
-        ],
-        (
-            jax.ShapeDtypeStruct((3, heads, halo + span, size), BF),
-            jax.ShapeDtypeStruct((width, span), F32),
-            jax.ShapeDtypeStruct((width, span), BF),
-            jax.ShapeDtypeStruct((heads, 1, span), F32),
-        ),
-        (
-            whole_spec((3, heads, halo + span, size)),
-            pl.BlockSpec((size, span), lambda h: (h, 0)),
-            pl.BlockSpec((size, span), lambda h: (h, 0)),
-            pl.BlockSpec((1, 1, span), lambda h: (h, 0, 0)),
-        ),
-        [],
-        2 * heads * (halo + span) * (width * 3 * size + 2 * halo * 256),
-        8 * span * width,
-    )
-    attended_t = in_order(long_attended, short_low, 1)
-
-    expert_count = centroids.shape[0]
+    def ordered(pair):
+        first = lax.dynamic_index_in_dim(pair, long_at, 0, keepdims=False)
+        second = lax.dynamic_index_in_dim(pair, 1 - long_at, 0, keepdims=False)
+        return jnp.stack([first, second])
+
+    long_tokens = lax.dynamic_index_in_dim(tokens, long_at, 0, keepdims=False)
+    short_tokens = lax.dynamic_index_in_dim(tokens, 1 - long_at, 0, keepdims=False)
+    token_rows = jnp.concatenate([long_tokens, short_tokens]).astype(F32)
+
     capacity = 2 * count // expert_count
     slots = expert_count * capacity
     route_flat = routes.reshape(count)
@@ -921,16 +1187,68 @@
     ranking = jnp.cumsum(onehot.astype(jnp.int32), axis=0) - 1
     slot_of = route_flat * capacity + jnp.sum(jnp.where(onehot, ranking, 0), axis=1)
     slot_line = jnp.arange(slots, dtype=jnp.int32)
-    to_slots = (slot_line[:, None] == slot_of[None, :]).astype(BF)
+
+    def to_experts(flat, slot_of):
+        to_slots = (slot_line[:, None] == slot_of[None, :]).astype(BF)
+        return dot_nn(to_slots, flat).astype(BF).reshape(expert_count, capacity, width)
+
+    sent_cot = to_experts(cotangent.reshape(count, width), slot_of)
+    slot_of = ordered(slot_of.reshape(rows, span)).reshape(count)
+    route_flat = ordered(routes.reshape(rows, span)).reshape(count)
+    onehot = route_flat[:, None] == jnp.arange(expert_count, dtype=jnp.int32)[None, :]
     from_slots = (slot_of[:, None] == slot_line[None, :]).astype(BF)
-
-    def to_experts(flat):
-        return dot_nn(to_slots, flat).astype(BF).reshape(expert_count, capacity, width)
-
-    grad_low = cotangent.reshape(count, width)
-    received_cot = lax.all_to_all(to_experts(grad_low), "expert", 0, 0, tiled=True)
-
-    token_rows = tokens.astype(F32).reshape(count, width)
+    grad_low = ordered(cotangent).reshape(count, width)
+
+    def grouped(matrix):
+        lead = matrix.shape[0]
+        split = matrix.reshape(lead, 3, heads, size)
+        split = jnp.pad(split, ((0, 0), (0, 0), (0, pad_heads), (0, 0)))
+        split = split.reshape(lead, 3, blocks, share, size).transpose(2, 0, 1, 3, 4)
+        return split.reshape(blocks, lead, 3 * share * size)
+
+    def ungrouped(matrix):
+        lead = matrix.shape[0]
+        split = matrix.reshape(lead, blocks, 3, share, size).transpose(0, 2, 1, 3, 4)
+        return split.reshape(lead, 3, blocks * share, size)[:, :, :heads].reshape(lead, 3, width)
+
+    short_ids = jnp.concatenate(
+        [
+            jnp.full((halo,), -1, jnp.int32),
+            lax.dynamic_index_in_dim(doc_ids, 1 - long_at, 0, keepdims=False),
+        ]
+    )
+    short_ids = lax.dynamic_slice_in_dim(short_ids, own * span, halo + span, 0)
+    key_ids = short_ids[:, None]
+    query_ids = short_ids[None, halo:]
+    shifts = jnp.concatenate([qv_bias[0], jnp.zeros((width,), F32), qv_bias[1]])
+    full_qkv, full_out, rest = run_front(
+        grouped(qkv_weight),
+        out_weight,
+        long_tokens,
+        short_tokens,
+        sent_cot,
+        ln1_gain[None],
+        ln1_bias[None],
+        grouped(shifts[None]),
+        key_ids,
+        query_ids,
+        expert_count,
+        blocks,
+    )
+    (
+        received_cot,
+        long_attended,
+        long_qkv,
+        long_wide,
+        long_total,
+        short_qkv,
+        short_wide,
+        short_low,
+        short_total,
+    ) = rest
+    long_attended = long_attended.reshape(-1, span)[:width]
+    attended_t = jnp.concatenate([long_attended, short_low], axis=1)
+
     middle = (
         token_rows
         + lax.dot_general(
@@ -940,7 +1258,7 @@
     )
     normal_two, scale_two = norm_parts(middle)
     normed_two = normal_two * ln2_gain + ln2_bias
-    outgoing = to_experts(normed_two.astype(BF))
+    outgoing = to_experts(normed_two.astype(BF), slot_of)
     centroid_rows = jnp.dot(onehot.astype(BF), centroids, preferred_element_type=F32)
     gate = jax.nn.sigmoid(jnp.sum(normed_two * centroid_rows, axis=1))
 
@@ -972,8 +1290,7 @@
         full_out, grad_middle_low, (((1,), (1,)), ((), ())), preferred_element_type=F32
     ).astype(BF)
     grad_pair = grad_attended_t.reshape(width, rows, span)
-    long_grad = lax.dynamic_index_in_dim(grad_pair, long_at, 1, keepdims=False)
-    short_grad = lax.dynamic_index_in_dim(grad_pair, 1 - long_at, 1, keepdims=False)
+    long_grad, short_grad = grad_pair[:, 0], grad_pair[:, 1]
     long_grad = jnp.pad(long_grad, ((0, pad_heads * size), (0, 0)))
     long_grad = lax.all_to_all(
         long_grad.reshape(blocks, share * size, span), "blk", 0, 0, tiled=True
@@ -999,7 +1316,6 @@
         8 * length * width,
     )
     long_back = lax.all_to_all(long_back, "blk", 0, 0, tiled=True)
-    long_back = long_back.transpose(1, 0, 2, 3).reshape(3, -1, span)[:, :width]
     query_back, own_back, halo_back = call(
         functools.partial(short_backward, block=halo),
         (heads,),
@@ -1029,8 +1345,12 @@
     halo_back = lax.ppermute(halo_back, "blk", [(i + 1, i) for i in range(blocks - 1)])
     own_back = own_back + jnp.pad(halo_back.astype(F32), ((0, 0), (0, 0), (span - halo, 0)))
     short_back = jnp.concatenate([query_back[None], own_back.astype(BF)], axis=0)
-    back_t = in_order(
-        long_back.reshape(3 * width, span), short_back.reshape(3 * width, span), 1
+    short_back = jnp.pad(
+        short_back.reshape(3, heads, size, span), ((0, 0), (0, pad_heads), (0, 0), (0, 0))
+    )
+    short_back = short_back.reshape(3, blocks, share, size, span).transpose(1, 0, 2, 3, 4)
+    back_t = jnp.concatenate(
+        [long_back.reshape(-1, span), short_back.reshape(-1, span)], axis=1
     )
 
     normal_one, scale_one = norm_parts(token_rows)
@@ -1038,9 +1358,12 @@
     qkv_term = lax.dot_general(
         normed_low, back_t, (((0,), (1,)), ((), ())), preferred_element_type=F32
     )
-    qv_sums = jnp.sum(back_t.astype(F32), axis=1)
+    qv_sums = ungrouped(jnp.sum(back_t.astype(F32), axis=1)[None])[0]
     grad_normed_one = lax.dot_general(
-        back_t, full_qkv, (((0,), (1,)), ((), ())), preferred_element_type=F32
+        back_t.reshape(blocks, -1, count),
+        full_qkv,
+        (((0, 1), (0, 2)), ((), ())),
+        preferred_element_type=F32,
     )
     inner_one, ln1_gain_term, ln1_bias_term = norm_back(
         grad_normed_one, normal_one, scale_one, ln1_gain
@@ -1059,8 +1382,8 @@
 
     small = jnp.stack(
         [
-            qv_sums[:width],
-            qv_sums[2 * width :],
+            qv_sums[0],
+            qv_sums[2],
             out_shift_term,
             ln1_gain_term,
             ln1_bias_term,
@@ -1070,13 +1393,21 @@
         axis=1,
     )
     n_small = small.shape[1]
-    packed = jnp.concatenate([qkv_term, out_term, small, centroid_term], axis=1).astype(BF)
-    packed = lax.psum_scatter(packed, "expert", scatter_dimension=0, tiled=True)
-    packed = lax.psum(packed, "blk").astype(F32)
-    qkv_sum = packed[:, : 3 * width]
-    out_sum = packed[:, 3 * width : 4 * width]
-    small_sum = packed[:, 4 * width : 4 * width + n_small]
-    centroid_sum = packed[:, 4 * width + n_small :].T
+    small = jnp.concatenate([small, centroid_term], axis=1)
+    small = jnp.pad(small, ((0, 0), (0, 128 - small.shape[1])))
+    columns = qkv_term.shape[1]
+    half = -(-columns // 256) * 128
+    qkv_sum, out_sum, small_sum = reduce_all(
+        (qkv_term.astype(BF), out_term.astype(BF), small.astype(BF)),
+        (
+            ((1, 0, width), (2, 0, 128)),
+            ((0, 0, half),),
+            ((0, half, columns - half),),
+        ),
+        expert_count,
+        blocks,
+    )
+    centroid_sum = small_sum[:, n_small : n_small + expert_count].T
     shift_sum = lax.psum_scatter(
         jnp.concatenate(
             [up_shift_term.reshape(blocks, -1), down_shift_term.reshape(blocks, -1)], axis=1
@@ -1088,11 +1419,11 @@
     up_shift_sum = shift_sum[:, : up_bias.shape[1] // blocks]
     down_shift_sum = shift_sum[:, up_bias.shape[1] // blocks :]
     return (
-        result.reshape(rows, span, width),
-        grad_tokens.reshape(rows, span, width),
+        ordered(result.reshape(rows, span, width)),
+        ordered(grad_tokens.reshape(rows, span, width)),
         small_sum[:, 3],
         small_sum[:, 4],
-        qkv_sum,
+        ungrouped(qkv_sum).reshape(-1, 3 * width),
         small_sum[:, :2].T,
         out_sum,
         small_sum[:, 2],

time: 713 us -> 636 us (0.89); the launches traced: 705 us -> 638 us
  waiting for transfers between devices: 133 us -> 19.9 us
  Pallas kernels: 361 us -> 439 us
  local copies, waits for them, and re-layouts: 60 us -> 42.3 us
  between operations: 15.5 us -> 2.19 us
  starting transfers between devices: 21 us -> 9.98 us
  matrix products: 49.3 us -> 56.6 us
    pallas_call x1 -> x2, Pallas kernels: 60.2 us -> 166 us  [the longest x1 97.1 us: run_front(): pl.pallas_call(functools.partial(front_kernel, experts, blocks, HEADS, ga...]
    reduce_scatter x1 -> x0, waiting for transfers between devices: 40.1 us -> none  [on_device(): packed = lax.psum_scatter(packed, 'expert', scatter_dimension=0, tiled=True)]
    pallas_call x4 -> x2, Pallas kernels: 78.5 us -> 39.6 us  [call(): pl.pallas_call(kernel, grid=grid, in_specs=in_specs, out_specs=out_specs,...]
    psum x1 -> x0, waiting for transfers between devices: 37.5 us -> none  [on_device(): packed = lax.psum(packed, 'blk').astype(F32)]
    ppermute x1, waiting for transfers between devices: 28.6 us -> 0.01 us  [on_device(): lax.ppermute(halo_back, 'blk', [(i + 1, i) for i in range(blocks - 1)])]
    all_to_all x1 -> x0, blocking collectives: 24.2 us -> none  [on_device(): lax.all_to_all(long_grad.reshape(blocks, share * size, span), 'blk', 0, 0...]
    unnamed x1, blocking collectives: 22.7 us -> 43.4 us
    pallas_call x1, Pallas kernels: 222 us -> 233 us  [run_expert(): pl.pallas_call(functools.partial(expert_kernel, experts, blocks, steps, c...]
  transfers between devices with their start and end apart: 6 -> 3, of which waited for: 4 -> 1; matrix products, arithmetic and copies ran while one was open for 6% -> 2% of each run, Pallas kernels for 5% -> 2%
where the time goes in v3:
time: 636 us; the launch traced here: 638 us
  Pallas kernels  439 us (69%)
  matrix products  56.6 us (9%)
  blocking collectives  43.4 us (7%)
  local copies, waits for them, and re-layouts  42.3 us (7%)
  other arithmetic  24.1 us (4%)
  waiting for transfers between devices  19.9 us (3%)
  starting transfers between devices  9.98 us (2%)
    pallas_call x1, Pallas kernels, run_expert(): pl.pallas_call(functools.partial(expert_kernel, experts, blocks, steps, c...  233 us
    pallas_call x1, Pallas kernels, run_front(): pl.pallas_call(functools.partial(front_kernel, experts, blocks, HEADS, ga...  97.1 us
    pallas_call x1, Pallas kernels, reduce_all(): pl.pallas_call(functools.partial(reduce_kernel, experts, blocks, parts),...  69.3 us
    unnamed x1, blocking collectives  43.4 us
    pallas_call x2, Pallas kernels, call(): pl.pallas_call(kernel, grid=grid, in_specs=in_specs, out_specs=out_specs,...  39.6 us
    dot_general x4, matrix products, dot_nn(): lax.dot_general(a, b, (((1,), (0,)), ((), ())), preferred_element_type=F32)  25.3 us
    all_to_all x1, waiting for transfers between devices, on_device(): lax.all_to_all(long_grad.reshape(blocks, share * size, span), 'blk', 0, 0...  19.9 us
    unnamed x73, local copies, waits for them, and re-layouts  16.5 us
  transfers between devices with their start and end apart: 3, of which 1 were waited for; matrix products, arithmetic and copies ran while one was open for 2% of the time, Pallas kernels for 2%

profile of v3, /device:TPU:0, one launch (start us, length us, event | category | flops | bytes accessed | tf_op | source)
XLA Modules:
  0.0 637.6 jit_solution(8740270114534236763)
XLA Ops:
  21.1 5.1 fusion.22
  26.2 97.1 %shard_map.280 = (bf16[4,768,576]{2,1,0:T(8,128)(2,1)}, bf16[8,96,768]{2,1,0:T(8,128)(2,1)}, bf16[8,256,768]{2,1,0:T(8,128)(2,1)}, bf16[4,3,64,512]{3,2,1,0:T(8,...) custom-call(bf16[4,96,576]{2,1,0:T(8,128)(2,1)} %copy.63.qkv_ref, ...), custom_call_target="tpu_custom_call" | custom-call | tf_op jit(solution)/shard_map/pallas_call | solution.py:542
  123.3 3.4 fusion.68
  129.5 3.3 multiply_reduce_fusion.2
  132.8 5.9 fusion.21
  138.7 233.2 %shard_map.281 = (bf16[8,256,768]{2,1,0:T(8,128)(2,1)}, bf16[8,256,768]{2,1,0:T(8,128)(2,1)}, f32[192,3072]{1,0:T(8,128)}, f32[768,768]{1,0:T(8,128)}, f32[4,1,768]{2,1,0:T(1,128)}, /*index=5*/f32[1,768]{1,0:T(1,128)}) custom-call(bf16[8,256,768]{2,1,0:T(8,128)(2,1)} %bitcast.163, bf16[8,256,768]{2,1,0:T(8,128)(2,1)} %get-tuple-element.41.cot_hbm, ...), custom_call_target="tpu_custom_call" | custom-call | flops 57982058496 | bytes 41943040 | tf_op jit(solution)/shard_map/pallas_call | solution.py:860
  371.9 7.4 %multiply_reduce_fusion = (bf16[768]{0:T(1024)(128)(2,1)S(1)}, f32[1024]{0:T(1024)S(1)}, f32[1024]{0:T(1024)S(1)}, bf16[768]{0:T(1024)(128)(2,1)S(1)}, f32[1024,768]{1,0:T(8,128)S(1)}) fusion(f32[1024]{0:T(1024)S(1)} %add_rsqrt_fusion.1, f32[1024,768]{1,0:T(8,128)} %copy-done.4, f32[1024]{0:T(1024)S(1)} %broadcast_multiply_fusion.6, ...), kind=kOutput, calls=%fused_computation.46 | convolution fusion | flops 3230396928 | bytes 9463808 | tf_op jit(solution)/shard_map/dot_general | solution.py:19
  381.3 6.9 %fusion.31 = (f32[1024]{0:T(1024)S(1)}, f32[1024,768]{1,0:T(8,128)}, bf16[768]{0:T(1024)(128)(2,1)S(1)}, f32[1024,768]{1,0:T(8,128)S(1)}) fusion(bf16[2,512,768]{2,1,0:T(8,128)(2,1)S(1)} %pad_maximum_fusion.5, f32[1024,768]{1,0:T(8,128)S(1)} %copy-done.6, f32[1024]{0:T(1024)S(1)} %add_divide_fusion, f32[1024]{0:T(1024)S(1)} %broadcast_multiply_fusion.4, ...), kind=kOutput, calls=%fused_computation.40 | convolution fusion | flops 3234330880 | bytes 17334784 | tf_op jit(solution)/shard_map/dot_general | solution.py:19
  389.8 2.6 convolution_convert_fusion.1
  392.4 2.6 copy.67
  394.9 2.4 fusion.66
  399.6 4.2 all-to-all-start
  405.0 19.9 %all-to-all-done.grad_ref = bf16[4,192,512]{2,1,0:T(8,128)(2,1)} async-done(((bf16[4,192,512]{2,1,0:T(8,128)(2,1)}), bf16[4,192,512]{2,1,0:T(8,128)(2,1)}, u32[]{:S(2)}, u32[]{:S(2)}) %all-to-all-start) | async-done | bytes 786464 | tf_op jit(solution)/shard_map/all_to_all | solution.py:1295
  424.9 23.9 %shard_map.282 = bf16[4,3,192,512]{3,2,1,0:T(8,128)(2,1)} custom-call(bf16[3,3,2048,64]{3,2,1,0:T(8,128)(2,1)} %get-tuple-element.44.qkv_ref, bf16[4,192,512]{2,1,0:T(8,128)(2,1)} %all-to-all-done.grad_ref, f32[192,2048]{1,0:T(8,128)} %get-tuple-element.45.wide_ref, f32[3,1,2048]{2,1,0:T(1,128)} %get-tuple-element.46.total_ref), custom_call_target="tpu_custom_call" | custom-call | flops 16106127360 | bytes 12582912 | tf_op jit(solution)/shard_map/pallas_call | solution.py:154
  448.8 4.5 all-to-all-start.1
  453.3 15.7 %shard_map.283 = (bf16[768,512]{1,0:T(8,128)(2,1)}, f32[2,768,512]{2,1,0:T(8,128)}, bf16[2,768,256]{2,1,0:T(8,128)(2,1)}) custom-call(bf16[3,12,768,64]{3,2,1,0:T(8,128)(2,1)} %get-tuple-element.47.qkv_ref, bf16[768,512]{1,0:T(8,128)(2,1)} %bitcast.133, f32[768,512]{1,0:T(8,128)} %get-tuple-element.48.wide_ref, f32[12,1,512]{2,1,0:T(1,128)} %get-tuple-element.49.total_ref, ...), custom_call_target="tpu_custom_call" | custom-call | flops 8053063680 | bytes 6291456 | tf_op jit(solution)/shard_map/pallas_call | solution.py:154
  471.0 43.4 %all-reduce.3 = bf16[4,960]{1,0:T(4,128)(2,1)S(1)} all-reduce(bf16[4,960]{1,0:T(4,128)(2,1)S(1)} %pad_maximum_fusion.9), channel_id=2, replica_groups=mesh['blk'=4,'expert'=8] {'blk'}, use_global_device_ids=true, to_apply=%region_19.20.clone | all-reduce | flops 3840 | bytes 15360
  517.6 2.4 fusion.46
  520.0 2.9 convolution_convert_fusion.2
  526.2 3.3 pad_maximum_fusion.2
  531.8 10.1 %fusion.29 = (bf16[768]{0:T(1024)(128)(2,1)S(1)}, f32[1024]{0:T(1024)S(1)}, f32[1024]{0:T(1024)S(1)}, bf16[768]{0:T(1024)(128)(2,1)S(1)}, f32[1024,768,1]{1,0,2:T(8,128)}) fusion(f32[1024]{0:T(1024)S(1)} %add_rsqrt_fusion, f32[1024]{0:T(1024)S(1)} %broadcast_multiply_fusion.2, bf16[512,768]{1,0:T(8,128)(2,1)S(1)} %copy-done, ...), kind=kOutput, calls=%fused_computation.38 | convolution fusion | flops 3643535872 | bytes 12998656 | tf_op jit(solution)/shard_map/dot_general | solution.py:1362
  542.9 6.7 %convolution_convert_fusion = bf16[768,2304]{1,0:T(8,128)(2,1)S(1)} fusion(bf16[2304,512]{1,0:T(8,128)(2,1)} %bitcast.129, bf16[2304,512]{1,0:T(8,128)(2,1)} %bitcast.36, f32[768]{0:T(1024)S(1)} %copy-done.21, f32[1024]{0:T(1024)S(1)} %add_rsqrt_fusion, f32[1024]{0:T(1024)S(1)} %broadcast_multiply_fusion.2, f32[768]{0:T(1024)S(1)} %copy-done.19, ...), kind=kOutput, calls=%fused_computation.7 | convolution fusion | flops 3642163200 | bytes 9844736 | tf_op jit(solution)/shard_map/dot_general | solution.py:1358
  549.6 69.3 %shard_map.284 = (f32[96,2304]{1,0:T(8,128)S(1)}, f32[96,768]{1,0:T(8,128)S(1)}, f32[96,128]{1,0:T(8,128)S(1)}) custom-call(bf16[4,2,96,2304]{3,2,1,0:T(8,128)(2,1)S(1)} %bitcast.113, bf16[4,2,96,768]{3,2,1,0:T(8,128)(2,1)S(1)} %bitcast.114, bf16[4,2,96,128]{3,2,1,0:T(8,128)(2,1)S(1)} %bitcast.115), custom_call_target="tpu_custom_call" | custom-call | tf_op jit(solution)/shard_map/pallas_call | solution.py:1121
  625.2 4.1 fusion.26
  (155 shorter events, 55.4 us)
Async XLA Ops:
  0.6 17.2 %copy-start.17 = (bf16[2,512,768]{2,1,0:T(8,128)(2,1)S(1)}, bf16[2,512,768]{2,1,0:T(8,128)(2,1)}, u32[]{:S(2)}) copy-start(bf16[2,512,768]{2,1,0:T(8,128)(2,1)} %param.17) | copy-start | bytes 4718596
  26.2 97.1 %copy-start = (bf16[512,768]{1,0:T(8,128)(2,1)S(1)}, bf16[512,768]{1,0:T(8,128)(2,1)}, u32[]{:S(2)}) copy-start(bf16[512,768]{1,0:T(8,128)(2,1)} %get-tuple-element.135.short_ref) | copy-start | bytes 2359300
  26.2 97.1 %copy-start.1 = (bf16[512,768]{1,0:T(8,128)(2,1)S(1)}, bf16[512,768]{1,0:T(8,128)(2,1)}, u32[]{:S(2)}) copy-start(bf16[512,768]{1,0:T(8,128)(2,1)} %get-tuple-element.136.row_ref) | copy-start | bytes 2359300
  26.2 97.1 %copy-start.25 = (f32[768]{0:T(1024)S(1)}, f32[768]{0:T(1024)}, u32[]{:S(2)}) copy-start(f32[768]{0:T(1024)} %param.25) | copy-start | bytes 9220
  128.9 3.9 copy-start.5
  371.9 7.5 %copy-start.13 = (bf16[1,512,768]{2,1,0:T(8,128)(2,1)S(1)}, bf16[1,512,768]{2,1,0:T(8,128)(2,1)}, u32[]{:S(2)}) copy-start(bf16[1,512,768]{2,1,0:T(8,128)(2,1)} %get-tuple-element.133) | copy-start | bytes 2359300
  371.9 7.5 %copy-start.14 = (bf16[1,512,768]{2,1,0:T(8,128)(2,1)S(1)}, bf16[1,512,768]{2,1,0:T(8,128)(2,1)}, u32[]{:S(2)}) copy-start(bf16[1,512,768]{2,1,0:T(8,128)(2,1)} %get-tuple-element.134) | copy-start | bytes 2359300
  371.9 7.7 %copy-start.28 = (bf16[8,256,768]{2,1,0:T(8,128)(2,1)S(1)}, bf16[8,256,768]{2,1,0:T(8,128)(2,1)}, u32[]{:S(2)}) copy-start(bf16[8,256,768]{2,1,0:T(8,128)(2,1)} %get-tuple-element.42) | copy-start | bytes 9437188
  381.3 8.5 %copy-start.24 = (bf16[8,96,768]{2,1,0:T(8,128)(2,1)S(1)}, bf16[8,96,768]{2,1,0:T(8,128)(2,1)}, u32[]{:S(2)}) copy-start(bf16[8,96,768]{2,1,0:T(8,128)(2,1)} %get-tuple-element.40) | copy-start | bytes 3538948
  399.6 25.3 %all-to-all-start = ((bf16[4,192,512]{2,1,0:T(8,128)(2,1)}), bf16[4,192,512]{2,1,0:T(8,128)(2,1)}, u32[]{:S(2)}, u32[]{:S(2)}) async-start(bf16[4,192,512]{2,1,0:T(8,128)(2,1)} %bitcast.26), calls=%async_computation | async-start | bytes 1572864 | tf_op jit(solution)/shard_map/all_to_all | solution.py:1295
  448.8 80.8 %all-to-all-start.1 = ((bf16[4,3,192,512]{3,2,1,0:T(8,128)(2,1)}), bf16[4,3,192,512]{3,2,1,0:T(8,128)(2,1)}, u32[]{:S(2)}, u32[]{:S(2)}) async-start(bf16[4,3,192,512]{3,2,1,0:T(8,128)(2,1)} %shard_map.282), calls=%async_computation.1 | async-start | bytes 4718592 | tf_op jit(solution)/shard_map/all_to_all | solution.py:1318
  453.3 17.0 %copy-start.22 = (f32[1,768]{1,0:T(1,128)S(1)}, f32[1,768]{1,0:T(1,128)}, u32[]{:S(2)}) copy-start(f32[1,768]{1,0:T(1,128)} %get-tuple-element.59) | copy-start | bytes 9220
  453.3 17.1 %copy-start.20 = (f32[4,1,768]{2,1,0:T(1,128)S(1)}, f32[4,1,768]{2,1,0:T(1,128)}, u32[]{:S(2)}) copy-start(f32[4,1,768]{2,1,0:T(1,128)} %get-tuple-element.58) | copy-start | bytes 36868
  453.3 17.1 %copy-start.29 = (u32[32]{0:T(128)S(1)}, u32[32]{0:T(128)}, u32[]{:S(2)}) copy-start(u32[32]{0:T(128)} %constant.109) | copy-start | bytes 388
  469.0 54.0 %collective-permute-start = (bf16[2,768,256]{2,1,0:T(8,128)(2,1)}, bf16[2,768,256]{2,1,0:T(8,128)(2,1)}, u32[]{:S(2)}, u32[]{:S(2)}) collective-permute-start(bf16[2,768,256]{2,1,0:T(8,128)(2,1)} %get-tuple-element.52), channel_id=1, source_target_pairs={{8,0},{16,8},{24,16},{9,1},{17,9},{25,17},{10,2},{18,10},{26,18},{... | collective-permute-start | bytes 2359304 | tf_op jit(solution)/shard_map/ppermute | solution.py:1345
  514.4 3.2 copy-start.7
  514.4 5.6 copy-start.11
  520.0 3.0 copy-start.12
  523.0 2.8 copy-start.8
  526.2 5.6 copy-start.19
  531.8 11.1 %copy-start.21 = (f32[768]{0:T(1024)S(1)}, f32[768]{0:T(1024)}, u32[]{:S(2)}) copy-start(f32[768]{0:T(1024)} %param.21) | copy-start | bytes 9220
  621.1 4.1 copy-start.2
  625.1 4.1 copy-start.9
  631.7 2.8 copy-start.16
  (9 other events, 18.5 us)

commit v4 on v3

--- a/solution.py
+++ b/solution.py
@@ -59,110 +59,10 @@
     return (query.astype(F32) * query.shape[-1] ** (-0.5)).astype(BF)
 
 
-def long_backward(
-    qkv_ref, grad_ref, wide_ref, total_ref, out_ref, key_acc, value_acc, *, block
-):
-    query, key, value = scaled(qkv_ref[0, 0]), qkv_ref[1, 0], qkv_ref[2, 0]
-    scale = query.shape[1] ** (-0.5)
-    key_t = key.T
-    visible = causal(block, block, 0)
-    count = query.shape[0] // block
-    key_acc[...] = jnp.zeros_like(key_acc)
-    value_acc[...] = jnp.zeros_like(value_acc)
-    for i in range(count):
-        lo, hi = i * block, (i + 1) * block
-        own = query[lo:hi]
-        grad_t = grad_ref[i]
-        grad = grad_t.T
-        delta = jnp.sum(grad_t.astype(F32) * wide_ref[:, lo:hi], axis=0, keepdims=True)
-        total = total_ref[0, :, lo:hi]
-        query_grad = None
-        for start, stop in ((lo, hi), (0, lo)):
-            if start == stop:
-                continue
-            weights = jnp.exp(dot_nt(key[start:stop], own) - total)
-            if start == lo:
-                weights = jnp.where(visible, weights, 0.0)
-            scores = weights * (dot_nt(value[start:stop], grad) - delta)
-            scores_low = scores.astype(BF)
-            value_acc[start:stop] += dot_nn(weights.astype(BF), grad)
-            key_acc[start:stop] += dot_nn(scores_low, own)
-            part = dot_nn(key_t[:, start:stop], scores_low)
-            query_grad = part if query_grad is None else query_grad + part
-        out_ref[i, 0] = (query_grad * scale).astype(BF)
-    key_grad = key_acc[...].T.astype(BF)
-    value_grad = value_acc[...].T.astype(BF)
-    for i in range(count):
-        out_ref[i, 1] = key_grad[:, i * block : (i + 1) * block]
-        out_ref[i, 2] = value_grad[:, i * block : (i + 1) * block]
-
-
 def short_visible(key_ids, query_ids, i, block, halo):
     lo = i * block
     same = key_ids[lo : lo + halo + block] == query_ids[:, lo : lo + block]
     return same & causal(halo + block, block, halo)
-
-
-def short_backward(
-    qkv_ref,
-    grad_ref,
-    wide_ref,
-    total_ref,
-    key_ids,
-    query_ids,
-    query_out,
-    own_out,
-    halo_out,
-    key_acc,
-    value_acc,
-    *,
-    block,
-):
-    query, key, value = scaled(qkv_ref[0, 0]), qkv_ref[1, 0], qkv_ref[2, 0]
-    scale = query.shape[1] ** (-0.5)
-    key_t = key.T
-    span = query_ids.shape[1]
-    halo = query.shape[0] - span
-    key_acc[...] = jnp.zeros_like(key_acc)
-    value_acc[...] = jnp.zeros_like(value_acc)
-    for i in range(span // block):
-        lo, hi = i * block, (i + 1) * block
-        visible = short_visible(key_ids[...], query_ids[...], i, block, halo)
-        own = query[lo + halo : hi + halo]
-        grad_t = grad_ref[:, lo:hi]
-        grad = grad_t.T
-        delta = jnp.sum(grad_t.astype(F32) * wide_ref[:, lo:hi], axis=0, keepdims=True)
-        scores = dot_nt(key[lo : hi + halo], own)
-        weights = jnp.exp(jnp.where(visible, scores, NEGATIVE) - total_ref[0, :, lo:hi])
-        scores = weights * (dot_nt(value[lo : hi + halo], grad) - delta)
-        scores_low = scores.astype(BF)
-        value_acc[lo : hi + halo] += dot_nn(weights.astype(BF), grad)
-        key_acc[lo : hi + halo] += dot_nn(scores_low, own)
-        part = dot_nn(key_t[:, lo : hi + halo], scores_low)
-        query_out[:, lo:hi] = (part * scale).astype(BF)
-    for n, acc in enumerate((key_acc, value_acc)):
-        whole = acc[...].T
-        halo_out[n] = whole[:, :halo].astype(BF)
-        own_out[n] = whole[:, halo:]
-
-
-def whole_spec(shape):
-    return pl.BlockSpec(shape, lambda *_: (0,) * len(shape))
-
-
-def call(kernel, grid, ins, in_specs, outs, out_specs, scratch, flops, bytes_accessed, vmem=56 << 20):
-    return pl.pallas_call(
-        kernel,
-        grid=grid,
-        in_specs=in_specs,
-        out_specs=out_specs,
-        out_shape=outs,
-        scratch_shapes=scratch,
-        compiler_params=pltpu.CompilerParams(vmem_limit_bytes=vmem),
-        cost_estimate=pl.CostEstimate(
-            flops=int(flops), bytes_accessed=int(bytes_accessed), transcendentals=0
-        ),
-    )(*ins)
 
 
 MESH = pl.DeviceIdType.MESH
@@ -603,6 +503,62 @@
     return qkv_shard, full_out, results
 
 
+def line_sums(z, blocks, up_held, down_held, part_send, part_recv, up_sum, down_sum):
+    rounds = len(up_held) - 1
+    lanes = down_held[0].shape[3]
+
+    def part_copies(r, p):
+        bit = 1 << r
+        mine = lax.rem(z // bit, 2)
+        partner = z + bit - 2 * bit * mine
+        copies = []
+        for k in range((blocks >> r) // 2):
+            for n, held in enumerate((up_held, down_held)):
+                copies.append(
+                    remote(
+                        held[r].at[p, 2 * k + 1 - mine],
+                        held[r + 1].at[p, k],
+                        part_send.at[r, n, p, k],
+                        part_recv.at[r, n, p, k],
+                        {"blk": partner},
+                    )
+                )
+        return copies
+
+    def add_parts(r, p):
+        mine = lax.rem(z // (1 << r), 2)
+        for copy in part_copies(r, p):
+            copy.wait_recv()
+        for k in range((blocks >> r) // 2):
+            up = up_held[r][p, 2 * k + mine].astype(F32) + up_held[r + 1][p, k].astype(F32)
+            down = down_held[r][p, 2 * k + mine].astype(F32) + down_held[r + 1][p, k].astype(F32)
+            if r + 1 < rounds:
+                up_held[r + 1][p, k] = up.astype(BF)
+                down_held[r + 1][p, k] = down.astype(BF)
+            else:
+                up_sum[p] = up
+                down_sum[p * lanes : (p + 1) * lanes, :] = down.T
+        if r + 1 < rounds:
+            for copy in part_copies(r + 1, p):
+                copy.start()
+
+    return part_copies, add_parts
+
+
+def sum_scratch(parts, blocks, depth, width, first):
+    rounds = (blocks - 1).bit_length()
+    lanes = 128
+    dma = pltpu.SemaphoreType.DMA
+    return (
+        [
+            pltpu.VMEM((parts, blocks >> r, depth, blocks * lanes), BF)
+            for r in range(first, rounds + 1)
+        ]
+        + [pltpu.VMEM((parts, blocks >> r, width, lanes), BF) for r in range(first, rounds + 1)]
+        + [dma((rounds, 2, parts, blocks // 2)), dma((rounds, 2, parts, blocks // 2))]
+    )
+
+
 def gelu_parts(hidden):
     cdf = 0.5 * (1.0 + lax.erf(hidden * 0.7071067811865476))
     density = jnp.exp(-0.5 * hidden * hidden) * 0.3989422804014327
@@ -613,6 +569,7 @@
     experts,
     blocks,
     steps,
+    rest,
     chunk,
     x_hbm,
     cot_hbm,
@@ -625,9 +582,11 @@
         down_shift_ref,
         centroid_ref,
         back_grad,
-        back_out,
+        produced,
         up_sum,
         down_sum,
+        up_rest,
+        down_rest,
         up_shift_out,
         down_shift_out,
         x_buf,
@@ -664,60 +623,22 @@
             device_id_type=MESH,
         )
 
-    def back_copy(n, d):
+    def back_copy(d):
         target = lax.rem(me + d, experts)
-        return pltpu.make_async_remote_copy(
-            src_ref=(low_buf, x_buf)[n].at[target],
-            dst_ref=(back_grad, back_out)[n].at[me],
-            send_sem=back_send.at[n, d],
-            recv_sem=back_recv.at[n, d],
-            device_id={"expert": target},
-            device_id_type=MESH,
-        )
-
-    def back_local(n):
-        return pltpu.make_async_copy(
-            (low_buf, x_buf)[n].at[me], (back_grad, back_out)[n].at[me], local_sem.at[n]
-        )
-
-    def part_copies(r, p):
-        bit = 1 << r
-        mine = lax.rem(z // bit, 2)
-        partner = z + bit - 2 * bit * mine
-        copies = []
-        for k in range((blocks >> r) // 2):
-            for n, held in enumerate((up_held, down_held)):
-                copies.append(
-                    pltpu.make_async_remote_copy(
-                        src_ref=held[r].at[p, 2 * k + 1 - mine],
-                        dst_ref=held[r + 1].at[p, k],
-                        send_sem=part_send.at[r, n, p, k],
-                        recv_sem=part_recv.at[r, n, p, k],
-                        device_id={"blk": partner},
-                        device_id_type=MESH,
-                    )
-                )
-        return copies
-
-    def add_parts(r, p):
-        mine = lax.rem(z // (1 << r), 2)
-        for copy in part_copies(r, p):
-            copy.wait_recv()
-        for k in range((blocks >> r) // 2):
-            up = up_held[r][p, 2 * k + mine].astype(F32) + up_held[r + 1][p, k].astype(F32)
-            down = down_held[r][p, 2 * k + mine].astype(F32) + down_held[r + 1][p, k].astype(F32)
-            if r + 1 < rounds:
-                up_held[r + 1][p, k] = up.astype(BF)
-                down_held[r + 1][p, k] = down.astype(BF)
-            else:
-                for j in range(blocks):
-                    at = j * steps * lanes + p * lanes
-                    up_sum[:, at : at + lanes] = up[:, j * lanes : (j + 1) * lanes]
-                down_sum[p * lanes : (p + 1) * lanes, :] = down.T
-        if r + 1 < rounds:
-            for copy in part_copies(r + 1, p):
-                copy.start()
-
+        return remote(
+            low_buf.at[target],
+            back_grad.at[me],
+            back_send.at[d],
+            back_recv.at[d],
+            {"expert": target},
+        )
+
+    back_local = pltpu.make_async_copy(low_buf.at[me], back_grad.at[me], local_sem.at[0])
+    out_copy = pltpu.make_async_copy(x_buf, produced, local_sem.at[1])
+
+    part_copies, add_parts = line_sums(
+        z, blocks, up_held, down_held, part_send, part_recv, up_sum, down_sum
+    )
     cot_copy = pltpu.make_async_copy(cot_hbm, low_buf, local_sem.at[2])
     own_copy = pltpu.make_async_copy(x_hbm.at[me], x_buf.at[me], local_sem.at[3])
     x_flat, low_flat = x_buf.reshape(rows, width), low_buf.reshape(rows, width)
@@ -781,15 +702,27 @@
     up_total, down_total, shift_total = totals
     up_total = up_total.astype(BF)
     depth = width // blocks
+    keep = steps - rest
     for j in range(blocks):
-        up_held[0][step, j] = up_total[j * depth : (j + 1) * depth]
-        down_held[0][step, j] = down_total[:, j * lanes : (j + 1) * lanes].astype(BF)
         up_shift_out[j] = shift_total[:, j * lanes : (j + 1) * lanes]
-    for copy in part_copies(0, step):
-        copy.start()
+
+    def store(up_target, down_target):
+        for j in range(blocks):
+            up_target[j] = up_total[j * depth : (j + 1) * depth]
+            down_target[j] = down_total[:, j * lanes : (j + 1) * lanes].astype(BF)
+
+    @pl.when(step < keep)
+    def _():
+        store(up_held[0].at[step], down_held[0].at[step])
+        for copy in part_copies(0, step):
+            copy.start()
+
+    @pl.when(step >= keep)
+    def _():
+        store(up_rest.at[0], down_rest.at[0])
 
     tasks = sorted(
-        ((r, p) for p in range(steps) for r in range(rounds)), key=lambda task: (sum(task), task[0])
+        ((r, p) for p in range(keep) for r in range(rounds)), key=lambda task: (sum(task), task[0])
     )
     early = [[] for _ in range(steps)]
     for turn, task in enumerate(tasks):
@@ -818,26 +751,18 @@
             low_flat[lo : lo + chunk] = (
                 grad_acc[lo : lo + chunk] + inner * (1.0 - gate) * centroid_ref[...]
             ).astype(BF)
-        back_local(0).start()
+        back_local.start()
         for d in range(1, experts):
-            back_copy(0, d).start()
-        back_local(1).start()
-        left = [task for task in tasks if all(task not in done for done in early)]
-        half = len(left) // 2
-        for r, p in left[:half]:
-            add_parts(r, p)
+            back_copy(d).start()
+        out_copy.start()
+        for r, p in tasks:
+            if all((r, p) not in done for done in early):
+                add_parts(r, p)
+        back_local.wait()
+        out_copy.wait()
         for d in range(1, experts):
-            back_copy(0, d).wait_send()
-            back_copy(1, d).start()
-        for r, p in left[half:]:
-            add_parts(r, p)
-        for n in range(2):
-            back_local(n).wait()
-            for d in range(1, experts):
-                back_copy(n, d).wait_recv()
-        for d in range(1, experts):
-            back_copy(1, d).wait_send()
-        for p in range(steps):
+            back_copy(d).wait()
+        for p in range(keep):
             for r in range(rounds):
                 for copy in part_copies(r, p):
                     copy.wait_send()
@@ -852,13 +777,15 @@
     rounds = (blocks - 1).bit_length()
     chunk = min(512, rows)
     depth = width // blocks
+    rest = steps // 3
+    keep = steps - rest
     any_spec = pl.BlockSpec(memory_space=pl.ANY)
 
     def once(shape):
         return pl.BlockSpec(shape, lambda f: (0,) * len(shape), pipeline_mode=pl.Buffered(1))
 
     return pl.pallas_call(
-        functools.partial(expert_kernel, experts, blocks, steps, chunk),
+        functools.partial(expert_kernel, experts, blocks, steps, rest, chunk),
         grid=(steps,),
         in_specs=[any_spec] * 2
         + [pl.BlockSpec((width, lanes), lambda f, j=j: (0, j * steps + f)) for j in range(blocks)]
@@ -868,16 +795,24 @@
         out_specs=(
             any_spec,
             any_spec,
-            once((depth, hidden)),
-            once((hidden // blocks, width)),
+            once((keep, depth, blocks * lanes)),
+            once((keep * lanes, width)),
+            pl.BlockSpec(
+                (1, blocks, depth, blocks * lanes), lambda f: (jnp.maximum(f - keep, 0), 0, 0, 0)
+            ),
+            pl.BlockSpec(
+                (1, blocks, width, lanes), lambda f: (jnp.maximum(f - keep, 0), 0, 0, 0)
+            ),
             pl.BlockSpec((blocks, 1, lanes), lambda f: (0, 0, f)),
             once((1, width)),
         ),
         out_shape=(
             jax.ShapeDtypeStruct(x.shape, BF),
             jax.ShapeDtypeStruct(x.shape, BF),
-            jax.ShapeDtypeStruct((depth, hidden), F32),
-            jax.ShapeDtypeStruct((hidden // blocks, width), F32),
+            jax.ShapeDtypeStruct((keep, depth, blocks * lanes), F32),
+            jax.ShapeDtypeStruct((keep * lanes, width), F32),
+            jax.ShapeDtypeStruct((rest, blocks, depth, blocks * lanes), BF),
+            jax.ShapeDtypeStruct((rest, blocks, width, lanes), BF),
             jax.ShapeDtypeStruct((blocks, 1, hidden // blocks), F32),
             jax.ShapeDtypeStruct((1, width), F32),
         ),
@@ -891,16 +826,11 @@
             pltpu.VMEM((rows, 1), F32),
             pltpu.SemaphoreType.DMA((experts,)),
             pltpu.SemaphoreType.DMA((experts,)),
-            pltpu.SemaphoreType.DMA((2, experts)),
-            pltpu.SemaphoreType.DMA((2, experts)),
+            pltpu.SemaphoreType.DMA((experts,)),
+            pltpu.SemaphoreType.DMA((experts,)),
             pltpu.SemaphoreType.DMA((4,)),
         ]
-        + [pltpu.VMEM((steps, blocks >> r, depth, blocks * lanes), BF) for r in range(rounds + 1)]
-        + [pltpu.VMEM((steps, blocks >> r, width, lanes), BF) for r in range(rounds + 1)]
-        + [
-            pltpu.SemaphoreType.DMA((rounds, 2, steps, blocks // 2)),
-            pltpu.SemaphoreType.DMA((rounds, 2, steps, blocks // 2)),
-        ],
+        + sum_scratch(keep, blocks, depth, width, 0),
         compiler_params=pltpu.CompilerParams(
             collective_id=1, has_side_effects=True, vmem_limit_bytes=62 << 20
         ),
@@ -915,6 +845,475 @@
         *([up_shift] * blocks),
         down_shift,
         centroid,
+    )
+
+
+def long_back_head(query, key, value, grad_ref, wide_ref, total_ref, out_ref, head, key_acc, value_acc):
+    scale = query.shape[1] ** (-0.5)
+    query = scaled(query)
+    key_t = key.T
+    count, _, _, block = grad_ref.shape
+    visible = causal(block, block, 0)
+    key_acc[...] = jnp.zeros_like(key_acc)
+    value_acc[...] = jnp.zeros_like(value_acc)
+    for i in range(count):
+        lo, hi = i * block, (i + 1) * block
+        own = query[lo:hi]
+        grad_t = grad_ref[i, head]
+        grad = grad_t.T
+        delta = jnp.sum(grad_t.astype(F32) * wide_ref[:, lo:hi], axis=0, keepdims=True)
+        total = total_ref[0, :, lo:hi]
+        query_grad = None
+        for start, stop in ((lo, hi), (0, lo)):
+            if start == stop:
+                continue
+            weights = jnp.exp(dot_nt(key[start:stop], own) - total)
+            if start == lo:
+                weights = jnp.where(visible, weights, 0.0)
+            scores = weights * (dot_nt(value[start:stop], grad) - delta)
+            scores_low = scores.astype(BF)
+            value_acc[start:stop] += dot_nn(weights.astype(BF), grad)
+            key_acc[start:stop] += dot_nn(scores_low, own)
+            part = dot_nn(key_t[:, start:stop], scores_low)
+            query_grad = part if query_grad is None else query_grad + part
+        out_ref[i, 0, head] = (query_grad * scale).astype(BF)
+    key_grad = key_acc[...].T.astype(BF)
+    value_grad = value_acc[...].T.astype(BF)
+    for i in range(count):
+        out_ref[i, 1, head] = key_grad[:, i * block : (i + 1) * block]
+        out_ref[i, 2, head] = value_grad[:, i * block : (i + 1) * block]
+
+
+def short_back_head(
+    query, key, value, grad_t, wide_ref, total_ref, key_ids, query_ids, key_acc, value_acc, query_out, block
+):
+    scale = query.shape[1] ** (-0.5)
+    query = scaled(query)
+    key_t = key.T
+    extent, span = query.shape[0], query_ids.shape[1]
+    halo = extent - span
+    key_acc[0:extent] = jnp.zeros((extent, key_acc.shape[1]), F32)
+    value_acc[0:extent] = jnp.zeros((extent, key_acc.shape[1]), F32)
+    for i in range(span // block):
+        lo, hi = i * block, (i + 1) * block
+        visible = short_visible(key_ids[...], query_ids[...], i, block, halo)
+        own = query[lo + halo : hi + halo]
+        part_t = grad_t[:, lo:hi]
+        grad = part_t.T
+        delta = jnp.sum(part_t.astype(F32) * wide_ref[:, lo:hi], axis=0, keepdims=True)
+        scores = dot_nt(key[lo : hi + halo], own)
+        weights = jnp.exp(jnp.where(visible, scores, NEGATIVE) - total_ref[0, :, lo:hi])
+        scores = weights * (dot_nt(value[lo : hi + halo], grad) - delta)
+        scores_low = scores.astype(BF)
+        value_acc[lo : hi + halo] += dot_nn(weights.astype(BF), grad)
+        key_acc[lo : hi + halo] += dot_nn(scores_low, own)
+        part = dot_nn(key_t[:, lo : hi + halo], scores_low)
+        query_out[:, lo:hi] = (part * scale).astype(BF)
+    return key_acc[0:extent].T, value_acc[0:extent].T
+
+
+def tail_kernel(
+    experts,
+    blocks,
+    heads,
+    lead,
+    rest,
+    back_grad,
+    slot_ref,
+    normal_ref,
+    scale_ref,
+    cot_ref,
+    gain_ref,
+    attended_ref,
+    out_weight,
+    long_qkv,
+    long_wide,
+    long_total,
+    short_qkv,
+    short_wide,
+    short_total,
+    key_ids,
+    query_ids,
+    produced,
+    up_rest,
+    down_rest,
+    shift_ref,
+    back_out,
+    long_back,
+    halo_in,
+    grad_middle,
+    out_term,
+    sums_ref,
+    query_out,
+    own_out,
+    up_sum,
+    down_sum,
+    shift_sum,
+    grad_low,
+    long_stage,
+    short_grad,
+    long_grad,
+    back_stage,
+    halo_stage,
+    shift_in,
+    key_acc,
+    value_acc,
+    out_send,
+    out_recv,
+    grad_send,
+    grad_recv,
+    back_send,
+    back_recv,
+    halo_send,
+    halo_recv,
+    shift_send,
+    shift_recv,
+    local_sem,
+    *refs,
+):
+    rounds = (blocks - 1).bit_length()
+    up_held = (up_rest,) + refs[:rounds]
+    down_held = (down_rest,) + refs[rounds : 2 * rounds]
+    part_send, part_recv = refs[2 * rounds :]
+    step = pl.program_id(0)
+    me, z = lax.axis_index("expert"), lax.axis_index("blk")
+    share, size, span = long_stage.shape[1:]
+    width = out_weight.shape[0]
+    count = slot_ref.shape[0]
+    halo = halo_stage.shape[3]
+    chunk = min(256, span)
+    part_copies, add_parts = line_sums(
+        z, blocks, up_held, down_held, part_send, part_recv, up_sum, down_sum
+    )
+    line = [lax.rem(z + d, blocks) for d in range(blocks)]
+
+    def out_copy(d):
+        target = lax.rem(me + d, experts)
+        return remote(
+            produced.at[target], back_out.at[me], out_send.at[d], out_recv.at[d], {"expert": target}
+        )
+
+    def grad_copy(d):
+        return remote(
+            long_stage.at[line[d]], long_grad.at[z], grad_send.at[d], grad_recv.at[d], {"blk": line[d]}
+        )
+
+    def back_copy(head, d):
+        return remote(
+            back_stage.at[line[d], :, head],
+            long_back.at[z, :, head],
+            back_send.at[head, d],
+            back_recv.at[head, d],
+            {"blk": line[d]},
+        )
+
+    def back_local(head):
+        return pltpu.make_async_copy(
+            back_stage.at[z, :, head], long_back.at[z, :, head], back_send.at[head, 0]
+        )
+
+    def shift_copy(d):
+        return remote(
+            shift_ref.at[line[d]], shift_in.at[d], shift_send.at[d], shift_recv.at[d], {"blk": line[d]}
+        )
+
+    def halo_copy(n):
+        part = pl.ds(0, lead) if n == 0 else pl.ds(lead, heads - lead)
+        left = lax.rem(z + blocks - 1, blocks)
+        return remote(
+            halo_stage.at[:, part], halo_in.at[:, part], halo_send.at[n], halo_recv.at[n], {"blk": left}
+        )
+
+    def halo_local(n):
+        part = pl.ds(0, lead) if n == 0 else pl.ds(lead, heads - lead)
+        return pltpu.make_async_copy(halo_stage.at[:, part], halo_in.at[:, part], halo_recv.at[n])
+
+    own_out_copy = pltpu.make_async_copy(produced.at[me], back_out.at[me], local_sem.at[0])
+
+    def send_halo(n):
+        @pl.when(z > 0)
+        def _():
+            halo_copy(n).start()
+
+        @pl.when(z == blocks - 1)
+        def _():
+            halo_local(n).start()
+
+    @pl.when(step == 0)
+    def _():
+        greet(experts, blocks)
+        for copy in part_copies(0, 0):
+            copy.start()
+        for d in range(1, blocks):
+            shift_copy(d).start()
+        own_out_copy.start()
+        for d in range(1, experts):
+            out_copy(d).start()
+        spare = blocks * share - heads
+        flat_stage = long_stage.reshape(blocks * share, size, span)
+        if spare:
+            flat_stage[heads:] = jnp.zeros((spare, size, span), BF)
+        slot_line = lax.broadcasted_iota(jnp.int32, (chunk, back_grad.shape[0]), 1)
+        sums = None
+        for lo in range(0, count, chunk):
+            hi = lo + chunk
+            chosen = (slot_ref[lo:hi] == slot_line).astype(F32).astype(BF)
+            upstream = dot_nn(chosen, back_grad[...])
+            normal = normal_ref[lo:hi]
+            inner, gain_part, bias_part = norm_back(upstream, normal, scale_ref[lo:hi], gain_ref[...])
+            middle = cot_ref[lo:hi].astype(F32) + inner
+            grad_middle[lo:hi] = middle
+            low = middle.astype(BF)
+            grad_low[lo:hi] = low
+            part = (gain_part, bias_part, jnp.sum(middle, axis=0))
+            sums = part if sums is None else tuple(a + b for a, b in zip(sums, part))
+            grad_t = dot_nt(out_weight[...], low).astype(BF).reshape(heads, size, chunk)
+            if lo < span:
+                flat_stage[:heads, :, lo:hi] = grad_t
+            else:
+                short_grad[:, :, lo - span : hi - span] = grad_t
+            if hi == span:
+                for d in range(1, blocks):
+                    grad_copy(d).start()
+        sums_ref[...] = jnp.zeros_like(sums_ref)
+        for n, part in enumerate(sums):
+            sums_ref[n] = part
+        out_term[...] = dot_nn(attended_ref[...], grad_low[...]).astype(BF)
+
+    first_long = lead + 1
+    is_long = (step >= first_long) & (step < first_long + share)
+
+    @pl.when((step > 0) & jnp.logical_not(is_long))
+    def _():
+        head = step - 1 - jnp.where(step >= first_long, share, 0)
+        query, key, value = (short_qkv[kind, 0] for kind in range(3))
+        grads = short_back_head(
+            query,
+            key,
+            value,
+            short_grad[head],
+            short_wide,
+            short_total,
+            key_ids,
+            query_ids,
+            key_acc,
+            value_acc,
+            query_out,
+            min(SHORT, span),
+        )
+        for n, grad in enumerate(grads):
+            halo_stage[n, head] = grad[:, :halo].astype(BF)
+            own_out[n] = grad[:, halo:]
+
+    @pl.when(step == lead)
+    def _():
+        send_halo(0)
+
+    @pl.when(step == first_long)
+    def _():
+        for d in range(1, blocks):
+            grad_copy(d).wait_recv()
+        long_grad[z] = long_stage[z]
+        add_parts(0, 0)
+        for p in range(1, rest):
+            for copy in part_copies(0, p):
+                copy.start()
+
+    @pl.when(is_long)
+    def _():
+        head = step - first_long
+        query, key, value = (long_qkv[kind, 0] for kind in range(3))
+        long_back_head(
+            query, key, value, long_grad, long_wide, long_total, back_stage, head, key_acc, value_acc
+        )
+        back_local(head).start()
+        for d in range(1, blocks):
+            back_copy(head, d).start()
+
+    tasks = sorted(
+        ((r, p) for p in range(rest) for r in range(rounds)), key=lambda task: (sum(task), task[0])
+    )[1:]
+
+    @pl.when(step == first_long + share)
+    def _():
+        for r, p in tasks[:-1]:
+            add_parts(r, p)
+
+    @pl.when(step == heads + share)
+    def _():
+        send_halo(1)
+        if tasks:
+            add_parts(*tasks[-1])
+        for d in range(1, blocks):
+            shift_copy(d).wait()
+        total = shift_ref[z]
+        for d in range(1, blocks):
+            total = total + shift_in[d]
+        shift_sum[...] = total
+        own_out_copy.wait()
+        for d in range(1, experts):
+            out_copy(d).wait()
+        for d in range(1, blocks):
+            grad_copy(d).wait_send()
+        for head in range(share):
+            back_local(head).wait()
+            for d in range(1, blocks):
+                back_copy(head, d).wait()
+        for p in range(rest):
+            for r in range(rounds):
+                for copy in part_copies(r, p):
+                    copy.wait_send()
+        for n in range(2):
+
+            @pl.when(z > 0)
+            def _(n=n):
+                halo_copy(n).wait_send()
+
+            @pl.when(z < blocks - 1)
+            def _(n=n):
+                halo_copy(n).wait_recv()
+
+            @pl.when(z == blocks - 1)
+            def _(n=n):
+                halo_local(n).wait()
+
+
+def run_tail(
+    back_grad,
+    slot_of,
+    normal,
+    scale,
+    cot,
+    gain,
+    attended_t,
+    out_weight,
+    long_parts,
+    short_parts,
+    key_ids,
+    query_ids,
+    produced,
+    up_rest,
+    down_rest,
+    shifts,
+    blocks,
+):
+    experts = produced.shape[0]
+    slots, width = back_grad.shape
+    count = slot_of.shape[0]
+    long_qkv, long_wide, long_total = long_parts
+    short_qkv, short_wide, short_total = short_parts
+    _, share, length, size = long_qkv.shape
+    extent, span = short_qkv.shape[2], query_ids.shape[1]
+    halo = extent - span
+    heads = HEADS
+    lead = heads // 2
+    rest, _, depth, _ = up_rest.shape
+    any_spec = pl.BlockSpec(memory_space=pl.ANY)
+    dma = pltpu.SemaphoreType.DMA
+
+    def whole(shape):
+        return pl.BlockSpec(shape, lambda f: (0,) * len(shape), pipeline_mode=pl.Buffered(1))
+
+    def short_at(f):
+        return jnp.where(f <= lead, jnp.maximum(f - 1, 0), jnp.maximum(f - 1 - share, lead - 1))
+
+    def long_at(f):
+        return jnp.clip(f - 1 - lead, 0, share - 1)
+
+    return pl.pallas_call(
+        functools.partial(tail_kernel, experts, blocks, heads, lead, rest),
+        grid=(1 + heads + share,),
+        in_specs=[
+            whole(back_grad.shape),
+            whole(slot_of.shape),
+            whole(normal.shape),
+            whole(scale.shape),
+            whole(cot.shape),
+            whole(gain.shape),
+            whole(attended_t.shape),
+            whole(out_weight.shape),
+            pl.BlockSpec((3, 1, length, size), lambda f: (0, long_at(f), 0, 0)),
+            pl.BlockSpec((size, length), lambda f: (long_at(f), 0)),
+            pl.BlockSpec((1, 1, length), lambda f: (long_at(f), 0, 0)),
+            pl.BlockSpec((3, 1, extent, size), lambda f: (0, short_at(f), 0, 0)),
+            pl.BlockSpec((size, span), lambda f: (short_at(f), 0)),
+            pl.BlockSpec((1, 1, span), lambda f: (short_at(f), 0, 0)),
+            whole(key_ids.shape),
+            whole(query_ids.shape),
+            any_spec,
+            whole(up_rest.shape),
+            whole(down_rest.shape),
+            whole(shifts.shape),
+        ],
+        out_specs=(
+            any_spec,
+            any_spec,
+            any_spec,
+            whole((count, width)),
+            whole((width, width)),
+            whole((8, width)),
+            pl.BlockSpec((size, span), lambda f: (short_at(f), 0)),
+            pl.BlockSpec((2, size, span), lambda f: (0, short_at(f), 0)),
+            whole((rest, depth, up_rest.shape[3])),
+            whole((rest * 128, width)),
+            whole(shifts.shape[1:]),
+        ),
+        out_shape=(
+            jax.ShapeDtypeStruct(produced.shape, BF),
+            jax.ShapeDtypeStruct((blocks, 3, share, size, span), BF),
+            jax.ShapeDtypeStruct((2, heads, size, halo), BF),
+            jax.ShapeDtypeStruct((count, width), F32),
+            jax.ShapeDtypeStruct((width, width), BF),
+            jax.ShapeDtypeStruct((8, width), F32),
+            jax.ShapeDtypeStruct((width, span), BF),
+            jax.ShapeDtypeStruct((2, width, span), F32),
+            jax.ShapeDtypeStruct((rest, depth, up_rest.shape[3]), F32),
+            jax.ShapeDtypeStruct((rest * 128, width), F32),
+            jax.ShapeDtypeStruct(shifts.shape[1:], F32),
+        ),
+        scratch_shapes=[
+            pltpu.VMEM((count, width), BF),
+            pltpu.VMEM((blocks, share, size, span), BF),
+            pltpu.VMEM((heads, size, span), BF),
+            pltpu.VMEM((blocks, share, size, span), BF),
+            pltpu.VMEM((blocks, 3, share, size, span), BF),
+            pltpu.VMEM((2, heads, size, halo), BF),
+            pltpu.VMEM(shifts.shape, F32),
+            pltpu.VMEM((length, size), F32),
+            pltpu.VMEM((length, size), F32),
+            dma((experts,)),
+            dma((experts,)),
+            dma((blocks,)),
+            dma((blocks,)),
+            dma((share, blocks)),
+            dma((share, blocks)),
+            dma((2,)),
+            dma((2,)),
+            dma((blocks,)),
+            dma((blocks,)),
+            dma((1,)),
+        ]
+        + sum_scratch(rest, blocks, depth, width, 1),
+        compiler_params=pltpu.CompilerParams(
+            collective_id=3, has_side_effects=True, vmem_limit_bytes=60 << 20
+        ),
+    )(
+        back_grad,
+        slot_of,
+        normal,
+        scale,
+        cot,
+        gain,
+        attended_t,
+        out_weight,
+        *long_parts,
+        *short_parts,
+        key_ids,
+        query_ids,
+        produced,
+        up_rest,
+        down_rest,
+        shifts,
     )
 
 
@@ -1265,7 +1664,7 @@
     own_centroid = lax.dynamic_index_in_dim(
         centroids.astype(F32), lax.axis_index("expert"), 0, keepdims=True
     )
-    back_grad, back_out, up_sum, down_sum, up_shift_term, down_shift_term = run_expert(
+    back_grad, produced, up_first, down_first, up_rest, down_rest, up_shift, down_shift = run_expert(
         outgoing,
         received_cot,
         up_weight[0],
@@ -1275,75 +1674,48 @@
         own_centroid,
         blocks,
     )
-    back_grad = back_grad.reshape(slots, width)
+    shift_parts = jnp.concatenate([up_shift, down_shift.reshape(blocks, 1, -1)], axis=2)
+    shift_parts = jnp.pad(shift_parts, ((0, 0), (0, 0), (0, -shift_parts.shape[2] % 128)))
+    (
+        back_out,
+        long_back,
+        halo_back,
+        grad_middle,
+        out_term,
+        tail_sums,
+        query_back,
+        own_back,
+        up_last,
+        down_last,
+        shift_sum,
+    ) = run_tail(
+        back_grad.reshape(slots, width),
+        slot_of[:, None],
+        normal_two,
+        scale_two,
+        grad_low,
+        ln2_gain[None],
+        attended_t,
+        full_out,
+        (long_qkv, long_wide, long_total),
+        (short_qkv, short_wide, short_total),
+        key_ids,
+        query_ids,
+        produced,
+        up_rest,
+        down_rest,
+        shift_parts,
+        blocks,
+    )
     back_out = back_out.reshape(slots, width)
-
-    grad_normed_two = dot_nn(from_slots, back_grad)
-    inner_two, ln2_gain_term, ln2_bias_term = norm_back(
-        grad_normed_two, normal_two, scale_two, ln2_gain
-    )
+    ln2_gain_term, ln2_bias_term, out_shift_term = tail_sums[0], tail_sums[1], tail_sums[2]
     grad_out = grad_low.astype(F32)
-    grad_middle = grad_out + inner_two
-    out_shift_term = jnp.sum(grad_middle, axis=0)
-    grad_middle_low = grad_middle.astype(BF)
-    grad_attended_t = lax.dot_general(
-        full_out, grad_middle_low, (((1,), (1,)), ((), ())), preferred_element_type=F32
-    ).astype(BF)
-    grad_pair = grad_attended_t.reshape(width, rows, span)
-    long_grad, short_grad = grad_pair[:, 0], grad_pair[:, 1]
-    long_grad = jnp.pad(long_grad, ((0, pad_heads * size), (0, 0)))
-    long_grad = lax.all_to_all(
-        long_grad.reshape(blocks, share * size, span), "blk", 0, 0, tiled=True
-    )
-    out_term = lax.dot_general(
-        attended_t, grad_middle_low, (((1,), (0,)), ((), ())), preferred_element_type=F32
-    )
-
-    long_back = call(
-        functools.partial(long_backward, block=span),
-        (share,),
-        (long_qkv, long_grad, long_wide, long_total),
-        [
-            pl.BlockSpec((3, 1, length, size), lambda h: (0, h, 0, 0)),
-            pl.BlockSpec((blocks, size, span), lambda h: (0, h, 0)),
-            pl.BlockSpec((size, length), lambda h: (h, 0)),
-            pl.BlockSpec((1, 1, length), lambda h: (h, 0, 0)),
-        ],
-        jax.ShapeDtypeStruct((blocks, 3, share * size, span), BF),
-        pl.BlockSpec((blocks, 3, size, span), lambda h: (0, 0, h, 0)),
-        [pltpu.VMEM((length, size), F32), pltpu.VMEM((length, size), F32)],
-        5 * share * length * length * 256,
-        8 * length * width,
-    )
-    long_back = lax.all_to_all(long_back, "blk", 0, 0, tiled=True)
-    query_back, own_back, halo_back = call(
-        functools.partial(short_backward, block=halo),
-        (heads,),
-        (short_qkv, short_grad, short_wide, short_total, key_ids, query_ids),
-        [
-            pl.BlockSpec((3, 1, halo + span, size), lambda h: (0, h, 0, 0)),
-            pl.BlockSpec((size, span), lambda h: (h, 0)),
-            pl.BlockSpec((size, span), lambda h: (h, 0)),
-            pl.BlockSpec((1, 1, span), lambda h: (h, 0, 0)),
-            whole_spec((halo + span, 1)),
-            whole_spec((1, span)),
-        ],
-        (
-            jax.ShapeDtypeStruct((width, span), BF),
-            jax.ShapeDtypeStruct((2, width, span), F32),
-            jax.ShapeDtypeStruct((2, width, halo), BF),
-        ),
-        (
-            pl.BlockSpec((size, span), lambda h: (h, 0)),
-            pl.BlockSpec((2, size, span), lambda h: (0, h, 0)),
-            pl.BlockSpec((2, size, halo), lambda h: (0, h, 0)),
-        ),
-        [pltpu.VMEM((halo + span, size), F32), pltpu.VMEM((halo + span, size), F32)],
-        5 * heads * span * 2 * 2 * halo * 256,
-        16 * span * width,
-    )
-    halo_back = lax.ppermute(halo_back, "blk", [(i + 1, i) for i in range(blocks - 1)])
-    own_back = own_back + jnp.pad(halo_back.astype(F32), ((0, 0), (0, 0), (span - halo, 0)))
+    up_sum = jnp.concatenate([up_first, up_last], axis=0)
+    up_sum = up_sum.reshape(-1, up_sum.shape[1], blocks, 128).transpose(1, 2, 0, 3)
+    up_sum = up_sum.reshape(up_sum.shape[0], -1)
+    down_sum = jnp.concatenate([down_first, down_last], axis=0)
+    halo_back = jnp.where(own < blocks - 1, halo_back.reshape(2, width, halo).astype(F32), 0.0)
+    own_back = own_back + jnp.pad(halo_back, ((0, 0), (0, 0), (span - halo, 0)))
     short_back = jnp.concatenate([query_back[None], own_back.astype(BF)], axis=0)
     short_back = jnp.pad(
         short_back.reshape(3, heads, size, span), ((0, 0), (0, pad_heads), (0, 0), (0, 0))
@@ -1398,7 +1770,7 @@
     columns = qkv_term.shape[1]
     half = -(-columns // 256) * 128
     qkv_sum, out_sum, small_sum = reduce_all(
-        (qkv_term.astype(BF), out_term.astype(BF), small.astype(BF)),
+        (qkv_term.astype(BF), out_term, small.astype(BF)),
         (
             ((1, 0, width), (2, 0, 128)),
             ((0, 0, half),),
@@ -1408,16 +1780,9 @@
         blocks,
     )
     centroid_sum = small_sum[:, n_small : n_small + expert_count].T
-    shift_sum = lax.psum_scatter(
-        jnp.concatenate(
-            [up_shift_term.reshape(blocks, -1), down_shift_term.reshape(blocks, -1)], axis=1
-        ).astype(BF),
-        "blk",
-        scatter_dimension=0,
-        tiled=True,
-    ).astype(F32)
-    up_shift_sum = shift_sum[:, : up_bias.shape[1] // blocks]
-    down_shift_sum = shift_sum[:, up_bias.shape[1] // blocks :]
+    shift_cut = up_bias.shape[1] // blocks
+    up_shift_sum = shift_sum[:, :shift_cut]
+    down_shift_sum = shift_sum[:, shift_cut : shift_cut + width // blocks]
     return (
         ordered(result.reshape(rows, span, width)),
         ordered(grad_tokens.reshape(rows, span, width)),

time: 636 us -> 566 us (0.89)
  blocking collectives: 43.4 us -> 0 us
  waiting for transfers between devices: 19.9 us -> 0 us
  Pallas kernels: 439 us -> 457 us
  matrix products: 56.6 us -> 39 us
  starting transfers between devices: 9.98 us -> 0 us
    unnamed x1 -> x0, blocking collectives: 43.4 us -> none
    pallas_call x3 -> x2, Pallas kernels: 273 us -> 298 us  [the longest x1 163 us: run_expert(): pl.pallas_call(functools.partial(expert_kernel, experts, blocks, steps, r...]
    all_to_all x2 -> x0, waiting for transfers between devices: 19.9 us -> none  [the longest x1 19.9 us: on_device(): lax.all_to_all(long_grad.reshape(blocks, share * size, span), 'blk', 0, 0...]
    all_to_all x2 -> x0, starting transfers between devices: 8.7 us -> none  [the longest x1 4.5 us: on_device(): long_back = lax.all_to_all(long_back, 'blk', 0, 0, tiled=True)]
    pallas_call x1, Pallas kernels: 69.3 us -> 61.4 us  [reduce_all(): pl.pallas_call(functools.partial(reduce_kernel, experts, blocks, parts),...]
    unnamed x73 -> x76, local copies, waits for them, and re-layouts: 16.5 us -> 8.88 us
    dot_general x4 -> x3, matrix products: 25.3 us -> 17.9 us  [dot_nn(): lax.dot_general(a, b, (((1,), (0,)), ((), ())), preferred_element_type=F32)]
    reshape x1 -> x3, local copies, waits for them, and re-layouts: 0.09 us -> 6.68 us  [the longest x2 6.6 us: on_device(): up_sum.reshape(-1, up_sum.shape[1], blocks, 128).transpose(1, 2, 0, 3)]
  transfers between devices with their start and end apart: 3 -> 0, of which waited for: 1 -> 0; matrix products, arithmetic and copies ran while one was open for 2% -> 0% of each run, Pallas kernels for 2% -> 0%
where the time goes in v4:
time: 566 us; the launch traced here: 562 us
  Pallas kernels  457 us (81%)
  matrix products  39 us (7%)
  local copies, waits for them, and re-layouts  36.1 us (6%)
  other arithmetic  28.3 us (5%)
    pallas_call x1, Pallas kernels, run_expert(): pl.pallas_call(functools.partial(expert_kernel, experts, blocks, steps, r...  163 us
    pallas_call x1, Pallas kernels, run_tail(): pl.pallas_call(functools.partial(tail_kernel, experts, blocks, heads, lea...  135 us
    pallas_call x1, Pallas kernels, run_front(): pl.pallas_call(functools.partial(front_kernel, experts, blocks, HEADS, ga...  97.3 us
    pallas_call x1, Pallas kernels, reduce_all(): pl.pallas_call(functools.partial(reduce_kernel, experts, blocks, parts),...  61.4 us
    dot_general x3, matrix products, dot_nn(): lax.dot_general(a, b, (((1,), (0,)), ((), ())), preferred_element_type=F32)  17.9 us

profile of v4, /device:TPU:0, one launch (start us, length us, event | category | flops | bytes accessed | tf_op | source)
XLA Modules:
  0.0 562.3 jit_solution(13425466631565018203)
XLA Ops:
  2.7 2.6 dynamic-slice_bitcast_fusion
  7.0 2.3 reduce-window.6
  9.8 5.1 fusion.20
  18.3 97.3 %shard_map.280 = (bf16[4,768,576]{2,1,0:T(8,128)(2,1)}, bf16[8,96,768]{2,1,0:T(8,128)(2,1)}, bf16[8,256,768]{2,1,0:T(8,128)(2,1)}, bf16[4,3,64,512]{3,2,1,0:T(8,...) custom-call(bf16[4,96,576]{2,1,0:T(8,128)(2,1)} %copy.64.qkv_ref, ...), custom_call_target="tpu_custom_call" | custom-call | tf_op jit(solution)/shard_map/pallas_call | solution.py:442
  115.6 3.4 fusion.62
  121.3 5.2 fusion.19
  127.2 163.0 %shard_map.281 = (bf16[8,256,768]{2,1,0:T(8,128)(2,1)}, bf16[8,256,768]{2,1,0:T(8,128)(2,1)}, f32[4,192,512]{2,1,0:T(8,128)}, f32[512,768]{1,0:T(8,128)}, bf16[2...) custom-call(bf16[8,256,768]{2,1,0:T(8,128)(2,1)} %bitcast.171, ...), custom_call_target="tpu_custom_call" | custom-call | flops 57982058496 | bytes 41943040 | tf_op jit(solution)/shard_map/pallas_call | solution.py:787
  297.9 135.2 %shard_map.282 = (bf16[8,256,768]{2,1,0:T(8,128)(2,1)}, bf16[4,3,3,64,512]{4,3,2,1,0:T(8,128)(2,1)}, bf16[2,12,64,256]{3,2,1,0:T(8,128)(2,1)}, f32[1024,768]{1,0...) custom-call(bf16[2048,768]{1,0:T(8,128)(2,1)} %bitcast.131, ...), custom_call_target="tpu_custom_call" | custom-call | tf_op jit(solution)/shard_map/pallas_call | solution.py:1223
  433.1 2.8 maximum_bitcast_fusion
  436.2 1.9 reshape.250
  438.1 4.7 copy.97
  442.8 4.1 broadcast_in_dim_reshape.5
  448.8 7.6 %multiply_reduce_fusion = (f32[1024]{0:T(1024)S(1)}, f32[1024,768]{1,0:T(8,128)}) fusion(bf16[2,512,768]{2,1,0:T(8,128)(2,1)} %pad_maximum_fusion.6, f32[1024,768]{1,0:T(8,128)S(1)} %copy-done.8, f32[1024]{0:T(1024)S(1)} %add_divide_fusion, bf16[2048,768]{1,0:T(8,128)(2,1)} %bitcast.170, s32[1024]{0:T(1024)S(1)} %bitcast.161), kind=kOutput, calls=%fused_computation.42 | convolution fusion | flops 3227253760 | bytes 11022336 | tf_op jit(solution)/shard_map/dot_general | solution.py:19
  456.4 2.1 fusion.43
  459.8 2.3 add_convert_fusion
  462.5 2.2 reduce.3
  464.9 1.5 pad_maximum_fusion.2
  467.4 1.5 copy-done.31
  468.8 8.1 %fusion.27 = (bf16[768]{0:T(1024)(128)(2,1)S(1)}, f32[1024]{0:T(1024)S(1)}, f32[1024]{0:T(1024)S(1)}, bf16[768]{0:T(1024)(128)(2,1)S(1)}, f32[1024,768,1]{1,0,2:T(8,128)}) fusion(f32[1024]{0:T(1024)S(1)} %add_rsqrt_fusion, f32[1024]{0:T(1024)S(1)} %broadcast_multiply_fusion.2, bf16[512,768]{1,0:T(8,128)(2,1)S(1)} %copy-done.4, ...), kind=kOutput, calls=%fused_computation.34 | convolution fusion | flops 3643535872 | bytes 12998656 | tf_op jit(solution)/shard_map/dot_general | solution.py:1734
  477.3 6.8 %convolution_convert_fusion = bf16[768,2304]{1,0:T(8,128)(2,1)S(1)} fusion(bf16[2304,512]{1,0:T(8,128)(2,1)} %bitcast.139, bf16[2304,512]{1,0:T(8,128)(2,1)} %bitcast.136, f32[768]{0:T(1024)S(1)} %copy-done.28, f32[1024]{0:T(1024)S(1)} %add_rsqrt_fusion, f32[1024]{0:T(1024)S(1)} %broadcast_multiply_fusion.2, f32[768]{0:T(1024)S(1)} %copy-done.25, ...), kind=kOutput, calls=%fused_computation.6 | convolution fusion | flops 3642163200 | bytes 9844736 | tf_op jit(solution)/shard_map/dot_general | solution.py:1730
  484.2 61.4 %shard_map.283 = (f32[96,2304]{1,0:T(8,128)S(1)}, f32[96,768]{1,0:T(8,128)S(1)}, f32[96,128]{1,0:T(8,128)S(1)}) custom-call(bf16[4,2,96,2304]{3,2,1,0:T(8,128)(2,1)S(1)} %bitcast.120, bf16[4,2,96,768]{3,2,1,0:T(8,128)(2,1)S(1)} %bitcast.121, bf16[4,2,96,128]{3,2,1,0:T(8,128)(2,1)S(1)} %bitcast.122), custom_call_target="tpu_custom_call" | custom-call | tf_op jit(solution)/shard_map/pallas_call | solution.py:1520
  551.8 4.1 fusion.24
  556.5 1.9 pad_maximum_fusion.1
  558.4 1.9 pad_maximum_fusion
  (146 shorter events, 31.5 us)
Async XLA Ops:
  0.6 4.7 copy-start.30
  0.7 6.3 %copy-start.21 = (s32[1,2,512,1]{2,3,1,0:T(1,128)S(1)}, s32[1,2,512,1]{2,3,1,0:T(1,128)}, u32[]{:S(2)}) copy-start(s32[1,2,512,1]{2,3,1,0:T(1,128)} %param.19) | copy-start | bytes 12292
  0.7 9.2 %copy-start.13 = (bf16[2,512,768]{2,1,0:T(8,128)(2,1)S(1)}, bf16[2,512,768]{2,1,0:T(8,128)(2,1)}, u32[]{:S(2)}) copy-start(bf16[2,512,768]{2,1,0:T(8,128)(2,1)} %param.33) | copy-start | bytes 4718596
  9.8 5.1 copy-start.27
  9.8 5.9 %copy-start.20 = (bf16[96,2304]{1,0:T(8,128)(2,1)S(1)}, bf16[96,2304]{1,0:T(8,128)(2,1)}, u32[]{:S(2)}) copy-start(bf16[96,2304]{1,0:T(8,128)(2,1)} %param.22) | copy-start | bytes 1327108
  17.1 98.4 %copy-start.3 = (bf16[512,768]{1,0:T(8,128)(2,1)S(1)}, bf16[512,768]{1,0:T(8,128)(2,1)}, u32[]{:S(2)}) copy-start(bf16[512,768]{1,0:T(8,128)(2,1)} %get-tuple-element.145.short_ref) | copy-start | bytes 2359300
  17.1 98.4 %copy-start.5 = (bf16[512,768]{1,0:T(8,128)(2,1)S(1)}, bf16[512,768]{1,0:T(8,128)(2,1)}, u32[]{:S(2)}) copy-start(bf16[512,768]{1,0:T(8,128)(2,1)} %get-tuple-element.146.row_ref) | copy-start | bytes 2359300
  17.2 98.5 %copy-start.32 = (f32[768]{0:T(1024)S(1)}, f32[768]{0:T(1024)}, u32[]{:S(2)}) copy-start(f32[768]{0:T(1024)} %param.25) | copy-start | bytes 9220
  121.0 5.6 copy-start.1
  121.3 5.2 copy-start.24
  127.2 165.3 %copy-start.18 = (bf16[4,3,64,512]{3,2,1,0:T(8,128)(2,1)S(1)}, bf16[4,3,64,512]{3,2,1,0:T(8,128)(2,1)}, u32[]{:S(2)}) copy-start(bf16[4,3,64,512]{3,2,1,0:T(8,128)(2,1)} %get-tuple-element.48) | copy-start | bytes 2359300
  127.2 165.3 %copy-start.19 = (bf16[768,512]{1,0:T(8,128)(2,1)S(1)}, bf16[768,512]{1,0:T(8,128)(2,1)}, u32[]{:S(2)}) copy-start(bf16[768,512]{1,0:T(8,128)(2,1)} %get-tuple-element.49) | copy-start | bytes 2359300
  290.2 5.7 %copy-start.14 = (bf16[2,512,768]{2,1,0:T(8,128)(2,1)S(1)}, bf16[2,512,768]{2,1,0:T(8,128)(2,1)}, u32[]{:S(2)}) copy-start(bf16[2,512,768]{2,1,0:T(8,128)(2,1)} %param.33) | copy-start | bytes 4718596
  297.9 135.2 %copy-start.16 = (f32[512,768]{1,0:T(8,128)S(1)}, f32[512,768]{1,0:T(8,128)}, u32[]{:S(2)}) copy-start(f32[512,768]{1,0:T(8,128)} %get-tuple-element.79) | copy-start | bytes 4718596
  433.1 2.9 copy-start.15
  433.1 2.9 copy-start.17
  442.8 4.1 copy-start.2
  462.5 3.9 copy-start.4
  462.5 3.9 copy-start.6
  464.9 3.9 copy-start.31
  466.4 10.5 %copy-start.12 = (bf16[3,4,3,64,512]{4,3,2,0,1:T(8,128)(2,1)}, bf16[3,4,3,64,512]{4,3,2,0,1:T(8,128)(2,1)S(1)}, u32[]{:S(2)}) copy-start(bf16[3,4,3,64,512]{4,3,2,0,1:T(8,128)(2,1)S(1)} %pad_maximum_fusion.2) | copy-start | bytes 7077892
  468.8 8.1 %copy-start.23 = (f32[8,768]{1,0:T(8,128)S(1)}, f32[8,768]{1,0:T(8,128)}, u32[]{:S(2)}) copy-start(f32[8,768]{1,0:T(8,128)} %get-tuple-element.72) | copy-start | bytes 73732
  477.3 6.8 %copy-start = (bf16[768,768]{1,0:T(8,128)(2,1)S(1)}, bf16[768,768]{1,0:T(8,128)(2,1)}, u32[]{:S(2)}) copy-start(bf16[768,768]{1,0:T(8,128)(2,1)} %get-tuple-element.71) | copy-start | bytes 3538948
  551.8 4.1 copy-start.10
  (9 other events, 16.6 us)

commit v5 on v4

--- a/solution.py
+++ b/solution.py
@@ -77,6 +77,15 @@
         device_id=device,
         device_id_type=MESH,
     )
+
+
+def across(place, mask, count):
+    bit = 1
+    while bit < count:
+        place_bit, mask_bit = lax.rem(place // bit, 2), lax.rem(mask // bit, 2)
+        place = place + bit * mask_bit * (1 - 2 * place_bit)
+        bit *= 2
+    return place
 
 
 def greet(experts, blocks):
@@ -105,8 +114,8 @@
     row_ref,
     short_ref,
     cot_ref,
-    gain_ref,
-    bias_ref,
+    route_ref,
+    vectors,
     shift_ref,
     key_ids,
     query_ids,
@@ -118,6 +127,7 @@
         full_qkv = qkv_ref
     (
         received_cot,
+        slot_out,
         attended,
         long_qkv,
         long_wide,
@@ -132,6 +142,7 @@
         long_store,
         short_store,
         low_stage,
+        cot_stage,
         shard_send,
         shard_recv,
         row_send,
@@ -187,7 +198,7 @@
         pltpu.make_async_copy(row_ref, rows_buf.at[z], local_sem.at[0]),
         pltpu.make_async_copy(short_ref, short_buf.at[pl.ds(halo, span)], local_sem.at[1]),
     ]
-    own_cot = pltpu.make_async_copy(cot_ref.at[me], received_cot.at[me], local_sem.at[2])
+    own_cot = pltpu.make_async_copy(cot_stage.at[me], received_cot.at[me], local_sem.at[2])
     load_weights = pltpu.make_async_copy(full_qkv, weights, local_sem.at[3])
     own_shards = []
     sent = []
@@ -207,7 +218,7 @@
     def cot_copy(d):
         target = lax.rem(me + d, experts)
         return remote(
-            cot_ref.at[target],
+            cot_stage.at[target],
             received_cot.at[me],
             cot_send.at[d],
             cot_recv.at[d],
@@ -248,15 +259,38 @@
             def _():
                 row(slot, 2 * k + 1, left).start()
 
-    def project(source, lo, count, groups, store):
-        low = norm_low(source, gain_ref[...], bias_ref[...])
+    def project(source, rows, groups, store):
+        low = norm_low(source, vectors[0:1], vectors[1:2])
         for n, group in enumerate(groups):
             part = (dot_nn(low, weights[group]) + shift_ref[group]).astype(BF)
             for kind in range(3):
                 for head in range(share):
                     at = (kind * share + head) * size
                     if n * share + head < store.shape[1]:
-                        store[kind, n * share + head, lo : lo + count] = part[:, at : at + size]
+                        store[kind, n * share + head, rows] = part[:, at : at + size]
+
+    def sort_cot():
+        capacity, width = cot_stage.shape[1:]
+        count = cot_ref.shape[0]
+        lines = -(-experts // 8) * 8
+        expert_line = lax.broadcasted_iota(jnp.int32, (lines, count), 0)
+        named = (route_ref[...] == expert_line).astype(F32)
+        upto = lax.broadcasted_iota(jnp.int32, (count, count), 0) <= lax.broadcasted_iota(
+            jnp.int32, (count, count), 1
+        )
+        ranks = dot_nn(named.astype(BF), upto.astype(F32).astype(BF))
+        slots = named * (ranks - 1.0 + (expert_line * capacity).astype(F32))
+        slots = jnp.sum(slots, axis=0, keepdims=True).astype(jnp.int32)
+        slot_out[...] = slots
+        flat = cot_stage.reshape(experts * capacity, width)
+        block_rows = min(512, experts * capacity)
+
+        @pl.loop(0, experts * capacity // block_rows)
+        def _(turn):
+            first = pl.multiple_of(turn * block_rows, block_rows)
+            line = lax.broadcasted_iota(jnp.int32, (block_rows, count), 0) + first
+            chosen = (line == slots).astype(F32).astype(BF)
+            flat[pl.ds(first, block_rows)] = dot_nn(chosen, cot_ref[...]).astype(BF)
 
     @pl.when(step == 0)
     def _():
@@ -279,6 +313,7 @@
 
         for copy in sent:
             copy.start()
+        sort_cot()
         hand_on(1)
         for copy in handed:
             copy.wait_recv()
@@ -305,8 +340,11 @@
         for copy in local:
             copy.wait()
         load_weights.wait()
-        for lo in range(0, halo + span, short_block):
-            project(short_buf[lo : lo + short_block], lo, short_block, range(blocks), short_store)
+
+        @pl.loop(0, (halo + span) // short_block)
+        def _(turn):
+            rows = pl.ds(pl.multiple_of(turn * short_block, short_block), short_block)
+            project(short_buf[rows], rows, range(blocks), short_store)
 
     for k in range(2, blocks):
 
@@ -336,8 +374,10 @@
 
     @pl.when(step == heads)
     def _():
-        for slot in range(blocks):
-            project(rows_buf[slot], slot * block, block, [z], long_store)
+        @pl.loop(0, blocks)
+        def _(slot):
+            rows = pl.ds(pl.multiple_of(slot * block, block), block)
+            project(rows_buf[slot], rows, [z], long_store)
 
     @pl.when(step >= heads)
     def _():
@@ -404,7 +444,7 @@
 
 
 def run_front(
-    qkv_shard, out_shard, row, short_row, cot, gain, bias, shifts, key_ids, query_ids, experts, blocks
+    qkv_shard, out_shard, row, short_row, cot, routes, vectors, shifts, key_ids, query_ids, experts, blocks
 ):
     span, width = row.shape
     size = width // HEADS
@@ -412,6 +452,7 @@
     part = qkv_shard.shape[2]
     share = part // size // 3
     length = blocks * span
+    sorted_shape = (experts, 2 * cot.shape[0] // experts, width)
     gathers = qkv_shard.shape[1] % 16 == 0
     if not gathers:
         qkv_shard = lax.all_gather(qkv_shard, "expert", axis=1, tiled=True)
@@ -444,10 +485,11 @@
             front_kernel, experts, blocks, HEADS, gathers, span, min(SHORT, span)
         ),
         grid=(HEADS + share,),
-        in_specs=[any_spec] * 5
+        in_specs=[any_spec] * 4
         + [
-            whole((1, width)),
-            whole((1, width)),
+            whole(cot.shape),
+            whole(routes.shape),
+            whole(vectors.shape),
             whole((blocks, 1, part)),
             whole((halo + span, 1)),
             whole((1, span)),
@@ -455,6 +497,7 @@
         out_specs=((any_spec,) * 2 if gathers else ())
         + (
             any_spec,
+            whole(routes.shape),
             any_spec,
             long_head(3, 1, length, size),
             pl.BlockSpec((size, length), lambda f: (jnp.maximum(f - HEADS, 0), 0)),
@@ -466,7 +509,8 @@
         ),
         out_shape=(gathered_shapes if gathers else ())
         + (
-            jax.ShapeDtypeStruct(cot.shape, BF),
+            jax.ShapeDtypeStruct(sorted_shape, BF),
+            jax.ShapeDtypeStruct(routes.shape, jnp.int32),
             jax.ShapeDtypeStruct((blocks, share, size, span), BF),
             jax.ShapeDtypeStruct((3, share, length, size), BF),
             jax.ShapeDtypeStruct((share * size, length), F32),
@@ -483,6 +527,7 @@
             pltpu.VMEM((3, share, length, size), BF),
             pltpu.VMEM((3, HEADS, halo + span, size), BF),
             pltpu.VMEM((blocks, share, size, span), BF),
+            pltpu.VMEM(sorted_shape, BF),
             dma((2, experts)),
             dma((2, experts)),
             dma((2 * blocks,)),
@@ -497,15 +542,14 @@
         compiler_params=pltpu.CompilerParams(
             collective_id=0, has_side_effects=True, vmem_limit_bytes=56 << 20
         ),
-    )(qkv_shard, out_shard, row, short_row, cot, gain, bias, shifts, key_ids, query_ids)
+    )(qkv_shard, out_shard, row, short_row, cot, routes, vectors, shifts, key_ids, query_ids)
     if gathers:
         return results[0], results[1].reshape(-1, out_shard.shape[1]), results[2:]
     return qkv_shard, full_out, results
 
 
-def line_sums(z, blocks, up_held, down_held, part_send, part_recv, up_sum, down_sum):
+def line_sums(z, blocks, up_held, down_held, part_send, part_recv, put):
     rounds = len(up_held) - 1
-    lanes = down_held[0].shape[3]
 
     def part_copies(r, p):
         bit = 1 << r
@@ -536,8 +580,7 @@
                 up_held[r + 1][p, k] = up.astype(BF)
                 down_held[r + 1][p, k] = down.astype(BF)
             else:
-                up_sum[p] = up
-                down_sum[p * lanes : (p + 1) * lanes, :] = down.T
+                put(p, up, down.T)
         if r + 1 < rounds:
             for copy in part_copies(r + 1, p):
                 copy.start()
@@ -596,6 +639,9 @@
         out_acc,
         grad_acc,
         gate_ref,
+        up_acc,
+        down_acc,
+        shift_acc,
         x_send,
         x_recv,
         back_send,
@@ -611,20 +657,16 @@
     capacity, width = x_buf.shape[1:]
     rows = experts * capacity
     lanes = 128
+    sources, chunks = chunk // capacity, rows // chunk
 
     def x_copy(d):
-        target = lax.rem(me + d, experts)
-        return pltpu.make_async_remote_copy(
-            src_ref=x_hbm.at[target],
-            dst_ref=x_buf.at[me],
-            send_sem=x_send.at[d],
-            recv_sem=x_recv.at[d],
-            device_id={"expert": target},
-            device_id_type=MESH,
+        target = across(me, jnp.int32(d), experts)
+        return remote(
+            x_hbm.at[target], x_buf.at[me], x_send.at[d], x_recv.at[d], {"expert": target}
         )
 
     def back_copy(d):
-        target = lax.rem(me + d, experts)
+        target = across(me, jnp.int32(d), experts)
         return remote(
             low_buf.at[target],
             back_grad.at[me],
@@ -636,8 +678,15 @@
     back_local = pltpu.make_async_copy(low_buf.at[me], back_grad.at[me], local_sem.at[0])
     out_copy = pltpu.make_async_copy(x_buf, produced, local_sem.at[1])
 
+
+    def put(p, up, down):
+        for j in range(blocks):
+            first = (j * steps + p) * lanes
+            up_sum[:, first : first + lanes] = up[:, j * lanes : (j + 1) * lanes]
+        down_sum[p * lanes : (p + 1) * lanes] = down
+
     part_copies, add_parts = line_sums(
-        z, blocks, up_held, down_held, part_send, part_recv, up_sum, down_sum
+        z, blocks, up_held, down_held, part_send, part_recv, put
     )
     cot_copy = pltpu.make_async_copy(cot_hbm, low_buf, local_sem.at[2])
     own_copy = pltpu.make_async_copy(x_hbm.at[me], x_buf.at[me], local_sem.at[3])
@@ -659,57 +708,86 @@
         pl.semaphore_wait(barrier, experts - 1 + rounds)
         for d in range(1, experts):
             x_copy(d).start()
+        up_sum[...] = jnp.zeros_like(up_sum)
+        down_sum[...] = jnp.zeros_like(down_sum)
         out_acc[...] = jnp.zeros_like(out_acc)
         grad_acc[...] = jnp.zeros_like(grad_acc)
         cot_copy.wait()
         own_copy.wait()
-        for d in range(1, experts):
-            x_copy(d).wait_recv()
-        for lo in range(0, rows, chunk):
-            x = x_flat[lo : lo + chunk]
-            logit = jnp.sum(x.astype(F32) * centroid_ref[...], axis=1, keepdims=True)
-            gate = 1.0 / (1.0 + jnp.exp(-logit))
-            gate_ref[lo : lo + chunk] = gate
-            low = (low_flat[lo : lo + chunk].astype(F32) * gate).astype(BF)
-            low_flat[lo : lo + chunk] = low
-            xt_ref[:, lo : lo + chunk] = x.T
-            gt_ref[:, lo : lo + chunk] = low.T
-            part = jnp.sum(low.astype(F32), axis=0, keepdims=True)
-            if lo:
-                down_shift_out[...] += part
-            else:
-                down_shift_out[...] = part
+        down_shift_out[...] = jnp.zeros_like(down_shift_out)
+
+    def prepare(at, near):
+        for n in range(sources):
+            d = near * sources + n
+
+            @pl.when(d != 0)
+            def _(d=d):
+                x_copy(d).wait_recv()
+
+        x = x_flat[at]
+        logit = jnp.sum(x.astype(F32) * centroid_ref[...], axis=1, keepdims=True)
+        gate = 1.0 / (1.0 + jnp.exp(-logit))
+        gate_ref[at] = gate
+        low = (low_flat[at].astype(F32) * gate).astype(BF)
+        low_flat[at] = low
+        xt_ref[:, at] = x.T
+        gt_ref[:, at] = low.T
+        down_shift_out[...] += jnp.sum(low.astype(F32), axis=0, keepdims=True)
+
+    def answer(at, near):
+        gate = gate_ref[at]
+        out = (out_acc[at] + down_shift_ref[...]).astype(BF)
+        inner = jnp.sum(low_flat[at].astype(F32) * out.astype(F32), axis=1, keepdims=True)
+        x_flat[at] = out
+        low_flat[at] = (grad_acc[at] + inner * (1.0 - gate) * centroid_ref[...]).astype(BF)
+        for n in range(sources):
+            d = near * sources + n
+
+            @pl.when(d != 0)
+            def _(d=d):
+                back_copy(d).start()
 
     up = jnp.concatenate([ref[...] for ref in ups], axis=1)
     down = jnp.concatenate([ref[...] for ref in downs], axis=0)
     up_shift = jnp.concatenate([ref[...] for ref in up_shifts], axis=1)
-    totals = None
-    for lo in range(0, rows, chunk):
-        x = x_flat[lo : lo + chunk]
-        low = low_flat[lo : lo + chunk]
+    up_acc[...] = jnp.zeros_like(up_acc)
+    down_acc[...] = jnp.zeros_like(down_acc)
+    shift_acc[...] = jnp.zeros_like(shift_acc)
+
+    @pl.loop(0, chunks)
+    def _(turn):
+        near = jnp.where(step == steps - 1, chunks - 1 - turn, turn)
+        at = pl.ds(pl.multiple_of(across(me // sources, near, chunks) * chunk, chunk), chunk)
+
+        @pl.when(step == 0)
+        def _():
+            prepare(at, near)
+
+        x = x_flat[at]
+        low = low_flat[at]
         hidden = dot_nn(x, up) + up_shift
         active, slope = gelu_parts(hidden)
         active = active.astype(BF)
         grad_low = (dot_nt(low, down) * slope).astype(BF)
-        out_acc[lo : lo + chunk] += dot_nn(active, down)
-        grad_acc[lo : lo + chunk] += dot_nt(grad_low, up)
-        parts = (
-            dot_nn(xt_ref[:, lo : lo + chunk], grad_low),
-            dot_nn(gt_ref[:, lo : lo + chunk], active),
-            jnp.sum(grad_low.astype(F32), axis=0, keepdims=True),
-        )
-        totals = parts if totals is None else tuple(a + b for a, b in zip(totals, parts))
-    up_total, down_total, shift_total = totals
-    up_total = up_total.astype(BF)
+        out_acc[at] += dot_nn(active, down)
+        grad_acc[at] += dot_nt(grad_low, up)
+        up_acc[...] += dot_nn(xt_ref[:, at], grad_low)
+        down_acc[...] += dot_nn(gt_ref[:, at], active)
+        shift_acc[...] += jnp.sum(grad_low.astype(F32), axis=0, keepdims=True)
+
+        @pl.when(step == steps - 1)
+        def _():
+            answer(at, near)
+
     depth = width // blocks
     keep = steps - rest
     for j in range(blocks):
-        up_shift_out[j] = shift_total[:, j * lanes : (j + 1) * lanes]
+        up_shift_out[j] = shift_acc[:, j * lanes : (j + 1) * lanes]
 
     def store(up_target, down_target):
         for j in range(blocks):
-            up_target[j] = up_total[j * depth : (j + 1) * depth]
-            down_target[j] = down_total[:, j * lanes : (j + 1) * lanes].astype(BF)
+            up_target[j] = up_acc[j * depth : (j + 1) * depth].astype(BF)
+            down_target[j] = down_acc[:, j * lanes : (j + 1) * lanes].astype(BF)
 
     @pl.when(step < keep)
     def _():
@@ -741,19 +819,7 @@
     def _():
         for d in range(1, experts):
             x_copy(d).wait_send()
-        for lo in range(0, rows, chunk):
-            gate = gate_ref[lo : lo + chunk]
-            out = (out_acc[lo : lo + chunk] + down_shift_ref[...]).astype(BF)
-            inner = jnp.sum(
-                low_flat[lo : lo + chunk].astype(F32) * out.astype(F32), axis=1, keepdims=True
-            )
-            x_flat[lo : lo + chunk] = out
-            low_flat[lo : lo + chunk] = (
-                grad_acc[lo : lo + chunk] + inner * (1.0 - gate) * centroid_ref[...]
-            ).astype(BF)
         back_local.start()
-        for d in range(1, experts):
-            back_copy(d).start()
         out_copy.start()
         for r, p in tasks:
             if all((r, p) not in done for done in early):
@@ -795,8 +861,8 @@
         out_specs=(
             any_spec,
             any_spec,
-            once((keep, depth, blocks * lanes)),
-            once((keep * lanes, width)),
+            once((depth, hidden)),
+            once((hidden // blocks, width)),
             pl.BlockSpec(
                 (1, blocks, depth, blocks * lanes), lambda f: (jnp.maximum(f - keep, 0), 0, 0, 0)
             ),
@@ -809,8 +875,8 @@
         out_shape=(
             jax.ShapeDtypeStruct(x.shape, BF),
             jax.ShapeDtypeStruct(x.shape, BF),
-            jax.ShapeDtypeStruct((keep, depth, blocks * lanes), F32),
-            jax.ShapeDtypeStruct((keep * lanes, width), F32),
+            jax.ShapeDtypeStruct((depth, hidden), F32),
+            jax.ShapeDtypeStruct((hidden // blocks, width), F32),
             jax.ShapeDtypeStruct((rest, blocks, depth, blocks * lanes), BF),
             jax.ShapeDtypeStruct((rest, blocks, width, lanes), BF),
             jax.ShapeDtypeStruct((blocks, 1, hidden // blocks), F32),
@@ -824,6 +890,9 @@
             pltpu.VMEM((rows, width), F32),
             pltpu.VMEM((rows, width), F32),
             pltpu.VMEM((rows, 1), F32),
+            pltpu.VMEM((width, blocks * lanes), F32),
+            pltpu.VMEM((width, blocks * lanes), F32),
+            pltpu.VMEM((1, blocks * lanes), F32),
             pltpu.SemaphoreType.DMA((experts,)),
             pltpu.SemaphoreType.DMA((experts,)),
             pltpu.SemaphoreType.DMA((experts,)),
@@ -885,7 +954,7 @@
 
 
 def short_back_head(
-    query, key, value, grad_t, wide_ref, total_ref, key_ids, query_ids, key_acc, value_acc, query_out, block
+    query, key, value, grad_t, wide_ref, total_ref, key_ids, query_ids, key_acc, value_acc, block
 ):
     scale = query.shape[1] ** (-0.5)
     query = scaled(query)
@@ -894,6 +963,7 @@
     halo = extent - span
     key_acc[0:extent] = jnp.zeros((extent, key_acc.shape[1]), F32)
     value_acc[0:extent] = jnp.zeros((extent, key_acc.shape[1]), F32)
+    query_grads = []
     for i in range(span // block):
         lo, hi = i * block, (i + 1) * block
         visible = short_visible(key_ids[...], query_ids[...], i, block, halo)
@@ -908,8 +978,9 @@
         value_acc[lo : hi + halo] += dot_nn(weights.astype(BF), grad)
         key_acc[lo : hi + halo] += dot_nn(scores_low, own)
         part = dot_nn(key_t[:, lo : hi + halo], scores_low)
-        query_out[:, lo:hi] = (part * scale).astype(BF)
-    return key_acc[0:extent].T, value_acc[0:extent].T
+        query_grads.append(part * scale)
+    query_grad = jnp.concatenate(query_grads, axis=1)
+    return query_grad, key_acc[0:extent].T, value_acc[0:extent].T
 
 
 def tail_kernel(
@@ -920,11 +991,13 @@
     rest,
     back_grad,
     slot_ref,
-    normal_ref,
-    scale_ref,
+    route_ref,
+    middle_ref,
     cot_ref,
-    gain_ref,
-    attended_ref,
+    vectors,
+    centroid_ref,
+    long_attended,
+    short_attended,
     out_weight,
     long_qkv,
     long_wide,
@@ -937,15 +1010,16 @@
     produced,
     up_rest,
     down_rest,
+    up_first,
+    down_first,
     shift_ref,
-    back_out,
     long_back,
-    halo_in,
+    short_back,
     grad_middle,
+    result_ref,
     out_term,
     sums_ref,
-    query_out,
-    own_out,
+    centroid_out,
     up_sum,
     down_sum,
     shift_sum,
@@ -955,6 +1029,11 @@
     long_grad,
     back_stage,
     halo_stage,
+    halo_in,
+    own_edge,
+    back_out,
+    up_last,
+    down_last,
     shift_in,
     key_acc,
     value_acc,
@@ -969,6 +1048,7 @@
     shift_send,
     shift_recv,
     local_sem,
+    put_sem,
     *refs,
 ):
     rounds = (blocks - 1).bit_length()
@@ -982,8 +1062,35 @@
     count = slot_ref.shape[0]
     halo = halo_stage.shape[3]
     chunk = min(256, span)
+    lanes = 128
+    steps = up_sum.shape[1] // blocks // lanes
+    keep = steps - rest
+
+    def put_copies(p):
+        copies = []
+        for j in range(blocks):
+            first = (j * steps + keep + p) * lanes
+            copies.append(
+                pltpu.make_async_copy(
+                    up_last.at[p, j], up_sum.at[:, pl.ds(first, lanes)], put_sem.at[p, j]
+                )
+            )
+        copies.append(
+            pltpu.make_async_copy(
+                down_last.at[p], down_sum.at[pl.ds((keep + p) * lanes, lanes)], put_sem.at[p, blocks]
+            )
+        )
+        return copies
+
+    def put(p, up, down):
+        for j in range(blocks):
+            up_last[p, j] = up[:, j * lanes : (j + 1) * lanes]
+        down_last[p] = down
+        for copy in put_copies(p):
+            copy.start()
+
     part_copies, add_parts = line_sums(
-        z, blocks, up_held, down_held, part_send, part_recv, up_sum, down_sum
+        z, blocks, up_held, down_held, part_send, part_recv, put
     )
     line = [lax.rem(z + d, blocks) for d in range(blocks)]
 
@@ -1024,20 +1131,12 @@
             halo_stage.at[:, part], halo_in.at[:, part], halo_send.at[n], halo_recv.at[n], {"blk": left}
         )
 
-    def halo_local(n):
-        part = pl.ds(0, lead) if n == 0 else pl.ds(lead, heads - lead)
-        return pltpu.make_async_copy(halo_stage.at[:, part], halo_in.at[:, part], halo_recv.at[n])
-
     own_out_copy = pltpu.make_async_copy(produced.at[me], back_out.at[me], local_sem.at[0])
 
     def send_halo(n):
         @pl.when(z > 0)
         def _():
             halo_copy(n).start()
-
-        @pl.when(z == blocks - 1)
-        def _():
-            halo_local(n).start()
 
     @pl.when(step == 0)
     def _():
@@ -1053,32 +1152,33 @@
         flat_stage = long_stage.reshape(blocks * share, size, span)
         if spare:
             flat_stage[heads:] = jnp.zeros((spare, size, span), BF)
+            short_back[...] = jnp.zeros_like(short_back)
         slot_line = lax.broadcasted_iota(jnp.int32, (chunk, back_grad.shape[0]), 1)
-        sums = None
-        for lo in range(0, count, chunk):
-            hi = lo + chunk
-            chosen = (slot_ref[lo:hi] == slot_line).astype(F32).astype(BF)
+        sums_ref[...] = jnp.zeros_like(sums_ref)
+
+        def back_rows(turn, first, store):
+            at = pl.multiple_of(turn * chunk, chunk)
+            rows = pl.ds(pl.multiple_of(first + at, chunk), chunk)
+            chosen = (slot_ref[rows] == slot_line).astype(F32).astype(BF)
             upstream = dot_nn(chosen, back_grad[...])
-            normal = normal_ref[lo:hi]
-            inner, gain_part, bias_part = norm_back(upstream, normal, scale_ref[lo:hi], gain_ref[...])
-            middle = cot_ref[lo:hi].astype(F32) + inner
-            grad_middle[lo:hi] = middle
+            normal, scale = norm_parts(middle_ref[rows])
+            inner, gain_part, bias_part = norm_back(upstream, normal, scale, vectors[2:3])
+            middle = cot_ref[rows].astype(F32) + inner
+            grad_middle[rows] = middle
             low = middle.astype(BF)
-            grad_low[lo:hi] = low
-            part = (gain_part, bias_part, jnp.sum(middle, axis=0))
-            sums = part if sums is None else tuple(a + b for a, b in zip(sums, part))
+            grad_low[rows] = low
+            for n, part in enumerate((gain_part, bias_part, jnp.sum(middle, axis=0))):
+                sums_ref[n] += part
             grad_t = dot_nt(out_weight[...], low).astype(BF).reshape(heads, size, chunk)
-            if lo < span:
-                flat_stage[:heads, :, lo:hi] = grad_t
-            else:
-                short_grad[:, :, lo - span : hi - span] = grad_t
-            if hi == span:
-                for d in range(1, blocks):
-                    grad_copy(d).start()
-        sums_ref[...] = jnp.zeros_like(sums_ref)
-        for n, part in enumerate(sums):
-            sums_ref[n] = part
-        out_term[...] = dot_nn(attended_ref[...], grad_low[...]).astype(BF)
+            store[:heads, :, pl.ds(at, chunk)] = grad_t
+
+        pl.loop(0, span // chunk)(lambda turn: back_rows(turn, 0, flat_stage))
+        for d in range(1, blocks):
+            grad_copy(d).start()
+        pl.loop(0, span // chunk)(lambda turn: back_rows(turn, span, short_grad))
+        out_term[...] = (
+            dot_nn(long_attended[...], grad_low[:span]) + dot_nn(short_attended[...], grad_low[span:])
+        ).astype(BF)
 
     first_long = lead + 1
     is_long = (step >= first_long) & (step < first_long + share)
@@ -1098,12 +1198,15 @@
             query_ids,
             key_acc,
             value_acc,
-            query_out,
             min(SHORT, span),
         )
+        group = head // share
+        place = head - group * share
         for n, grad in enumerate(grads):
-            halo_stage[n, head] = grad[:, :halo].astype(BF)
-            own_out[n] = grad[:, halo:]
+            short_back[group, n, place] = grad[:, grad.shape[1] - span :].astype(BF)
+            if n:
+                halo_stage[n - 1, head] = grad[:, :halo].astype(BF)
+                own_edge[n - 1, head] = grad[:, span:]
 
     @pl.when(step == lead)
     def _():
@@ -1142,17 +1245,52 @@
     @pl.when(step == heads + share)
     def _():
         send_halo(1)
+        own_out_copy.wait()
+        for d in range(1, experts):
+            out_copy(d).wait_recv()
+        answers = back_out.reshape(back_grad.shape)
+        slot_line = lax.broadcasted_iota(jnp.int32, (chunk, back_grad.shape[0]), 1)
+        expert_line = lax.broadcasted_iota(jnp.int32, (chunk, 128), 1)
+        centroid_rows = jnp.concatenate(
+            [centroid_ref[...], jnp.zeros((128 - experts, width), F32)], axis=0
+        ).astype(BF)
+        centroid_out[...] = jnp.zeros_like(centroid_out)
+
+        @pl.loop(0, count // chunk)
+        def _(turn):
+            rows = pl.ds(pl.multiple_of(turn * chunk, chunk), chunk)
+            chosen = (slot_ref[rows] == slot_line).astype(F32).astype(BF)
+            answer = dot_nn(chosen, answers[...])
+            middle = middle_ref[rows]
+            normed = norm_parts(middle)[0] * vectors[2:3] + vectors[3:4]
+            named = (route_ref[rows] == expert_line).astype(F32)
+            logit = jnp.sum(
+                normed * dot_nn(named.astype(BF), centroid_rows), axis=1, keepdims=True
+            )
+            gate = 1.0 / (1.0 + jnp.exp(-logit))
+            result_ref[rows] = middle + gate * answer
+            inner = jnp.sum(cot_ref[rows].astype(F32) * answer, axis=1, keepdims=True)
+            part = lax.dot_general(
+                named,
+                inner * gate * (1.0 - gate) * normed,
+                (((0,), (0,)), ((), ())),
+                preferred_element_type=F32,
+            )
+            centroid_out[...] += part[:experts]
+
         if tasks:
             add_parts(*tasks[-1])
+        for p in range(rest):
+            for copy in put_copies(p):
+                copy.wait()
         for d in range(1, blocks):
             shift_copy(d).wait()
         total = shift_ref[z]
         for d in range(1, blocks):
             total = total + shift_in[d]
         shift_sum[...] = total
-        own_out_copy.wait()
         for d in range(1, experts):
-            out_copy(d).wait()
+            out_copy(d).wait_send()
         for d in range(1, blocks):
             grad_copy(d).wait_send()
         for head in range(share):
@@ -1173,19 +1311,24 @@
             def _(n=n):
                 halo_copy(n).wait_recv()
 
-            @pl.when(z == blocks - 1)
-            def _(n=n):
-                halo_local(n).wait()
+        @pl.when(z < blocks - 1)
+        def _():
+            for head in range(heads):
+                for n in range(2):
+                    edge = own_edge[n, head] + halo_in[n, head].astype(F32)
+                    short_back[head // share, 1 + n, head % share, :, span - halo :] = edge.astype(BF)
 
 
 def run_tail(
     back_grad,
     slot_of,
-    normal,
-    scale,
+    route_of,
+    middle,
     cot,
-    gain,
-    attended_t,
+    vectors,
+    centroids,
+    long_attended,
+    short_attended,
     out_weight,
     long_parts,
     short_parts,
@@ -1194,6 +1337,8 @@
     produced,
     up_rest,
     down_rest,
+    up_first,
+    down_first,
     shifts,
     blocks,
 ):
@@ -1208,6 +1353,7 @@
     heads = HEADS
     lead = heads // 2
     rest, _, depth, _ = up_rest.shape
+    hidden = up_first.shape[1]
     any_spec = pl.BlockSpec(memory_space=pl.ANY)
     dma = pltpu.SemaphoreType.DMA
 
@@ -1226,11 +1372,13 @@
         in_specs=[
             whole(back_grad.shape),
             whole(slot_of.shape),
-            whole(normal.shape),
-            whole(scale.shape),
+            whole(route_of.shape),
+            whole(middle.shape),
             whole(cot.shape),
-            whole(gain.shape),
-            whole(attended_t.shape),
+            whole(vectors.shape),
+            whole(centroids.shape),
+            whole(long_attended.shape),
+            whole(short_attended.shape),
             whole(out_weight.shape),
             pl.BlockSpec((3, 1, length, size), lambda f: (0, long_at(f), 0, 0)),
             pl.BlockSpec((size, length), lambda f: (long_at(f), 0)),
@@ -1243,32 +1391,32 @@
             any_spec,
             whole(up_rest.shape),
             whole(down_rest.shape),
+            any_spec,
+            any_spec,
             whole(shifts.shape),
         ],
         out_specs=(
             any_spec,
-            any_spec,
-            any_spec,
+            whole((blocks, 3, share, size, span)),
+            whole((count, width)),
             whole((count, width)),
             whole((width, width)),
             whole((8, width)),
-            pl.BlockSpec((size, span), lambda f: (short_at(f), 0)),
-            pl.BlockSpec((2, size, span), lambda f: (0, short_at(f), 0)),
-            whole((rest, depth, up_rest.shape[3])),
-            whole((rest * 128, width)),
+            whole((experts, width)),
+            any_spec,
+            any_spec,
             whole(shifts.shape[1:]),
         ),
         out_shape=(
-            jax.ShapeDtypeStruct(produced.shape, BF),
             jax.ShapeDtypeStruct((blocks, 3, share, size, span), BF),
-            jax.ShapeDtypeStruct((2, heads, size, halo), BF),
+            jax.ShapeDtypeStruct((blocks, 3, share, size, span), BF),
+            jax.ShapeDtypeStruct((count, width), F32),
             jax.ShapeDtypeStruct((count, width), F32),
             jax.ShapeDtypeStruct((width, width), BF),
             jax.ShapeDtypeStruct((8, width), F32),
-            jax.ShapeDtypeStruct((width, span), BF),
-            jax.ShapeDtypeStruct((2, width, span), F32),
-            jax.ShapeDtypeStruct((rest, depth, up_rest.shape[3]), F32),
-            jax.ShapeDtypeStruct((rest * 128, width), F32),
+            jax.ShapeDtypeStruct((experts, width), F32),
+            jax.ShapeDtypeStruct((depth, hidden), F32),
+            jax.ShapeDtypeStruct((hidden // blocks, width), F32),
             jax.ShapeDtypeStruct(shifts.shape[1:], F32),
         ),
         scratch_shapes=[
@@ -1278,6 +1426,11 @@
             pltpu.VMEM((blocks, share, size, span), BF),
             pltpu.VMEM((blocks, 3, share, size, span), BF),
             pltpu.VMEM((2, heads, size, halo), BF),
+            pltpu.VMEM((2, heads, size, halo), BF),
+            pltpu.VMEM((2, heads, size, halo), F32),
+            pltpu.VMEM(produced.shape, BF),
+            pltpu.VMEM((rest, blocks, depth, 128), F32),
+            pltpu.VMEM((rest, 128, width), F32),
             pltpu.VMEM(shifts.shape, F32),
             pltpu.VMEM((length, size), F32),
             pltpu.VMEM((length, size), F32),
@@ -1292,19 +1445,23 @@
             dma((blocks,)),
             dma((blocks,)),
             dma((1,)),
+            dma((rest, blocks + 1)),
         ]
         + sum_scratch(rest, blocks, depth, width, 1),
+        input_output_aliases={21: 7, 22: 8},
         compiler_params=pltpu.CompilerParams(
             collective_id=3, has_side_effects=True, vmem_limit_bytes=60 << 20
         ),
     )(
         back_grad,
         slot_of,
-        normal,
-        scale,
+        route_of,
+        middle,
         cot,
-        gain,
-        attended_t,
+        vectors,
+        centroids,
+        long_attended,
+        short_attended,
         out_weight,
         *long_parts,
         *short_parts,
@@ -1313,33 +1470,79 @@
         produced,
         up_rest,
         down_rest,
+        up_first,
+        down_first,
         shifts,
     )
 
 
-def reduce_kernel(experts, blocks, parts, *refs):
-    arrays = 1 + max(piece[0] for part in parts for piece in part)
-    ins, refs = refs[:arrays], refs[arrays:]
-    outs, refs = refs[:arrays], refs[arrays:]
-    number = len(parts)
+def close_kernel(
+    experts,
+    blocks,
+    out_ref,
+    long_back,
+    short_back,
+    long_tokens,
+    short_tokens,
+    vectors,
+    weights,
+    grad_middle,
+    sums_ref,
+    centroid_ref,
+    token_grad,
+    *refs,
+):
+    number = 2 + blocks // 2
+    outs, refs = refs[:number], refs[number:]
+    made, refs = (out_ref,) + refs[: number - 1], refs[number - 1 :]
     from_mate, refs = refs[:number], refs[number:]
     pair_sum, refs = refs[:number], refs[number:]
     from_chips, refs = refs[:number], refs[number:]
     group_sum, refs = refs[:number], refs[number:]
     from_line, refs = refs[:number], refs[number:]
     whole, refs = refs[:number], refs[number:]
-    mate_send, mate_recv, chip_send, chip_recv, line_send, line_recv, back_send, back_recv = refs
+    (
+        normed_t,
+        rows_ref,
+        tokens_buf,
+        back_buf,
+        load_sem,
+        mate_send,
+        mate_recv,
+        chip_send,
+        chip_recv,
+        line_send,
+        line_recv,
+        back_send,
+        back_recv,
+    ) = refs
     rounds = (blocks - 1).bit_length()
     chips = experts // 2
     me, z = lax.axis_index("expert"), lax.axis_index("blk")
     core = lax.rem(me, 2)
     chip = me // 2
     mate = me + 1 - 2 * core
+    span, width = long_tokens.shape
+    part = weights.shape[2]
+    chunk = min(256, span)
 
     def line_partner(r):
         bit = 1 << r
         return z + bit - 2 * bit * lax.rem(z // bit, 2)
 
+    loads = [
+        pltpu.make_async_copy(source, target, load_sem.at[n])
+        for n, (source, target) in enumerate(
+            (
+                (long_tokens, tokens_buf.at[0]),
+                (short_tokens, tokens_buf.at[1]),
+                (long_back, back_buf.at[0]),
+                (short_back, back_buf.at[1]),
+            )
+        )
+    ]
+    for copy in loads:
+        copy.start()
     barrier = pltpu.get_barrier_semaphore()
     pl.semaphore_signal(barrier, inc=1, device_id={"expert": mate}, device_id_type=MESH)
     for d in range(1, chips):
@@ -1351,38 +1554,17 @@
         )
     pl.semaphore_wait(barrier, chips + rounds)
 
-    def send(source, target, send_sem, recv_sem, device):
-        return pltpu.make_async_remote_copy(
-            src_ref=source,
-            dst_ref=target,
-            send_sem=send_sem,
-            recv_sem=recv_sem,
-            device_id=device,
-            device_id_type=MESH,
-        )
-
-    def mate_copies(p):
-        at = 0
-        copies = []
-        for n, (array, first, columns) in enumerate(parts[p]):
-            copies.append(
-                send(
-                    ins[array].at[:, 1 - core, :, pl.ds(first, columns)],
-                    from_mate[p].at[:, :, pl.ds(at, columns)],
-                    mate_send.at[p, n],
-                    mate_recv.at[p, n],
-                    {"expert": mate},
-                )
-            )
-            at += columns
-        return copies
+    def mate_copy(p):
+        return remote(
+            made[p].at[:, 1 - core], from_mate[p], mate_send.at[p], mate_recv.at[p], {"expert": mate}
+        )
 
     def chip_copies(p):
         copies = []
         for d in range(1, chips):
             there = lax.rem(chip + d, chips)
             copies.append(
-                send(
+                remote(
                     pair_sum[p].at[there],
                     from_chips[p].at[d - 1],
                     chip_send.at[p, d],
@@ -1403,7 +1585,7 @@
         start, groups = segment(p, r)
         half = groups // 2
         mine = lax.rem(z // (1 << r), 2)
-        return send(
+        return remote(
             group_sum[p].at[pl.ds(start + (1 - mine) * half, half)],
             from_line[p].at[r, pl.ds(0, half)],
             line_send.at[p, r],
@@ -1411,9 +1593,12 @@
             {"blk": line_partner(r)},
         )
 
-    def back_copy(p, r):
+    def back_copy(p, r, arrives):
         start, groups = segment(p, r + 1)
-        return send(
+        if arrives:
+            start, _ = segment(p, r)
+            start = start + (1 - lax.rem(z // (1 << r), 2)) * groups
+        return remote(
             whole[p].at[pl.ds(start, groups)],
             whole[p].at[pl.ds(start, groups)],
             back_send.at[p, r],
@@ -1421,34 +1606,22 @@
             {"blk": line_partner(r)},
         )
 
-    def back_arrival(p, r):
-        start, groups = segment(p, r)
-        mine = lax.rem(z // (1 << r), 2)
-        start = start + (1 - mine) * (groups // 2)
-        return send(
-            whole[p].at[pl.ds(start, groups // 2)],
-            whole[p].at[pl.ds(start, groups // 2)],
-            back_send.at[p, r],
-            back_recv.at[p, r],
-            {"blk": line_partner(r)},
-        )
+    def add_line(p, r):
+        line_copy(p, r).wait_recv()
+        start, groups = segment(p, r + 1)
+        held = group_sum[p][pl.ds(start, groups)].astype(F32)
+        group_sum[p][pl.ds(start, groups)] = (
+            held + from_line[p][r, pl.ds(0, groups)].astype(F32)
+        ).astype(BF)
 
     def run(p, stage):
         if stage == 0:
-            for copy in mate_copies(p):
-                copy.start()
+            mate_copy(p).start()
         elif stage == 1:
-            for copy in mate_copies(p):
-                copy.wait_recv()
+            mate_copy(p).wait_recv()
             for k in range(chips):
-                at = 0
-                for array, first, columns in parts[p]:
-                    own = ins[array][k, core, :, first : first + columns]
-                    came = from_mate[p][k, :, at : at + columns]
-                    pair_sum[p][k, :, at : at + columns] = (
-                        own.astype(F32) + came.astype(F32)
-                    ).astype(BF)
-                    at += columns
+                own = made[p][k, core].astype(F32)
+                pair_sum[p][k] = (own + from_mate[p][k].astype(F32)).astype(BF)
             for copy in chip_copies(p):
                 copy.start()
         elif stage == 2:
@@ -1473,67 +1646,168 @@
             add_line(p, r)
             start, groups = segment(p, rounds)
             whole[p][pl.ds(start, groups)] = group_sum[p][pl.ds(start, groups)]
-            back_copy(p, r).start()
+            back_copy(p, r, False).start()
         else:
             r = rounds - 1 - (stage - 3 - rounds)
-            back_arrival(p, r).wait_recv()
+            back_copy(p, r, True).wait_recv()
             if r:
-                back_copy(p, r - 1).start()
+                back_copy(p, r - 1, False).start()
             else:
-                at = 0
-                for array, first, columns in parts[p]:
-                    for c in range(0, columns, 128):
-                        outs[array][:, first + c : first + c + 128] = whole[p][
-                            (at + c) // 128
-                        ].astype(F32)
-                    at += columns
-
-    def add_line(p, r):
-        line_copy(p, r).wait_recv()
-        start, groups = segment(p, r + 1)
-        held = group_sum[p][pl.ds(start, groups)].astype(F32)
-        group_sum[p][pl.ds(start, groups)] = (
-            held + from_line[p][r, pl.ds(0, groups)].astype(F32)
-        ).astype(BF)
+                for c in range(0, outs[p].shape[1], 128):
+                    outs[p][:, c : c + 128] = whole[p][c // 128].astype(F32)
+
+    turns = span // chunk
+
+    def rows_of(turn):
+        at = pl.multiple_of(lax.rem(turn, turns) * chunk, chunk)
+        return turn // turns, pl.ds(at, chunk), pl.ds(pl.multiple_of(turn * chunk, chunk), chunk)
+
+    def norm_rows():
+        for copy in loads:
+            copy.wait()
+
+        @pl.loop(0, 2 * turns)
+        def _(turn):
+            half, inner, outer = rows_of(turn)
+            low = norm_low(tokens_buf[half, inner], vectors[0:1], vectors[1:2])
+            normed_t[:, outer] = low.T
+
+    def weight_part(q):
+        target = made[1 + q]
+        rows = target.shape[2]
+
+        def term(lead):
+            total = None
+            for half in range(2):
+                back = back_buf[half, 2 * q : 2 * q + 2].reshape(2 * part, span)
+                product = dot_nt(normed_t[lead, half * span : (half + 1) * span], back)
+                total = product if total is None else total + product
+            return total
+
+        if rows % 16 == 0:
+            flat = target.reshape(width, 2 * part)
+
+            @pl.loop(0, width // 256)
+            def _(turn):
+                lead = pl.ds(pl.multiple_of(turn * 256, 256), 256)
+                flat[lead] = term(lead).astype(BF)
+        else:
+            target[...] = term(slice(None)).reshape(target.shape).astype(BF)
+
+    def finish_rows():
+        rows_ref[...] = jnp.zeros_like(rows_ref)
+        ones = jnp.ones((span, 128), BF)
+        shift_total = None
+        for half in range(2):
+            shift_part = dot_nn(back_buf[half].reshape(blocks * part, span), ones)
+            shift_total = shift_part if shift_total is None else shift_total + shift_part
+
+        @pl.loop(0, 2 * turns)
+        def _(turn):
+            half, inner, outer = rows_of(turn)
+            grad_t = None
+            for n in range(blocks):
+                product = dot_nn(weights[n], back_buf[half, n, :, :, :, inner].reshape(part, chunk))
+                grad_t = product if grad_t is None else grad_t + product
+            normal, scale = norm_parts(tokens_buf[half, inner].astype(F32))
+            moved, gain_part, bias_part = norm_back(grad_t.T, normal, scale, vectors[0:1])
+            token_grad[outer] = grad_middle[outer] + moved
+            rows_ref[8 + experts] += gain_part
+            rows_ref[9 + experts] += bias_part
+
+        rows_ref[0:8] = sums_ref[...]
+        rows_ref[8 : 8 + experts] = centroid_ref[...]
+        small = rows_ref[...].T
+        lane = lax.broadcasted_iota(jnp.int32, small.shape, 1)
+        shift_total = shift_total.reshape(blocks, 3, part // 3, 128)
+        for n, kind in enumerate((0, 2)):
+            column = shift_total[:, kind].reshape(-1, 128)[:width]
+            small = jnp.where(lane == 126 + n, column, small)
+        made[number - 1][...] = small.reshape(made[number - 1].shape).astype(BF)
 
     stages = 3 + 2 * rounds
     for turn in range(number + stages - 1):
         for p in range(number):
-            if 0 <= turn - p < stages:
+            if 0 < turn - p < stages:
                 run(p, turn - p)
+        if turn < number:
+            if turn == 1:
+                norm_rows()
+            if 0 < turn < number - 1:
+                weight_part(turn - 1)
+            if turn == number - 1:
+                finish_rows()
+            run(turn, 0)
     for p in range(number):
-        for copy in mate_copies(p) + chip_copies(p):
+        for copy in [mate_copy(p)] + chip_copies(p):
             copy.wait_send()
         for r in range(rounds):
             line_copy(p, r).wait_send()
-            back_copy(p, r).wait_send()
-
-
-def reduce_all(arrays, parts, experts, blocks):
-    rows = arrays[0].shape[0] // experts
+            back_copy(p, r, False).wait_send()
+
+
+def run_close(
+    out_term,
+    long_back,
+    short_back,
+    long_tokens,
+    short_tokens,
+    vectors,
+    weights,
+    grad_middle,
+    sums,
+    centroid_term,
+    experts,
+    blocks,
+):
+    width = out_term.shape[0]
+    rows = width // experts
     chips = experts // 2
     rounds = (blocks - 1).bit_length()
-    number = len(parts)
-    widths = [sum(piece[2] for piece in part) for part in parts]
-    groups = [-(-width // 128 // blocks) * blocks for width in widths]
+    part = weights.shape[2]
+    count = grad_middle.shape[0]
+    widths = [width] + [2 * part] * (blocks // 2) + [128]
+    number = len(widths)
+    groups = [-(-w // 128 // blocks) * blocks for w in widths]
     dma = pltpu.SemaphoreType.DMA
+    vmem = pl.BlockSpec(memory_space=pltpu.VMEM)
     return pl.pallas_call(
-        functools.partial(reduce_kernel, experts, blocks, parts),
-        in_specs=[pl.BlockSpec(memory_space=pltpu.VMEM)] * len(arrays),
-        out_specs=tuple(pl.BlockSpec(memory_space=pltpu.VMEM) for _ in arrays),
-        out_shape=tuple(jax.ShapeDtypeStruct((rows, a.shape[1]), F32) for a in arrays),
-        scratch_shapes=[pltpu.VMEM((chips, rows, w), BF) for w in widths]
+        functools.partial(close_kernel, experts, blocks),
+        in_specs=[vmem] + [pl.BlockSpec(memory_space=pl.ANY)] * 4 + [vmem] * 5,
+        out_specs=(vmem,) * (1 + number),
+        out_shape=(jax.ShapeDtypeStruct((count, width), F32),)
+        + tuple(jax.ShapeDtypeStruct((rows, w), F32) for w in widths),
+        scratch_shapes=[pltpu.VMEM((chips, 2, rows, w), BF) for w in widths[1:]]
+        + [pltpu.VMEM((chips, rows, w), BF) for w in widths]
         + [pltpu.VMEM((chips, rows, w), BF) for w in widths]
         + [pltpu.VMEM((chips - 1, rows, w), BF) for w in widths]
         + [pltpu.VMEM((g, rows, 128), BF) for g in groups]
         + [pltpu.VMEM((rounds, g // 2, rows, 128), BF) for g in groups]
         + [pltpu.VMEM((g, rows, 128), BF) for g in groups]
-        + [dma((number, 3)), dma((number, 3)), dma((number, chips)), dma((number, chips))]
+        + [
+            pltpu.VMEM((width, count), BF),
+            pltpu.VMEM((128, width), F32),
+            pltpu.VMEM((2,) + long_tokens.shape, BF),
+            pltpu.VMEM((2,) + long_back.shape, BF),
+            dma((4,)),
+        ]
+        + [dma((number,)), dma((number,)), dma((number, chips)), dma((number, chips))]
         + [dma((number, rounds))] * 4,
         compiler_params=pltpu.CompilerParams(
-            collective_id=2, has_side_effects=True, vmem_limit_bytes=40 << 20
+            collective_id=2, has_side_effects=True, vmem_limit_bytes=60 << 20
         ),
-    )(*[a.reshape(chips, 2, rows, a.shape[1]) for a in arrays])
+    )(
+        out_term.reshape(chips, 2, rows, width),
+        long_back,
+        short_back,
+        long_tokens,
+        short_tokens,
+        vectors,
+        weights,
+        grad_middle,
+        sums,
+        centroid_term,
+    )
 
 
 def on_device(
@@ -1581,22 +1855,16 @@
 
     capacity = 2 * count // expert_count
     slots = expert_count * capacity
-    route_flat = routes.reshape(count)
-    onehot = route_flat[:, None] == jnp.arange(expert_count, dtype=jnp.int32)[None, :]
-    ranking = jnp.cumsum(onehot.astype(jnp.int32), axis=0) - 1
-    slot_of = route_flat * capacity + jnp.sum(jnp.where(onehot, ranking, 0), axis=1)
     slot_line = jnp.arange(slots, dtype=jnp.int32)
-
-    def to_experts(flat, slot_of):
-        to_slots = (slot_line[:, None] == slot_of[None, :]).astype(BF)
-        return dot_nn(to_slots, flat).astype(BF).reshape(expert_count, capacity, width)
-
-    sent_cot = to_experts(cotangent.reshape(count, width), slot_of)
-    slot_of = ordered(slot_of.reshape(rows, span)).reshape(count)
-    route_flat = ordered(routes.reshape(rows, span)).reshape(count)
-    onehot = route_flat[:, None] == jnp.arange(expert_count, dtype=jnp.int32)[None, :]
-    from_slots = (slot_of[:, None] == slot_line[None, :]).astype(BF)
-    grad_low = ordered(cotangent).reshape(count, width)
+    vectors = jnp.concatenate(
+        [
+            ln1_gain[None],
+            ln1_bias[None],
+            ln2_gain[None],
+            ln2_bias[None],
+            jnp.zeros((4, width), F32),
+        ]
+    )
 
     def grouped(matrix):
         lead = matrix.shape[0]
@@ -1625,9 +1893,9 @@
         out_weight,
         long_tokens,
         short_tokens,
-        sent_cot,
-        ln1_gain[None],
-        ln1_bias[None],
+        cotangent.reshape(count, width),
+        routes.reshape(1, count),
+        vectors,
         grouped(shifts[None]),
         key_ids,
         query_ids,
@@ -1636,6 +1904,7 @@
     )
     (
         received_cot,
+        slot_of,
         long_attended,
         long_qkv,
         long_wide,
@@ -1647,6 +1916,9 @@
     ) = rest
     long_attended = long_attended.reshape(-1, span)[:width]
     attended_t = jnp.concatenate([long_attended, short_low], axis=1)
+    slot_of = ordered(slot_of.reshape(rows, span)).reshape(count)
+    route_flat = ordered(routes.reshape(rows, span)).reshape(count)
+    grad_low = ordered(cotangent).reshape(count, width)
 
     middle = (
         token_rows
@@ -1655,11 +1927,9 @@
         )
         + out_bias
     )
-    normal_two, scale_two = norm_parts(middle)
-    normed_two = normal_two * ln2_gain + ln2_bias
-    outgoing = to_experts(normed_two.astype(BF), slot_of)
-    centroid_rows = jnp.dot(onehot.astype(BF), centroids, preferred_element_type=F32)
-    gate = jax.nn.sigmoid(jnp.sum(normed_two * centroid_rows, axis=1))
+    to_slots = (slot_line[:, None] == slot_of[None, :]).astype(BF)
+    expert_in = layer_norm(middle, ln2_gain, ln2_bias).astype(BF)
+    outgoing = dot_nn(to_slots, expert_in).astype(BF).reshape(expert_count, capacity, width)
 
     own_centroid = lax.dynamic_index_in_dim(
         centroids.astype(F32), lax.axis_index("expert"), 0, keepdims=True
@@ -1677,25 +1947,26 @@
     shift_parts = jnp.concatenate([up_shift, down_shift.reshape(blocks, 1, -1)], axis=2)
     shift_parts = jnp.pad(shift_parts, ((0, 0), (0, 0), (0, -shift_parts.shape[2] % 128)))
     (
-        back_out,
         long_back,
-        halo_back,
+        short_back,
         grad_middle,
+        result,
         out_term,
         tail_sums,
-        query_back,
-        own_back,
-        up_last,
-        down_last,
+        centroid_term,
+        up_sum,
+        down_sum,
         shift_sum,
     ) = run_tail(
         back_grad.reshape(slots, width),
         slot_of[:, None],
-        normal_two,
-        scale_two,
+        route_flat[:, None],
+        middle,
         grad_low,
-        ln2_gain[None],
-        attended_t,
+        vectors,
+        centroids.astype(F32),
+        long_attended,
+        short_low,
         full_out,
         (long_qkv, long_wide, long_total),
         (short_qkv, short_wide, short_total),
@@ -1704,97 +1975,42 @@
         produced,
         up_rest,
         down_rest,
+        up_first,
+        down_first,
         shift_parts,
         blocks,
     )
-    back_out = back_out.reshape(slots, width)
-    ln2_gain_term, ln2_bias_term, out_shift_term = tail_sums[0], tail_sums[1], tail_sums[2]
-    grad_out = grad_low.astype(F32)
-    up_sum = jnp.concatenate([up_first, up_last], axis=0)
-    up_sum = up_sum.reshape(-1, up_sum.shape[1], blocks, 128).transpose(1, 2, 0, 3)
-    up_sum = up_sum.reshape(up_sum.shape[0], -1)
-    down_sum = jnp.concatenate([down_first, down_last], axis=0)
-    halo_back = jnp.where(own < blocks - 1, halo_back.reshape(2, width, halo).astype(F32), 0.0)
-    own_back = own_back + jnp.pad(halo_back, ((0, 0), (0, 0), (span - halo, 0)))
-    short_back = jnp.concatenate([query_back[None], own_back.astype(BF)], axis=0)
-    short_back = jnp.pad(
-        short_back.reshape(3, heads, size, span), ((0, 0), (0, pad_heads), (0, 0), (0, 0))
-    )
-    short_back = short_back.reshape(3, blocks, share, size, span).transpose(1, 0, 2, 3, 4)
-    back_t = jnp.concatenate(
-        [long_back.reshape(-1, span), short_back.reshape(-1, span)], axis=1
-    )
-
-    normal_one, scale_one = norm_parts(token_rows)
-    normed_low = (normal_one * ln1_gain + ln1_bias).astype(BF)
-    qkv_term = lax.dot_general(
-        normed_low, back_t, (((0,), (1,)), ((), ())), preferred_element_type=F32
-    )
-    qv_sums = ungrouped(jnp.sum(back_t.astype(F32), axis=1)[None])[0]
-    grad_normed_one = lax.dot_general(
-        back_t.reshape(blocks, -1, count),
+    grad_tokens, out_sum, *qkv_sums, small_sum = run_close(
+        out_term,
+        long_back,
+        short_back,
+        long_tokens,
+        short_tokens,
+        vectors,
         full_qkv,
-        (((0, 1), (0, 2)), ((), ())),
-        preferred_element_type=F32,
-    )
-    inner_one, ln1_gain_term, ln1_bias_term = norm_back(
-        grad_normed_one, normal_one, scale_one, ln1_gain
-    )
-    grad_tokens = grad_middle + inner_one
-
-    expert_rows = dot_nn(from_slots, back_out)
-    result = middle + gate[:, None] * expert_rows
-    grad_logit = jnp.sum(grad_out * expert_rows, axis=1) * gate * (1.0 - gate)
-    centroid_term = jnp.einsum(
-        "te,td->de",
-        onehot.astype(F32) * grad_logit[:, None],
-        normed_two,
-        precision=lax.Precision.HIGHEST,
-    )
-
-    small = jnp.stack(
-        [
-            qv_sums[0],
-            qv_sums[2],
-            out_shift_term,
-            ln1_gain_term,
-            ln1_bias_term,
-            ln2_gain_term,
-            ln2_bias_term,
-        ],
-        axis=1,
-    )
-    n_small = small.shape[1]
-    small = jnp.concatenate([small, centroid_term], axis=1)
-    small = jnp.pad(small, ((0, 0), (0, 128 - small.shape[1])))
-    columns = qkv_term.shape[1]
-    half = -(-columns // 256) * 128
-    qkv_sum, out_sum, small_sum = reduce_all(
-        (qkv_term.astype(BF), out_term, small.astype(BF)),
-        (
-            ((1, 0, width), (2, 0, 128)),
-            ((0, 0, half),),
-            ((0, half, columns - half),),
-        ),
+        grad_middle,
+        tail_sums,
+        centroid_term,
         expert_count,
         blocks,
     )
-    centroid_sum = small_sum[:, n_small : n_small + expert_count].T
+    qkv_sum = jnp.concatenate(qkv_sums, axis=1)
+    norm_at = 8 + expert_count
     shift_cut = up_bias.shape[1] // blocks
     up_shift_sum = shift_sum[:, :shift_cut]
     down_shift_sum = shift_sum[:, shift_cut : shift_cut + width // blocks]
     return (
         ordered(result.reshape(rows, span, width)),
         ordered(grad_tokens.reshape(rows, span, width)),
-        small_sum[:, 3],
-        small_sum[:, 4],
+        small_sum[:, norm_at],
+        small_sum[:, norm_at + 1],
         ungrouped(qkv_sum).reshape(-1, 3 * width),
-        small_sum[:, :2].T,
+        small_sum[:, 126:].T,
         out_sum,
         small_sum[:, 2],
-        small_sum[:, 5],
-        small_sum[:, 6],
-        centroid_sum,
+        small_sum[:, 0],
+        small_sum[:, 1],
+        small_sum[:, 8:norm_at].T,
         up_sum[None],
         up_shift_sum,
         down_sum[None],

time: 566 us -> 551 us (0.973)
  Pallas kernels: 457 us -> 487 us
  matrix products: 39 us -> 9.46 us
  other arithmetic: 28.3 us -> 11.7 us
    dot_general x4 -> x0, matrix products: 17.7 us -> none  [the longest x1 8.06 us: on_device(): lax.dot_general(back_t.reshape(blocks, -1, count), full_qkv, (((0, 1), (0...]
    pallas_call x1, Pallas kernels: 61.4 us -> 76.1 us  [run_close(): pl.pallas_call(functools.partial(close_kernel, experts, blocks), in_specs...]
    pallas_call x1, Pallas kernels: 135 us -> 149 us  [run_tail(): pl.pallas_call(functools.partial(tail_kernel, experts, blocks, heads, lea...]
    dot_general x3 -> x1, matrix products: 17.9 us -> 6.1 us  [dot_nn(): lax.dot_general(a, b, (((1,), (0,)), ((), ())), preferred_element_type=F32)]
    reshape x2 -> x1, local copies, waits for them, and re-layouts: 6.6 us -> 0.01 us  [on_device(): slot_of = ordered(slot_of.reshape(rows, span)).reshape(count)]
    unnamed x76 -> x38, local copies, waits for them, and re-layouts: 8.88 us -> 11.6 us
where the time goes in v5:
time: 551 us; the launch traced here: 547 us
  Pallas kernels  487 us (88%)
  local copies, waits for them, and re-layouts  36.3 us (7%)
  other arithmetic  11.7 us (2%)
  matrix products  9.46 us (2%)
    pallas_call x1, Pallas kernels, run_expert(): pl.pallas_call(functools.partial(expert_kernel, experts, blocks, steps, r...  164 us
    pallas_call x1, Pallas kernels, run_tail(): pl.pallas_call(functools.partial(tail_kernel, experts, blocks, heads, lea...  149 us
    pallas_call x1, Pallas kernels, run_front(): pl.pallas_call(functools.partial(front_kernel, experts, blocks, HEADS, ga...  98.7 us
    pallas_call x1, Pallas kernels, run_close(): pl.pallas_call(functools.partial(close_kernel, experts, blocks), in_specs...  76.1 us
    unnamed x38, local copies, waits for them, and re-layouts  11.6 us

profile of v5, /device:TPU:0, one launch (start us, length us, event | category | flops | bytes accessed | tf_op | source)
XLA Modules:
  0.0 546.7 jit_solution(3237403802691156581)
XLA Ops:
  0.7 1.3 slice.39
  11.9 1.0 copy.59
  13.0 1.4 copy.39
  14.4 1.0 copy.42.qkv_ref
  15.5 2.6 dynamic-slice_bitcast_fusion
  18.2 1.3 pad_maximum_fusion.2
  19.5 98.7 %shard_map.280 = (bf16[4,768,576]{2,1,0:T(8,128)(2,1)}, bf16[8,96,768]{2,1,0:T(8,128)(2,1)}, bf16[8,256,768]{2,1,0:T(8,128)(2,1)}, s32[1,1024]{1,0:T(1,128)}, bf...) custom-call(bf16[4,96,576]{2,1,0:T(8,128)(2,1)} %copy.42.qkv_ref, ...), custom_call_target="tpu_custom_call" | custom-call | tf_op jit(solution)/shard_map/pallas_call | solution.py:483
  118.6 1.3 reduce.18
  120.1 1.0 copy.57
  121.1 3.4 fusion.16
  125.3 6.1 %fusion.2 = bf16[2048,768]{1,0:T(8,128)(2,1)} fusion(s32[1024]{0:T(1024)S(1)} %bitcast.79, f32[1024,768]{1,0:T(8,128)S(1)} %get-tuple-element.137.middle_ref, f32[768]{0:T(1024)S(1)} %copy-done.10, f32[768]{0:T(1024)S(1)} %copy-done.9, f32[1024]{0:T(1024)S(1)} %add_rsqrt_fusion, f32[1024]{0:T(1024)S(1)} %broadcast_multiply_fusion), kind=kOutput, calls=%fused_computation.3 | convolution fusion | flops 3228827648 | bytes 6309888 | tf_op jit(solution)/shard_map/dot_general | solution.py:19
  131.4 163.5 %shard_map.281 = (bf16[8,256,768]{2,1,0:T(8,128)(2,1)}, bf16[8,256,768]{2,1,0:T(8,128)(2,1)}, f32[192,3072]{1,0:T(8,128)}, f32[768,768]{1,0:T(8,128)}, bf16[2,4,...) custom-call(bf16[8,256,768]{2,1,0:T(8,128)(2,1)} %bitcast.88, ...), custom_call_target="tpu_custom_call" | custom-call | flops 57982058496 | bytes 41943040 | tf_op jit(solution)/shard_map/pallas_call | solution.py:853
  295.7 1.3 fusion.10.shift_ref
  297.0 149.2 %shard_map.282 = (bf16[4,3,3,64,512]{4,3,2,1,0:T(8,128)(2,1)}, bf16[4,3,3,64,512]{4,3,2,1,0:T(8,128)(2,1)}, f32[1024,768]{1,0:T(8,128)}, f32[1024,768]{1,0:T(8,1...) custom-call(bf16[2048,768]{1,0:T(8,128)(2,1)} %bitcast.60, ...), custom_call_target="tpu_custom_call", output_to_operand_aliasing={{7}: (21, {}), {8}: (22, {})} | custom-call | tf_op jit(solution)/shard_map/pallas_call | solution.py:1369
  446.2 76.1 %shard_map.283 = (f32[1024,768]{1,0:T(8,128)}, f32[96,768]{1,0:T(8,128)}, f32[96,1152]{1,0:T(8,128)}, f32[96,1152]{1,0:T(8,128)}, f32[96,128]{1,0:T(8,128)}) custom-call(bf16[4,2,96,768]{3,2,1,0:T(8,128)(2,1)} %bitcast.69, bf16[4,3,3,64,512]{4,3,2,1,0:T(8,128)(2,1)} %get-tuple-element.71.long_back, bf16[4,3,3,64,512]{4,3,2,1,0:T(8,128)(2,1)} %get-tuple-element.72.short_back, ...), custom_call_target="tpu_custom_call" | custom-call | tf_op jit(solution)/shard_map/pallas_call | solution.py:1774
  522.3 3.4 constant_dynamic-slice_fusion.1
  525.8 1.9 pad_maximum_fusion.1
  531.0 2.1 pad_maximum_fusion.3
  533.2 2.6 copy.49
  535.7 2.4 copy.50
  538.1 2.5 copy.51
  540.7 1.9 pad_maximum_fusion
  543.7 1.4 copy.66
  545.1 1.4 copy.67
  (68 shorter events, 16.1 us)
Async XLA Ops:
  10.4 7.7 %copy-start.8 = (f32[8,768]{1,0:T(8,128)}, f32[8,768]{1,0:T(8,128)S(1)}, u32[]{:S(2)}) copy-start(f32[8,768]{1,0:T(8,128)S(1)} %convert_element_type.27.centroid_ref) | copy-start | bytes 73732
  13.0 5.1 copy-start.5
  19.5 101.6 %copy-start.3 = (bf16[512,768]{1,0:T(8,128)(2,1)S(1)}, bf16[512,768]{1,0:T(8,128)(2,1)}, u32[]{:S(2)}) copy-start(bf16[512,768]{1,0:T(8,128)(2,1)} %get-tuple-element.128.short_ref.short_tokens) | copy-start | bytes 2359300
  19.5 101.6 %copy-start.4 = (bf16[512,768]{1,0:T(8,128)(2,1)S(1)}, bf16[512,768]{1,0:T(8,128)(2,1)}, u32[]{:S(2)}) copy-start(bf16[512,768]{1,0:T(8,128)(2,1)} %get-tuple-element.129.row_ref.long_tokens) | copy-start | bytes 2359300
  19.5 101.6 %copy-start.12 = (f32[768]{0:T(1024)S(1)}, f32[768]{0:T(1024)}, u32[]{:S(2)}) copy-start(f32[768]{0:T(1024)} %param.25) | copy-start | bytes 9220
  124.5 6.9 %copy-start = (f32[1024,768]{1,0:T(8,128)}, f32[1024,768]{1,0:T(8,128)S(1)}, u32[]{:S(2)}) copy-start(f32[1024,768]{1,0:T(8,128)S(1)} %get-tuple-element.137.middle_ref) | copy-start | bytes 9437188
  124.5 0.7 copy-start.9
  124.5 0.8 copy-start.10
  525.7 1.9 copy-start.11
  525.8 3.0 copy-start.6
  540.7 1.9 copy-start.7
  540.7 3.0 copy-start.1
  542.5 2.5 copy-start.2

commit v6 on v5

--- a/solution.py
+++ b/solution.py
@@ -586,6 +586,38 @@
                 copy.start()
 
     return part_copies, add_parts
+
+
+def late_sums(up_last, down_last, up_sum, down_sum, put_sem, first_part, steps):
+    lanes = down_last.shape[1]
+    blocks = up_last.shape[1]
+
+    def put_copies(p):
+        copies = []
+        for j in range(blocks):
+            first = (j * steps + first_part + p) * lanes
+            copies.append(
+                pltpu.make_async_copy(
+                    up_last.at[p, j], up_sum.at[:, pl.ds(first, lanes)], put_sem.at[p, j]
+                )
+            )
+        copies.append(
+            pltpu.make_async_copy(
+                down_last.at[p],
+                down_sum.at[pl.ds((first_part + p) * lanes, lanes)],
+                put_sem.at[p, blocks],
+            )
+        )
+        return copies
+
+    def put(p, up, down):
+        for j in range(blocks):
+            up_last[p, j] = up[:, j * lanes : (j + 1) * lanes]
+        down_last[p] = down
+        for copy in put_copies(p):
+            copy.start()
+
+    return put, put_copies
 
 
 def sum_scratch(parts, blocks, depth, width, first):
@@ -1062,33 +1094,9 @@
     count = slot_ref.shape[0]
     halo = halo_stage.shape[3]
     chunk = min(256, span)
-    lanes = 128
-    steps = up_sum.shape[1] // blocks // lanes
-    keep = steps - rest
-
-    def put_copies(p):
-        copies = []
-        for j in range(blocks):
-            first = (j * steps + keep + p) * lanes
-            copies.append(
-                pltpu.make_async_copy(
-                    up_last.at[p, j], up_sum.at[:, pl.ds(first, lanes)], put_sem.at[p, j]
-                )
-            )
-        copies.append(
-            pltpu.make_async_copy(
-                down_last.at[p], down_sum.at[pl.ds((keep + p) * lanes, lanes)], put_sem.at[p, blocks]
-            )
-        )
-        return copies
-
-    def put(p, up, down):
-        for j in range(blocks):
-            up_last[p, j] = up[:, j * lanes : (j + 1) * lanes]
-        down_last[p] = down
-        for copy in put_copies(p):
-            copy.start()
-
+    steps = up_sum.shape[1] // blocks // 128
+    keep = steps - up_rest.shape[0]
+    put, put_copies = late_sums(up_last, down_last, up_sum, down_sum, put_sem, keep, steps)
     part_copies, add_parts = line_sums(
         z, blocks, up_held, down_held, part_send, part_recv, put
     )
@@ -1124,8 +1132,10 @@
             shift_ref.at[line[d]], shift_in.at[d], shift_send.at[d], shift_recv.at[d], {"blk": line[d]}
         )
 
+    halo_parts = [part for part in ((0, lead), (lead, heads - lead)) if part[1]]
+
     def halo_copy(n):
-        part = pl.ds(0, lead) if n == 0 else pl.ds(lead, heads - lead)
+        part = pl.ds(*halo_parts[n])
         left = lax.rem(z + blocks - 1, blocks)
         return remote(
             halo_stage.at[:, part], halo_in.at[:, part], halo_send.at[n], halo_recv.at[n], {"blk": left}
@@ -1244,7 +1254,8 @@
 
     @pl.when(step == heads + share)
     def _():
-        send_halo(1)
+        if len(halo_parts) > 1:
+            send_halo(1)
         own_out_copy.wait()
         for d in range(1, experts):
             out_copy(d).wait_recv()
@@ -1301,7 +1312,7 @@
             for r in range(rounds):
                 for copy in part_copies(r, p):
                     copy.wait_send()
-        for n in range(2):
+        for n in range(len(halo_parts)):
 
             @pl.when(z > 0)
             def _(n=n):
@@ -1317,6 +1328,10 @@
                 for n in range(2):
                     edge = own_edge[n, head] + halo_in[n, head].astype(F32)
                     short_back[head // share, 1 + n, head % share, :, span - halo :] = edge.astype(BF)
+
+
+def tail_share(rest):
+    return (rest + 1) // 2
 
 
 def run_tail(
@@ -1352,7 +1367,8 @@
     halo = extent - span
     heads = HEADS
     lead = heads // 2
-    rest, _, depth, _ = up_rest.shape
+    depth = up_rest.shape[2]
+    rest = tail_share(up_rest.shape[0])
     hidden = up_first.shape[1]
     any_spec = pl.BlockSpec(memory_space=pl.ANY)
     dma = pltpu.SemaphoreType.DMA
@@ -1489,7 +1505,13 @@
     grad_middle,
     sums_ref,
     centroid_ref,
+    up_rest,
+    down_rest,
+    up_first,
+    down_first,
     token_grad,
+    up_sum,
+    down_sum,
     *refs,
 ):
     number = 2 + blocks // 2
@@ -1515,8 +1537,26 @@
         line_recv,
         back_send,
         back_recv,
+        *refs,
     ) = refs
     rounds = (blocks - 1).bit_length()
+    done = tail_share(up_rest.shape[0])
+    late = up_rest.shape[0] - done
+    if late:
+        (up_last, down_last, put_sem), refs = refs[:3], refs[3:]
+        steps = up_sum.shape[1] // blocks // 128
+        put, put_copies = late_sums(
+            up_last, down_last, up_sum, down_sum, put_sem, steps - late, steps
+        )
+        part_copies, add_parts = line_sums(
+            lax.axis_index("blk"),
+            blocks,
+            (up_rest.at[pl.ds(done, late)],) + tuple(refs[:rounds]),
+            (down_rest.at[pl.ds(done, late)],) + tuple(refs[rounds : 2 * rounds]),
+            refs[2 * rounds],
+            refs[2 * rounds + 1],
+            put,
+        )
     chips = experts // 2
     me, z = lax.axis_index("expert"), lax.axis_index("blk")
     core = lax.rem(me, 2)
@@ -1725,6 +1765,9 @@
             small = jnp.where(lane == 126 + n, column, small)
         made[number - 1][...] = small.reshape(made[number - 1].shape).astype(BF)
 
+    for p in range(late):
+        for copy in part_copies(0, p):
+            copy.start()
     stages = 3 + 2 * rounds
     for turn in range(number + stages - 1):
         for p in range(number):
@@ -1738,12 +1781,22 @@
             if turn == number - 1:
                 finish_rows()
             run(turn, 0)
+        for r in range(rounds):
+            if turn == 2 + 2 * r:
+                for p in range(late):
+                    add_parts(r, p)
     for p in range(number):
         for copy in [mate_copy(p)] + chip_copies(p):
             copy.wait_send()
         for r in range(rounds):
             line_copy(p, r).wait_send()
             back_copy(p, r, False).wait_send()
+    for p in range(late):
+        for copy in put_copies(p):
+            copy.wait()
+        for r in range(rounds):
+            for copy in part_copies(r, p):
+                copy.wait_send()
 
 
 def run_close(
@@ -1757,6 +1810,10 @@
     grad_middle,
     sums,
     centroid_term,
+    up_rest,
+    down_rest,
+    up_first,
+    down_first,
     experts,
     blocks,
 ):
@@ -1771,11 +1828,25 @@
     groups = [-(-w // 128 // blocks) * blocks for w in widths]
     dma = pltpu.SemaphoreType.DMA
     vmem = pl.BlockSpec(memory_space=pltpu.VMEM)
+    any_spec = pl.BlockSpec(memory_space=pl.ANY)
+    late = up_rest.shape[0] - tail_share(up_rest.shape[0])
+    depth = up_rest.shape[2]
+    late_scratch = []
+    if late:
+        late_scratch = [
+            pltpu.VMEM((late, blocks, depth, 128), F32),
+            pltpu.VMEM((late, 128, width), F32),
+            dma((late, blocks + 1)),
+        ] + sum_scratch(late, blocks, depth, width, 1)
     return pl.pallas_call(
         functools.partial(close_kernel, experts, blocks),
-        in_specs=[vmem] + [pl.BlockSpec(memory_space=pl.ANY)] * 4 + [vmem] * 5,
-        out_specs=(vmem,) * (1 + number),
-        out_shape=(jax.ShapeDtypeStruct((count, width), F32),)
+        in_specs=[vmem] + [any_spec] * 4 + [vmem] * 7 + [any_spec] * 2,
+        out_specs=(vmem, any_spec, any_spec) + (vmem,) * number,
+        out_shape=(
+            jax.ShapeDtypeStruct((count, width), F32),
+            jax.ShapeDtypeStruct(up_first.shape, F32),
+            jax.ShapeDtypeStruct(down_first.shape, F32),
+        )
         + tuple(jax.ShapeDtypeStruct((rows, w), F32) for w in widths),
         scratch_shapes=[pltpu.VMEM((chips, 2, rows, w), BF) for w in widths[1:]]
         + [pltpu.VMEM((chips, rows, w), BF) for w in widths]
@@ -1792,7 +1863,9 @@
             dma((4,)),
         ]
         + [dma((number,)), dma((number,)), dma((number, chips)), dma((number, chips))]
-        + [dma((number, rounds))] * 4,
+        + [dma((number, rounds))] * 4
+        + late_scratch,
+        input_output_aliases={12: 1, 13: 2},
         compiler_params=pltpu.CompilerParams(
             collective_id=2, has_side_effects=True, vmem_limit_bytes=60 << 20
         ),
@@ -1807,6 +1880,10 @@
         grad_middle,
         sums,
         centroid_term,
+        up_rest,
+        down_rest,
+        up_first,
+        down_first,
     )
 
 
@@ -1980,7 +2057,7 @@
         shift_parts,
         blocks,
     )
-    grad_tokens, out_sum, *qkv_sums, small_sum = run_close(
+    grad_tokens, up_sum, down_sum, out_sum, *qkv_sums, small_sum = run_close(
         out_term,
         long_back,
         short_back,
@@ -1991,6 +2068,10 @@
         grad_middle,
         tail_sums,
         centroid_term,
+        up_rest,
+        down_rest,
+        up_sum,
+        down_sum,
         expert_count,
         blocks,
     )

time: 551 us -> 538 us (0.976)
  Pallas kernels: 487 us -> 474 us
    pallas_call x1, Pallas kernels: 149 us -> 127 us  [run_tail(): pl.pallas_call(functools.partial(tail_kernel, experts, blocks, heads, lea...]
    pallas_call x1, Pallas kernels: 76.1 us -> 85.3 us  [run_close(): pl.pallas_call(functools.partial(close_kernel, experts, blocks), in_specs...]
where the time goes in v6:
time: 538 us; the launch traced here: 533 us
  Pallas kernels  474 us (88%)
  local copies, waits for them, and re-layouts  36.3 us (7%)
  other arithmetic  11.7 us (2%)
  matrix products  9.46 us (2%)
    pallas_call x1, Pallas kernels, run_expert(): pl.pallas_call(functools.partial(expert_kernel, experts, blocks, steps, r...  164 us
    pallas_call x1, Pallas kernels, run_tail(): pl.pallas_call(functools.partial(tail_kernel, experts, blocks, heads, lea...  127 us
    pallas_call x1, Pallas kernels, run_front(): pl.pallas_call(functools.partial(front_kernel, experts, blocks, HEADS, ga...  98.6 us
    pallas_call x1, Pallas kernels, run_close(): pl.pallas_call(functools.partial(close_kernel, experts, blocks), in_specs...  85.3 us
    unnamed x38, local copies, waits for them, and re-layouts  11.6 us

profile of v6, /device:TPU:0, one launch (start us, length us, event | category | flops | bytes accessed | tf_op | source)
XLA Modules:
  0.0 533.2 jit_solution(7948494162447291305)
XLA Ops:
  0.7 1.3 slice.39
  11.9 1.0 copy.61
  13.0 1.4 copy.41
  14.4 1.0 copy.44.qkv_ref
  15.5 2.6 dynamic-slice_bitcast_fusion
  18.2 1.3 pad_maximum_fusion.2
  19.5 98.6 %shard_map.280 = (bf16[4,768,576]{2,1,0:T(8,128)(2,1)}, bf16[8,96,768]{2,1,0:T(8,128)(2,1)}, bf16[8,256,768]{2,1,0:T(8,128)(2,1)}, s32[1,1024]{1,0:T(1,128)}, bf...) custom-call(bf16[4,96,576]{2,1,0:T(8,128)(2,1)} %copy.44.qkv_ref, ...), custom_call_target="tpu_custom_call" | custom-call | tf_op jit(solution)/shard_map/pallas_call | solution.py:483
  118.6 1.3 reduce.18
  120.1 1.0 copy.59
  121.1 3.4 fusion.16
  125.2 6.1 %fusion.2 = bf16[2048,768]{1,0:T(8,128)(2,1)} fusion(s32[1024]{0:T(1024)S(1)} %bitcast.79, f32[1024,768]{1,0:T(8,128)S(1)} %get-tuple-element.141.middle_ref, f32[768]{0:T(1024)S(1)} %copy-done.10, f32[768]{0:T(1024)S(1)} %copy-done.9, f32[1024]{0:T(1024)S(1)} %add_rsqrt_fusion, f32[1024]{0:T(1024)S(1)} %broadcast_multiply_fusion), kind=kOutput, calls=%fused_computation.3 | convolution fusion | flops 3228827648 | bytes 6309888 | tf_op jit(solution)/shard_map/dot_general | solution.py:19
  131.4 163.5 %shard_map.281 = (bf16[8,256,768]{2,1,0:T(8,128)(2,1)}, bf16[8,256,768]{2,1,0:T(8,128)(2,1)}, f32[192,3072]{1,0:T(8,128)}, f32[768,768]{1,0:T(8,128)}, bf16[2,4,...) custom-call(bf16[8,256,768]{2,1,0:T(8,128)(2,1)} %bitcast.88, ...), custom_call_target="tpu_custom_call" | custom-call | flops 57982058496 | bytes 41943040 | tf_op jit(solution)/shard_map/pallas_call | solution.py:885
  295.7 1.3 fusion.10.shift_ref
  297.0 126.6 %shard_map.282 = (bf16[4,3,3,64,512]{4,3,2,1,0:T(8,128)(2,1)}, bf16[4,3,3,64,512]{4,3,2,1,0:T(8,128)(2,1)}, f32[1024,768]{1,0:T(8,128)}, f32[1024,768]{1,0:T(8,1...) custom-call(bf16[2048,768]{1,0:T(8,128)(2,1)} %bitcast.60, ...), custom_call_target="tpu_custom_call", output_to_operand_aliasing={{7}: (21, {}), {8}: (22, {})} | custom-call | tf_op jit(solution)/shard_map/pallas_call | solution.py:1385
  423.6 85.3 %shard_map.283 = (f32[1024,768]{1,0:T(8,128)}, f32[192,3072]{1,0:T(8,128)}, f32[768,768]{1,0:T(8,128)}, f32[96,768]{1,0:T(8,128)}, f32[96,1152]{1,0:T(8,128)}, /*index=5*/f32[96,1152]{1,0:T(8,128)}, f32[96,128]{1,0:T(8,128)}) custom-call(bf16[4,2,96,768]{3,2,1,0:T(8,128)(2,1)} %bitcast.69, ...), custom_call_target="tpu_custom_call", output_to_operand_aliasing={{1}: (12, {}), {2}: (13, {})} | custom-call | tf_op jit(solution)/shard_map/pallas_call | solution.py:1841
  508.8 3.4 constant_dynamic-slice_fusion.1
  512.3 1.9 pad_maximum_fusion.1
  517.6 2.1 pad_maximum_fusion.3
  519.7 2.6 copy.51
  522.2 2.4 copy.52
  524.7 2.5 copy.53
  527.2 1.9 pad_maximum_fusion
  530.2 1.4 copy.70
  531.6 1.4 copy.71
  (68 shorter events, 16.1 us)
Async XLA Ops:
  10.4 7.7 %copy-start.8 = (f32[8,768]{1,0:T(8,128)}, f32[8,768]{1,0:T(8,128)S(1)}, u32[]{:S(2)}) copy-start(f32[8,768]{1,0:T(8,128)S(1)} %convert_element_type.27.centroid_ref) | copy-start | bytes 73732
  13.0 5.1 copy-start.5
  19.5 101.6 %copy-start.3 = (bf16[512,768]{1,0:T(8,128)(2,1)S(1)}, bf16[512,768]{1,0:T(8,128)(2,1)}, u32[]{:S(2)}) copy-start(bf16[512,768]{1,0:T(8,128)(2,1)} %get-tuple-element.132.short_ref.short_tokens) | copy-start | bytes 2359300
  19.5 101.6 %copy-start.4 = (bf16[512,768]{1,0:T(8,128)(2,1)S(1)}, bf16[512,768]{1,0:T(8,128)(2,1)}, u32[]{:S(2)}) copy-start(bf16[512,768]{1,0:T(8,128)(2,1)} %get-tuple-element.133.row_ref.long_tokens) | copy-start | bytes 2359300
  19.5 101.6 %copy-start.12 = (f32[768]{0:T(1024)S(1)}, f32[768]{0:T(1024)}, u32[]{:S(2)}) copy-start(f32[768]{0:T(1024)} %param.25) | copy-start | bytes 9220
  124.5 6.9 %copy-start.2 = (f32[1024,768]{1,0:T(8,128)}, f32[1024,768]{1,0:T(8,128)S(1)}, u32[]{:S(2)}) copy-start(f32[1024,768]{1,0:T(8,128)S(1)} %get-tuple-element.141.middle_ref) | copy-start | bytes 9437188
  124.5 0.7 copy-start.9
  124.5 0.8 copy-start.10
  512.3 1.9 copy-start.11
  512.3 3.0 copy-start.6
  527.2 1.9 copy-start.7
  527.2 3.0 copy-start
  529.1 2.5 copy-start.1

commit v7 on v6

--- a/solution.py
+++ b/solution.py
@@ -1950,11 +1950,6 @@
         split = split.reshape(lead, 3, blocks, share, size).transpose(2, 0, 1, 3, 4)
         return split.reshape(blocks, lead, 3 * share * size)
 
-    def ungrouped(matrix):
-        lead = matrix.shape[0]
-        split = matrix.reshape(lead, blocks, 3, share, size).transpose(0, 2, 1, 3, 4)
-        return split.reshape(lead, 3, blocks * share, size)[:, :, :heads].reshape(lead, 3, width)
-
     short_ids = jnp.concatenate(
         [
             jnp.full((halo,), -1, jnp.int32),
@@ -2075,7 +2070,15 @@
         expert_count,
         blocks,
     )
-    qkv_sum = jnp.concatenate(qkv_sums, axis=1)
+    group_columns = share * size
+    pieces = []
+    for kind in range(3):
+        for n in range(blocks):
+            kept = min(group_columns, width - n * group_columns)
+            if kept > 0:
+                first = (n % 2 * 3 + kind) * group_columns
+                pieces.append(qkv_sums[n // 2][:, first : first + kept])
+    qkv_sum = jnp.concatenate(pieces, axis=1)
     norm_at = 8 + expert_count
     shift_cut = up_bias.shape[1] // blocks
     up_shift_sum = shift_sum[:, :shift_cut]
@@ -2085,7 +2088,7 @@
         ordered(grad_tokens.reshape(rows, span, width)),
         small_sum[:, norm_at],
         small_sum[:, norm_at + 1],
-        ungrouped(qkv_sum).reshape(-1, 3 * width),
+        qkv_sum,
         small_sum[:, 126:].T,
         out_sum,
         small_sum[:, 2],

time: 538 us -> 533 us (level)
    unnamed x38 -> x37, local copies, waits for them, and re-layouts: 11.6 us -> 9.05 us
where the time goes in v7:
time: 533 us; the launch traced here: 528 us
  Pallas kernels  474 us (89%)
  local copies, waits for them, and re-layouts  33.6 us (6%)
  other arithmetic  9.61 us (2%)
  matrix products  9.46 us (2%)
    pallas_call x1, Pallas kernels, run_expert(): pl.pallas_call(functools.partial(expert_kernel, experts, blocks, steps, r...  164 us
    pallas_call x1, Pallas kernels, run_tail(): pl.pallas_call(functools.partial(tail_kernel, experts, blocks, heads, lea...  127 us
    pallas_call x1, Pallas kernels, run_front(): pl.pallas_call(functools.partial(front_kernel, experts, blocks, HEADS, ga...  98.6 us
    pallas_call x1, Pallas kernels, run_close(): pl.pallas_call(functools.partial(close_kernel, experts, blocks), in_specs...  85.3 us

profile of v7, /device:TPU:0, one launch (start us, length us, event | category | flops | bytes accessed | tf_op | source)
XLA Modules:
  0.0 528.4 jit_solution(13452096217399307275)
XLA Ops:
  0.7 1.3 slice.75
  11.0 0.9 broadcast_in_dim.47.key_ids
  11.9 1.0 copy.57
  13.0 1.4 copy.40
  14.4 1.0 copy.43.qkv_ref
  15.5 2.6 dynamic-slice_bitcast_fusion
  18.2 1.3 pad_maximum_fusion.2
  19.5 98.6 %shard_map.280 = (bf16[4,768,576]{2,1,0:T(8,128)(2,1)}, bf16[8,96,768]{2,1,0:T(8,128)(2,1)}, bf16[8,256,768]{2,1,0:T(8,128)(2,1)}, s32[1,1024]{1,0:T(1,128)}, bf...) custom-call(bf16[4,96,576]{2,1,0:T(8,128)(2,1)} %copy.43.qkv_ref, ...), custom_call_target="tpu_custom_call" | custom-call | tf_op jit(solution)/shard_map/pallas_call | solution.py:483
  118.6 1.3 reduce.18
  120.1 1.0 copy.55
  121.1 3.4 fusion.18
  125.2 6.1 %fusion.2 = bf16[2048,768]{1,0:T(8,128)(2,1)} fusion(s32[1024]{0:T(1024)S(1)} %bitcast.73, f32[1024,768]{1,0:T(8,128)S(1)} %get-tuple-element.153.middle_ref, f32[768]{0:T(1024)S(1)} %copy-done.10, f32[768]{0:T(1024)S(1)} %copy-done.9, f32[1024]{0:T(1024)S(1)} %add_rsqrt_fusion, f32[1024]{0:T(1024)S(1)} %broadcast_multiply_fusion), kind=kOutput, calls=%fused_computation.3 | convolution fusion | flops 3228827648 | bytes 6309888 | tf_op jit(solution)/shard_map/dot_general | solution.py:19
  131.4 163.5 %shard_map.281 = (bf16[8,256,768]{2,1,0:T(8,128)(2,1)}, bf16[8,256,768]{2,1,0:T(8,128)(2,1)}, f32[192,3072]{1,0:T(8,128)}, f32[768,768]{1,0:T(8,128)}, bf16[2,4,...) custom-call(bf16[8,256,768]{2,1,0:T(8,128)(2,1)} %bitcast.82, ...), custom_call_target="tpu_custom_call" | custom-call | flops 57982058496 | bytes 41943040 | tf_op jit(solution)/shard_map/pallas_call | solution.py:885
  295.7 1.3 fusion.10.shift_ref
  297.0 126.6 %shard_map.282 = (bf16[4,3,3,64,512]{4,3,2,1,0:T(8,128)(2,1)}, bf16[4,3,3,64,512]{4,3,2,1,0:T(8,128)(2,1)}, f32[1024,768]{1,0:T(8,128)}, f32[1024,768]{1,0:T(8,1...) custom-call(bf16[2048,768]{1,0:T(8,128)(2,1)} %bitcast.54, ...), custom_call_target="tpu_custom_call", output_to_operand_aliasing={{7}: (21, {}), {8}: (22, {})} | custom-call | tf_op jit(solution)/shard_map/pallas_call | solution.py:1385
  423.6 85.3 %shard_map.283 = (f32[1024,768]{1,0:T(8,128)}, f32[192,3072]{1,0:T(8,128)}, f32[768,768]{1,0:T(8,128)}, f32[96,768]{1,0:T(8,128)}, f32[96,1152]{1,0:T(8,128)}, /*index=5*/f32[96,1152]{1,0:T(8,128)}, f32[96,128]{1,0:T(8,128)}) custom-call(bf16[4,2,96,768]{3,2,1,0:T(8,128)(2,1)} %bitcast.63, ...), custom_call_target="tpu_custom_call", output_to_operand_aliasing={{1}: (12, {}), {2}: (13, {})} | custom-call | tf_op jit(solution)/shard_map/pallas_call | solution.py:1841
  508.8 3.4 constant_dynamic-slice_fusion.1
  512.3 1.9 pad_maximum_fusion.1
  515.3 0.8 slice_reduce_fusion
  517.6 2.4 fusion.16
  520.0 2.4 concatenate.27
  522.4 1.9 pad_maximum_fusion
  525.4 1.4 copy.66
  526.8 1.4 copy.67
  (66 shorter events, 14.4 us)
Async XLA Ops:
  10.4 7.7 %copy-start.8 = (f32[8,768]{1,0:T(8,128)}, f32[8,768]{1,0:T(8,128)S(1)}, u32[]{:S(2)}) copy-start(f32[8,768]{1,0:T(8,128)S(1)} %convert_element_type.27.centroid_ref) | copy-start | bytes 73732
  13.0 5.1 copy-start.5
  19.5 101.6 %copy-start.3 = (bf16[512,768]{1,0:T(8,128)(2,1)S(1)}, bf16[512,768]{1,0:T(8,128)(2,1)}, u32[]{:S(2)}) copy-start(bf16[512,768]{1,0:T(8,128)(2,1)} %get-tuple-element.132.short_ref.short_tokens) | copy-start | bytes 2359300
  19.5 101.6 %copy-start.4 = (bf16[512,768]{1,0:T(8,128)(2,1)S(1)}, bf16[512,768]{1,0:T(8,128)(2,1)}, u32[]{:S(2)}) copy-start(bf16[512,768]{1,0:T(8,128)(2,1)} %get-tuple-element.133.row_ref.long_tokens) | copy-start | bytes 2359300
  19.5 101.6 %copy-start.12 = (f32[768]{0:T(1024)S(1)}, f32[768]{0:T(1024)}, u32[]{:S(2)}) copy-start(f32[768]{0:T(1024)} %param.25) | copy-start | bytes 9220
  124.5 6.9 %copy-start.2 = (f32[1024,768]{1,0:T(8,128)}, f32[1024,768]{1,0:T(8,128)S(1)}, u32[]{:S(2)}) copy-start(f32[1024,768]{1,0:T(8,128)S(1)} %get-tuple-element.153.middle_ref) | copy-start | bytes 9437188
  124.5 0.7 copy-start.9
  124.5 0.8 copy-start.10
  512.3 1.9 copy-start.11
  512.3 3.0 copy-start.6
  522.4 1.9 copy-start.7
  522.4 3.0 copy-start
  524.2 2.5 copy-start.1
